TPU v7x, 32 devices: a whole 2x2x4 slice. The times are simulated.
32 devices in a mesh: gx: 4 (over y, core), gy: 8 (over z, x).
Axes of the slice: x: 2, y: 2, z: 4, core: 2. Of those that a mesh axis runs over, the one named last changes fastest.
Arguments:
- elem_volume: float32 [73728], P(('gx', 'gy')), may hold values from 0.5 to 1.5
- elem_velocity: float32 [3, 73728], P(None, ('gx', 'gy')), may hold values from -6 to 6
- elem_energy: float32 [73728], P(('gx', 'gy')), may hold values from 0.3 to 3
- elem_mat: int32 [73728], P(('gx', 'gy')), may hold values from 0 to 7
- elem_dest: int32 [576], P(('gx', 'gy')), may hold values from 0 to 31, as said below
- tile_slot: int32 [4096], P(('gx', 'gy')), may hold values from 0 to 63, as said below
- tile_cell: int32 [4096], P(('gx', 'gy')), may hold values from 0 to 1023
- tile_weight: bfloat16 [4096, 128, 128], P(('gx', 'gy')), may hold values from 0.00390625 to 0.01171875
- tile_count: int32 [32], P(('gx', 'gy')), may hold values from 32 to 128, as said below
- cell_state: float32 [12, 256, 16384], P(None, 'gx', 'gy'), may hold values from -4 to 4, as said below
- mat_props: float32 [2, 8], replicated, may hold values from 0.5 to 4
Outputs:
- remapped: float32 [12, 256, 16384], P(None, 'gx', 'gy')
- elem_pressure: bfloat16 [73728], P(('gx', 'gy'))
Inputs may be any that keep to these rules, and one draw needn't show every extreme that they name: `elem_dest`: each device sends exactly 2 of its blocks to each of the nine devices at offsets -1, 0, +1 along gx and along gy, wrapping at the ends, itself included. `tile_slot`: A value is source * 2 + rank of a block that was sent to this device; every block sent to a device is named by some tile below its count. `tile_count`: some device has all 128 tiles counted. `cell_state`: the volume and energy rows lie between 0.1 and 1; the three momentum rows are signed.
All inputs are finite; a program needn't handle non-finite values.
Results may differ from a plain program's by a relative error of at most 0.0024.
Values may be sent and summed in bfloat16 or wider, within the bound.
No kernel may reach another device: no remote copies, remote signals or barrier semaphores. Data moves between devices by JAX's collectives and lax.ppermute only.
A program may use at most 192 MiB of HBM per device.

v0:
```python
import jax
import jax.numpy as jnp
from jax import lax
from jax.sharding import PartitionSpec as P

MAT = 8
NZ = 64
BLK = 128
CAP = 2


time_step = 0.8


def from_behind(value, axis, steps):
    count = lax.axis_size(axis)
    pairs = [(source, (source + steps) % count) for source in range(count)]
    return lax.ppermute(value, axis, pairs)


def with_halo(value, sides, width):
    for axis, dim in sides:
        size, length = (lax.axis_size(axis), value.shape[dim])
        up = [(i, (i + 1) % size) for i in range(size - 1)]
        down = [(j, i) for i, j in up]
        last = lax.slice_in_dim(value, length - width, length, axis=dim)
        leading = lax.slice_in_dim(value, 0, width, axis=dim)
        before = lax.ppermute(last, axis, up)
        after = lax.ppermute(leading, axis, down)
        value = jnp.concatenate([before, value, after], axis=dim)
    return value


def face_flux(q_lo, q_hi, u_lo, u_hi):
    speed = 0.5 * (u_lo + u_hi)
    return 0.5 * (speed * (q_lo + q_hi) - jnp.abs(speed) * (q_hi - q_lo))


def wrap_offset(diff, extent):
    value = (diff + extent) % extent
    return jnp.where(value == extent - 1, -1, value)


def neighbours(parcel, sign):
    middle = []
    for first in range(3):
        band = parcel[first]
        if first != 1:
            band = from_behind(band, "gx", sign * (first - 1))
        middle.append(band)
    middle = jnp.stack(middle)
    columns = []
    for second in range(3):
        column = middle[:, second]
        if second != 1:
            column = from_behind(column, "gy", sign * (second - 1))
        columns.append(column)
    return jnp.stack(columns, axis=1)


def per_device(
    elem_volume,
    elem_velocity,
    elem_energy,
    elem_mat,
    elem_dest,
    tile_slot,
    tile_cell,
    tile_weight,
    tile_count,
    cell_state,
    mat_props,
):
    grid_x = lax.axis_size("gx")
    grid_y = lax.axis_size("gy")
    pos_x = lax.axis_index("gx")
    pos_y = lax.axis_index("gy")
    n_blocks = elem_dest.shape[0]
    n_tiles = tile_weight.shape[0]
    count_q = cell_state.shape[0]
    width_x = cell_state.shape[1]
    width_y = cell_state.shape[2] // NZ
    n_cellblk = width_x * width_y * NZ // BLK
    density = mat_props[0]
    modulus = mat_props[1]
    onehot = (elem_mat[None, :] == jnp.arange(MAT, dtype=jnp.int32)[:, None]).astype(jnp.float32)
    mass_e = elem_volume * jnp.sum(onehot * density[:, None], axis=0)
    momentum = mass_e[None, :] * elem_velocity
    heat = (mass_e * elem_energy)[None, :]
    rows = jnp.concatenate([onehot * elem_volume[None, :], momentum, heat], axis=0).astype(
        jnp.bfloat16
    )
    n_rows = rows.shape[0]
    blocks = rows.reshape(n_rows, n_blocks, BLK).transpose(1, 0, 2)
    index = jnp.arange(n_blocks, dtype=jnp.int32)
    same = elem_dest[:, None] == elem_dest[None, :]
    rank = jnp.sum((same & (index[:, None] > index[None, :])).astype(jnp.int32), axis=1)
    near = (
        (wrap_offset(elem_dest // grid_y - pos_x, grid_x) + 1) * 3
        + wrap_offset(elem_dest % grid_y - pos_y, grid_y)
        + 1
    )
    outgoing = jnp.zeros((9 * CAP, n_rows, BLK), jnp.bfloat16).at[near * CAP + rank].set(blocks)
    incoming = neighbours(outgoing.reshape(3, 3, CAP, n_rows, BLK), 1)
    received = incoming.reshape(9 * CAP, n_rows, BLK)
    source = tile_slot // CAP
    step_x = wrap_offset(pos_x - source // grid_y, grid_x)
    step_y = wrap_offset(pos_y - source % grid_y, grid_y)
    local_slot = ((step_x + 1) * 3 + step_y + 1) * CAP + tile_slot % CAP
    n_slots = 9 * CAP
    tile_rows = jnp.take(received, local_slot, axis=0)
    valid = (jnp.arange(n_tiles, dtype=jnp.int32) < tile_count[0]).astype(jnp.float32)
    contrib = (
        jnp.einsum("trb,tbc->rtc", tile_rows, tile_weight, preferred_element_type=jnp.float32)
        * valid[None, :, None]
    )
    cell_pick = (tile_cell[None, :] == jnp.arange(n_cellblk, dtype=jnp.int32)[:, None]).astype(
        jnp.float32
    )
    dep = jnp.einsum("kt,rtc->rkc", cell_pick, contrib, precision=lax.Precision.HIGHEST)
    dep = dep.reshape(count_q, width_x, width_y, NZ)
    state = cell_state.reshape(count_q, width_x, width_y, NZ) + dep
    mass = 1.0 + jnp.sum(density[:, None, None, None] * state[:MAT], axis=0)
    speeds = jnp.stack([state[MAT] / mass, state[MAT + 1] / mass], axis=0)
    packed = jnp.concatenate([state, speeds], axis=0)
    framed = with_halo(packed.astype(jnp.bfloat16), (("gx", 1), ("gy", 2)), 1).astype(packed.dtype)
    along_x = framed[:, :, 1:-1]
    flux_x = face_flux(
        along_x[:count_q, :-1],
        along_x[:count_q, 1:],
        along_x[count_q : count_q + 1, :-1],
        along_x[count_q : count_q + 1, 1:],
    )
    along_y = framed[:, 1:-1]
    flux_y = face_flux(
        along_y[:count_q, :, :-1],
        along_y[:count_q, :, 1:],
        along_y[count_q + 1 : count_q + 2, :, :-1],
        along_y[count_q + 1 : count_q + 2, :, 1:],
    )
    fresh = state - time_step * (
        flux_x[:, 1:] - flux_x[:, :-1] + flux_y[:, :, 1:] - flux_y[:, :, :-1]
    )
    remapped = fresh.reshape(count_q, width_x, width_y * NZ)
    volumes = fresh[:MAT]
    pressure = (
        jnp.sum(modulus[:, None, None, None] * volumes * (1.0 + 0.5 * volumes), axis=0)
        + 0.4 * fresh[count_q - 1]
    )
    press_blocks = pressure.astype(jnp.bfloat16).reshape(n_cellblk, BLK)
    picked = jnp.take(press_blocks, tile_cell, axis=0)
    probe = jnp.stack([picked, jnp.ones_like(picked)], axis=1)
    both = (
        jnp.einsum("tec,tkc->tke", tile_weight, probe, preferred_element_type=jnp.float32)
        * valid[:, None, None]
    )
    slot_pick = (local_slot[None, :] == jnp.arange(n_slots, dtype=jnp.int32)[:, None]).astype(
        jnp.float32
    )
    sums = jnp.dot(
        slot_pick, both.reshape(n_tiles, 2 * BLK), precision=lax.Precision.HIGHEST
    ).reshape(n_slots, 2, BLK)
    answer = (sums[:, 0] / jnp.maximum(sums[:, 1], 1.0)).astype(jnp.bfloat16)
    returned = neighbours(answer.reshape(3, 3, CAP, BLK), -1).reshape(9 * CAP, BLK)
    mine = jnp.take(returned, near * CAP + rank, axis=0)
    return (remapped, mine.reshape(n_blocks * BLK))


def solution(mesh):
    placed = (
        P(("gx", "gy")),
        P(None, ("gx", "gy")),
        P(("gx", "gy")),
        P(("gx", "gy")),
        P(("gx", "gy")),
        P(("gx", "gy")),
        P(("gx", "gy")),
        P(("gx", "gy"), None, None),
        P(("gx", "gy")),
        P(None, "gx", "gy"),
        P(),
    )
    return jax.shard_map(
        per_device,
        mesh=mesh,
        in_specs=placed,
        out_specs=(P(None, "gx", "gy"), P(("gx", "gy"))),
        check_vma=False,
    )
```

profile of v0, /device:TPU:0, one launch (start us, length us, event | category | flops | bytes accessed | tf_op | source)
XLA Modules:
  0.0 186.6 jit_solution(3210299603953594929)
XLA Ops:
  0.6 0.9 convert_reduce_fusion
  1.5 0.8 slice_bitcast_fusion.6
  2.3 0.8 select_reduce_fusion
  3.1 0.7 fusion.25
  3.9 0.8 fusion.18
  4.6 0.7 select_convert_fusion
  5.4 0.7 compare_and_fusion.1
  6.1 1.5 scatter_fusion
  7.7 0.5 collective-permute-start.1
  8.2 2.0 %collective-permute-start = (bf16[3,2,12,128]{3,1,2,0:T(2,128)(2,1)S(1)}, bf16[3,2,12,128]{3,1,2,0:T(2,128)(2,1)S(1)}, u32[]{:S(2)}, u32[]{:S(2)}) collective-permute-start(bf16[3,2,12,128]{3,1,2,0:T(2,128)(2,1)S(1)} %copy.50), channel_id=1, source_target_pairs={{0,24},{8,0},{16,8},{24,16},{1,25},{9,1},{17,9},{25,17},{2,26},{10... | collective-permute-start | bytes 55304 | tf_op jit(solution)/shard_map/ppermute | solution.py:18
  10.9 0.7 compare_and_fusion.2
  11.7 0.0 collective-permute-done.1
  11.7 0.1 collective-permute-done
  11.7 0.1 pad_maximum_fusion.8
  11.9 2.3 %collective-permute-start.3 = (bf16[3,2,12,128]{3,1,0,2:T(2,128)(2,1)S(1)}, bf16[3,2,12,128]{3,1,0,2:T(2,128)(2,1)S(1)}, u32[]{:S(2)}, u32[]{:S(2)}) collective-permute-start(bf16[3,2,12,128]{3,1,0,2:T(2,128)(2,1)S(1)} %get-tuple-element.24), channel_id=1, source_target_pairs={{0,1},{1,2},{2,3},{3,4},{4,5},{5,6},{6,7},{7,0},{8,9},{9,10},{10,1... | collective-permute-start | bytes 55304 | tf_op jit(solution)/shard_map/ppermute | solution.py:18
  14.2 3.1 %collective-permute-start.2 = (bf16[3,2,12,128]{3,1,0,2:T(2,128)(2,1)S(1)}, bf16[3,2,12,128]{3,1,0,2:T(2,128)(2,1)S(1)}, u32[]{:S(2)}, u32[]{:S(2)}) collective-permute-start(bf16[3,2,12,128]{3,1,0,2:T(2,128)(2,1)S(1)} %get-tuple-element.23), channel_id=1, source_target_pairs={{0,7},{1,0},{2,1},{3,2},{4,3},{5,4},{6,5},{7,6},{8,15},{9,8},{10,9... | collective-permute-start | bytes 55304 | tf_op jit(solution)/shard_map/ppermute | solution.py:18
  17.3 11.4 %reshape.141 = f32[12,64,32,64]{3,2,1,0:T(8,128)} reshape(f32[12,64,2048]{2,1,0:T(8,128)} %param.20) | data formatting | bytes 12582912 | tf_op jit(solution)/shard_map/reshape | solution.py:122
  28.7 0.1 pad_maximum_fusion.9
  28.8 0.7 gather_fusion
  29.5 3.5 %fusion.3 = f32[12,128,128]{2,0,1:T(8,128)S(1)} fusion(bf16[128,128,128]{2,1,0:T(8,128)(2,1)} %param.18, f32[128]{0:T(128)S(1)} %get-tuple-element.34, bf16[128,12,128]{2,1,0:T(8,128)(2,1)S(1)} %gather_fusion, pred[128]{0:T(512)(128)(4,1)S(1)} %get-tuple-element.6), kind=kOutput, calls=%fused_computation.17 | convolution fusion | flops 50724864 | bytes 5374592 | tf_op jit(solution)/shard_map/trb,tbc->rtc/dot_general | solution.py:114
  33.0 4.6 %convolution_bitcast_fusion = f32[12,1024,128]{1,2,0:T(8,128)} fusion(f32[12,128,128]{2,0,1:T(8,128)S(1)} %fusion.3, s32[128]{0:T(128)S(1)} %copy-done.2), kind=kOutput, calls=%fused_computation.15 | convolution fusion | flops 2416050176 | bytes 7078400 | tf_op jit(solution)/shard_map/kt,rtc->rkc/dot_general | solution.py:120
  37.6 6.6 %copy.57 = f32[12,1024,128]{2,1,0:T(8,128)} copy(f32[12,1024,128]{1,2,0:T(8,128)} %convolution_bitcast_fusion) | data formatting | bytes 12582912 | tf_op jit(solution)/shard_map/kt,rtc->rkc/transpose | solution.py:120
  44.2 10.2 %reshape.143 = f32[12,64,32,64]{3,2,1,0:T(8,128)} reshape(f32[12,1024,128]{2,1,0:T(8,128)} %copy.57) | data formatting | bytes 12582912 | tf_op jit(solution)/shard_map/reshape | solution.py:121
  54.4 9.7 %fusion.44 = (bf16[12,64,32,64]{3,2,1,0:T(8,128)(2,1)S(1)}, f32[12,64,32,64]{3,2,1,0:T(8,128)S(1)}) fusion(f32[12,64,32,64]{3,2,1,0:T(8,128)} %reshape.141, f32[12,64,32,64]{3,2,1,0:T(8,128)} %reshape.143), kind=kLoop, calls=%fused_computation.141 | loop fusion | flops 3145728 | bytes 22020096 | tf_op jit(solution)/shard_map/convert
  64.2 0.0 copy-start.1
  64.2 1.2 fusion.2
  65.4 0.4 fusion.7
  65.8 0.1 pad_maximum_fusion.7
  65.9 1.3 collective-permute-start.5
  67.2 3.9 %collective-permute-start.4 = (bf16[14,1,32,64]{3,2,1,0:T(8,128)(2,1)S(1)}, bf16[14,1,32,64]{3,2,1,0:T(8,128)(2,1)S(1)}, u32[]{:S(2)}, u32[]{:S(2)}) collective-permute-start(bf16[14,1,32,64]{3,2,1,0:T(8,128)(2,1)S(1)} %get-tuple-element.18), channel_id=1, source_target_pairs={{0,8},{8,16},{16,24},{1,9},{9,17},{17,25},{2,10},{10,18},{18,26},{... | collective-permute-start | bytes 172040 | tf_op jit(solution)/shard_map/ppermute | solution.py:28
  71.1 0.0 collective-permute-done.5
  71.1 0.9 collective-permute-done.4
  72.0 2.4 %pad_maximum_fusion.4 = (bf16[14,66,1,64]{3,2,1,0:T(2,128)(2,1)S(1)}, bf16[14,66,1,64]{3,2,1,0:T(2,128)(2,1)S(1)}) fusion(bf16[14,1,32,64]{3,2,1,0:T(8,128)(2,1)S(1)} %collective-permute-done.5, bf16[14,1,32,64]{3,2,1,0:T(8,128)(2,1)S(1)} %collective-permute-done.4, bf16[1,64,32,64]{3,2,1,0:T(8,128)(2,1)S(1)} %get-tuple-element.15, ...), kind=kLoop, calls=%fused_computation.40 | loop fusion | flops 1182720 | bytes 4021248 | tf_op jit(solution)/shard_map/slice | solution.py:26
  74.4 1.3 collective-permute-start.7
  75.7 4.8 %collective-permute-start.6 = (bf16[14,66,1,64]{3,2,1,0:T(2,128)(2,1)S(1)}, bf16[14,66,1,64]{3,2,1,0:T(2,128)(2,1)S(1)}, u32[]{:S(2)}, u32[]{:S(2)}) collective-permute-start(bf16[14,66,1,64]{3,2,1,0:T(2,128)(2,1)S(1)} %get-tuple-element.16), channel_id=1, source_target_pairs={{0,1},{1,2},{2,3},{3,4},{4,5},{5,6},{6,7},{8,9},{9,10},{10,11},{11... | collective-permute-start | bytes 354824 | tf_op jit(solution)/shard_map/ppermute | solution.py:28
  80.5 7.8 %collective-permute-done.7 = bf16[14,66,1,64]{3,2,1,0:T(2,128)(2,1)S(1)} collective-permute-done((bf16[14,66,1,64]{3,2,1,0:T(2,128)(2,1)S(1)}, bf16[14,66,1,64]{3,2,1,0:T(2,128)(2,1)S(1)}, u32[]{:S(2)}, u32[]{:S(2)}) %collective-permute-start.7) | collective-permute-done | bytes 118304 | tf_op jit(solution)/shard_map/ppermute | solution.py:29
  88.3 8.8 %collective-permute-done.6 = bf16[14,66,1,64]{3,2,1,0:T(2,128)(2,1)S(1)} collective-permute-done((bf16[14,66,1,64]{3,2,1,0:T(2,128)(2,1)S(1)}, bf16[14,66,1,64]{3,2,1,0:T(2,128)(2,1)S(1)}, u32[]{:S(2)}, u32[]{:S(2)}) %collective-permute-start.6) | collective-permute-done | bytes 118304 | tf_op jit(solution)/shard_map/ppermute | solution.py:28
  97.1 13.2 %maximum_convert_fusion = f32[14,66,34,64]{3,2,1,0:T(8,128)S(1)} fusion(bf16[14,66,1,64]{3,2,1,0:T(2,128)(2,1)S(1)} %collective-permute-done.7, bf16[14,1,32,64]{3,2,1,0:T(8,128)(2,1)S(1)} %collective-permute-done.5, bf16[1,64,32,64]{3,2,1,0:T(8,128)(2,1)S(1)} %get-tuple-element.15, bf16[1,64,32,64]{3,2,1,0:T(8,128)(2,1)S(1)} %get-tuple-element.14, ...), kind=kLoop, calls=%fused_computation.11 | loop fusion | flops 28148736 | bytes 12063744 | tf_op jit(solution)/shard_map/convert_element_type | solution.py:126
  110.3 0.3 fusion.13
  110.5 1.2 fusion.14
  111.7 7.2 %subtract_multiply_fusion = f32[12,64,33,64]{3,2,1,0:T(8,128)} fusion(f32[14,66,34,64]{3,2,1,0:T(8,128)S(1)} %maximum_convert_fusion, f32[64,33,64]{2,1,0:T(8,128)S(1)} %get-tuple-element.13, f32[64,33,64]{2,1,0:T(8,128)S(1)} %get-tuple-element.12), kind=kLoop, calls=%fused_computation.4 | loop fusion | flops 9732096 | bytes 20545536 | tf_op jit(solution)/shard_map/mul | solution.py:36
  118.9 8.8 %subtract_multiply_fusion.1 = f32[12,65,32,64]{3,2,1,0:T(8,128)} fusion(f32[14,66,34,64]{3,2,1,0:T(8,128)S(1)} %maximum_convert_fusion, f32[65,32,64]{2,1,0:T(8,128)} %get-tuple-element.11, f32[65,32,64]{2,1,0:T(8,128)S(1)} %get-tuple-element.10), kind=kLoop, calls=%fused_computation.5 | loop fusion | flops 9584640 | bytes 20234240 | tf_op jit(solution)/shard_map/mul | solution.py:36
  127.7 27.3 %fusion.1 = f32[12,64,32,64]{3,2,1,0:T(8,128)} fusion(f32[12,64,32,64]{3,2,1,0:T(8,128)} %copy-done, f32[12,64,33,64]{3,2,1,0:T(8,128)} %subtract_multiply_fusion, f32[12,65,32,64]{3,2,1,0:T(8,128)} %subtract_multiply_fusion.1), kind=kLoop, calls=%fused_computation.8 | loop fusion | flops 7864320 | bytes 37748736 | tf_op jit(solution)/shard_map/sub | solution.py:141
  155.1 1.3 slice_multiply_fusion.1
  156.4 4.5 %multiply_reduce_fusion = f32[64,32,64]{2,1,0:T(8,128)S(1)} fusion(f32[12,64,32,64]{3,2,1,0:T(8,128)} %fusion.1, f32[8]{0:T(128)S(1)} %get-tuple-element.32), kind=kLoop, calls=%fused_computation.14 | loop fusion | flops 5111808 | bytes 4718624 | tf_op jit(solution)/shard_map/reduce_sum | solution.py:147
  160.9 0.2 reduce_sum.42
  161.1 0.2 mul.223
  161.3 0.1 add_convert_fusion
  161.4 0.7 gather_fusion.1
  162.1 0.2 broadcast_select_fusion
  162.3 4.4 %convolution_multiply_fusion.1 = f32[128,2,128]{2,1,0:T(2,128)S(1)} fusion(bf16[128,128,128]{2,1,0:T(8,128)(2,1)} %param.18, f32[128]{0:T(128)S(1)} %get-tuple-element.34, bf16[128,1,128]{2,1,0:T(2,128)(2,1)S(1)} %broadcast_select_fusion), kind=kOutput, calls=%fused_computation.21 | convolution fusion | flops 8421376 | bytes 4358656 | tf_op jit(solution)/shard_map/tec,tkc->tke/dot_general | solution.py:154
  166.8 0.1 copy.59
  166.9 0.2 fusion.23
  167.1 0.8 collective-permute-start.9
  167.9 0.0 collective-permute-start.8
  167.9 1.3 collective-permute-done.9
  169.2 1.7 collective-permute-done.8
  170.9 2.4 %collective-permute-start.11 = (bf16[3,2,128]{2,1,0:T(2,128)(2,1)S(1)}, bf16[3,2,128]{2,1,0:T(2,128)(2,1)S(1)}, u32[]{:S(2)}, u32[]{:S(2)}) collective-permute-start(bf16[3,2,128]{2,1,0:T(2,128)(2,1)S(1)} %get-tuple-element.30), channel_id=1, source_target_pairs={{0,7},{1,0},{2,1},{3,2},{4,3},{5,4},{6,5},{7,6},{8,15},{9,8},{10,9... | collective-permute-start | bytes 4616 | tf_op jit(solution)/shard_map/ppermute | solution.py:18
  173.3 0.2 collective-permute-start.10
  173.5 11.8 %reshape.144 = f32[12,64,2048]{2,1,0:T(8,128)} reshape(f32[12,64,32,64]{3,2,1,0:T(8,128)} %fusion.1) | data formatting | bytes 12582912 | tf_op jit(solution)/shard_map/reshape | solution.py:144
  185.3 0.0 collective-permute-done.11
  185.3 0.0 collective-permute-done.10
  185.4 0.6 gather_fusion.2
  185.9 0.7 select_bitcast_fusion
  (33 shorter events, 0.4 us)
Async XLA Ops:
  7.7 3.9 %collective-permute-start.1 = (bf16[3,2,12,128]{3,1,2,0:T(2,128)(2,1)S(1)}, bf16[3,2,12,128]{3,1,2,0:T(2,128)(2,1)S(1)}, u32[]{:S(2)}, u32[]{:S(2)}) collective-permute-start(bf16[3,2,12,128]{3,1,2,0:T(2,128)(2,1)S(1)} %copy.51), channel_id=1, source_target_pairs={{0,8},{8,16},{16,24},{24,0},{1,9},{9,17},{17,25},{25,1},{2,10},{10... | collective-permute-start | bytes 55304 | tf_op jit(solution)/shard_map/ppermute | solution.py:18
  8.2 3.5 %collective-permute-start = (bf16[3,2,12,128]{3,1,2,0:T(2,128)(2,1)S(1)}, bf16[3,2,12,128]{3,1,2,0:T(2,128)(2,1)S(1)}, u32[]{:S(2)}, u32[]{:S(2)}) collective-permute-start(bf16[3,2,12,128]{3,1,2,0:T(2,128)(2,1)S(1)} %copy.50), channel_id=1, source_target_pairs={{0,24},{8,0},{16,8},{24,16},{1,25},{9,1},{17,9},{25,17},{2,26},{10... | collective-permute-start | bytes 55304 | tf_op jit(solution)/shard_map/ppermute | solution.py:18
  11.9 16.8 %collective-permute-start.3 = (bf16[3,2,12,128]{3,1,0,2:T(2,128)(2,1)S(1)}, bf16[3,2,12,128]{3,1,0,2:T(2,128)(2,1)S(1)}, u32[]{:S(2)}, u32[]{:S(2)}) collective-permute-start(bf16[3,2,12,128]{3,1,0,2:T(2,128)(2,1)S(1)} %get-tuple-element.24), channel_id=1, source_target_pairs={{0,1},{1,2},{2,3},{3,4},{4,5},{5,6},{6,7},{7,0},{8,9},{9,10},{10,1... | collective-permute-start | bytes 55304 | tf_op jit(solution)/shard_map/ppermute | solution.py:18
  14.2 14.5 %collective-permute-start.2 = (bf16[3,2,12,128]{3,1,0,2:T(2,128)(2,1)S(1)}, bf16[3,2,12,128]{3,1,0,2:T(2,128)(2,1)S(1)}, u32[]{:S(2)}, u32[]{:S(2)}) collective-permute-start(bf16[3,2,12,128]{3,1,0,2:T(2,128)(2,1)S(1)} %get-tuple-element.23), channel_id=1, source_target_pairs={{0,7},{1,0},{2,1},{3,2},{4,3},{5,4},{6,5},{7,6},{8,15},{9,8},{10,9... | collective-permute-start | bytes 55304 | tf_op jit(solution)/shard_map/ppermute | solution.py:18
  17.3 15.7 %copy-start.2 = (s32[128]{0:T(128)S(1)}, s32[128]{0:T(128)}, u32[]{:S(2)}) copy-start(s32[128]{0:T(128)} %param.17) | copy-start | bytes 1540
  64.2 10.2 %copy-start = (f32[12,64,32,64]{3,2,1,0:T(8,128)}, f32[12,64,32,64]{3,2,1,0:T(8,128)S(1)}, u32[]{:S(2)}) copy-start(f32[12,64,32,64]{3,2,1,0:T(8,128)S(1)} %get-tuple-element.5) | copy-start | bytes 18874372
  64.2 10.2 %copy-start.1 = (bf16[12,64,32,64]{3,2,1,0:T(8,128)(2,1)}, bf16[12,64,32,64]{3,2,1,0:T(8,128)(2,1)S(1)}, u32[]{:S(2)}) copy-start(bf16[12,64,32,64]{3,2,1,0:T(8,128)(2,1)S(1)} %get-tuple-element.4) | copy-start | bytes 9437188
  65.9 5.2 %collective-permute-start.5 = (bf16[14,1,32,64]{3,2,1,0:T(8,128)(2,1)S(1)}, bf16[14,1,32,64]{3,2,1,0:T(8,128)(2,1)S(1)}, u32[]{:S(2)}, u32[]{:S(2)}) collective-permute-start(bf16[14,1,32,64]{3,2,1,0:T(8,128)(2,1)S(1)} %get-tuple-element.19), channel_id=1, source_target_pairs={{8,0},{16,8},{24,16},{9,1},{17,9},{25,17},{10,2},{18,10},{26,18},{... | collective-permute-start | bytes 172040 | tf_op jit(solution)/shard_map/ppermute | solution.py:29
  67.2 4.8 %collective-permute-start.4 = (bf16[14,1,32,64]{3,2,1,0:T(8,128)(2,1)S(1)}, bf16[14,1,32,64]{3,2,1,0:T(8,128)(2,1)S(1)}, u32[]{:S(2)}, u32[]{:S(2)}) collective-permute-start(bf16[14,1,32,64]{3,2,1,0:T(8,128)(2,1)S(1)} %get-tuple-element.18), channel_id=1, source_target_pairs={{0,8},{8,16},{16,24},{1,9},{9,17},{17,25},{2,10},{10,18},{18,26},{... | collective-permute-start | bytes 172040 | tf_op jit(solution)/shard_map/ppermute | solution.py:28
  74.4 13.9 %collective-permute-start.7 = (bf16[14,66,1,64]{3,2,1,0:T(2,128)(2,1)S(1)}, bf16[14,66,1,64]{3,2,1,0:T(2,128)(2,1)S(1)}, u32[]{:S(2)}, u32[]{:S(2)}) collective-permute-start(bf16[14,66,1,64]{3,2,1,0:T(2,128)(2,1)S(1)} %get-tuple-element.17), channel_id=1, source_target_pairs={{1,0},{2,1},{3,2},{4,3},{5,4},{6,5},{7,6},{9,8},{10,9},{11,10},{12... | collective-permute-start | bytes 354824 | tf_op jit(solution)/shard_map/ppermute | solution.py:29
  75.7 21.4 %collective-permute-start.6 = (bf16[14,66,1,64]{3,2,1,0:T(2,128)(2,1)S(1)}, bf16[14,66,1,64]{3,2,1,0:T(2,128)(2,1)S(1)}, u32[]{:S(2)}, u32[]{:S(2)}) collective-permute-start(bf16[14,66,1,64]{3,2,1,0:T(2,128)(2,1)S(1)} %get-tuple-element.16), channel_id=1, source_target_pairs={{0,1},{1,2},{2,3},{3,4},{4,5},{5,6},{6,7},{8,9},{9,10},{10,11},{11... | collective-permute-start | bytes 354824 | tf_op jit(solution)/shard_map/ppermute | solution.py:28
  167.1 2.1 %collective-permute-start.9 = (bf16[3,2,128]{2,1,0:T(2,128)(2,1)S(1)}, bf16[3,2,128]{2,1,0:T(2,128)(2,1)S(1)}, u32[]{:S(2)}, u32[]{:S(2)}) collective-permute-start(bf16[3,2,128]{2,1,0:T(2,128)(2,1)S(1)} %squeeze.38), channel_id=1, source_target_pairs={{0,24},{8,0},{16,8},{24,16},{1,25},{9,1},{17,9},{25,17},{2,26},{10... | collective-permute-start | bytes 4616 | tf_op jit(solution)/shard_map/ppermute | solution.py:18
  167.9 3.0 %collective-permute-start.8 = (bf16[3,2,128]{2,1,0:T(2,128)(2,1)S(1)}, bf16[3,2,128]{2,1,0:T(2,128)(2,1)S(1)}, u32[]{:S(2)}, u32[]{:S(2)}) collective-permute-start(bf16[3,2,128]{2,1,0:T(2,128)(2,1)S(1)} %squeeze.37), channel_id=1, source_target_pairs={{0,8},{8,16},{16,24},{24,0},{1,9},{9,17},{17,25},{25,1},{2,10},{10... | collective-permute-start | bytes 4616 | tf_op jit(solution)/shard_map/ppermute | solution.py:18
  170.9 14.4 %collective-permute-start.11 = (bf16[3,2,128]{2,1,0:T(2,128)(2,1)S(1)}, bf16[3,2,128]{2,1,0:T(2,128)(2,1)S(1)}, u32[]{:S(2)}, u32[]{:S(2)}) collective-permute-start(bf16[3,2,128]{2,1,0:T(2,128)(2,1)S(1)} %get-tuple-element.30), channel_id=1, source_target_pairs={{0,7},{1,0},{2,1},{3,2},{4,3},{5,4},{6,5},{7,6},{8,15},{9,8},{10,9... | collective-permute-start | bytes 4616 | tf_op jit(solution)/shard_map/ppermute | solution.py:18
  173.3 12.0 %collective-permute-start.10 = (bf16[3,2,128]{2,1,0:T(2,128)(2,1)S(1)}, bf16[3,2,128]{2,1,0:T(2,128)(2,1)S(1)}, u32[]{:S(2)}, u32[]{:S(2)}) collective-permute-start(bf16[3,2,128]{2,1,0:T(2,128)(2,1)S(1)} %get-tuple-element.29), channel_id=1, source_target_pairs={{0,1},{1,2},{2,3},{3,4},{4,5},{5,6},{6,7},{7,0},{8,9},{9,10},{10,1... | collective-permute-start | bytes 4616 | tf_op jit(solution)/shard_map/ppermute | solution.py:18
where the time goes:
time: 188 us; the launch traced here: 187 us
  other arithmetic  84.1 us (45%)
  local copies, waits for them, and re-layouts  45 us (24%)
  starting transfers between devices  22.6 us (12%)
  waiting for transfers between devices  20.6 us (11%)
  matrix products  12.7 us (7%)
    sub x1, other arithmetic, per_device(): state - time_step * (flux_x[:, 1:] - flux_x[:, :-1] + flux_y[:, :, 1:] -...  27.3 us
    mul x4, other arithmetic, face_flux(): return 0.5 * (speed * (q_lo + q_hi) - jnp.abs(speed) * (q_hi - q_lo))  17.5 us
    convert_element_type x1, other arithmetic, per_device(): with_halo(packed.astype(jnp.bfloat16), (('gx', 1), ('gy', 2)), 1)  13.2 us
    reshape x1, local copies, waits for them, and re-layouts, per_device(): remapped = fresh.reshape(count_q, width_x, width_y * NZ)  11.8 us
    reshape x1, local copies, waits for them, and re-layouts, per_device(): state = cell_state.reshape(count_q, width_x, width_y, NZ) + dep  11.4 us
    ppermute x8, starting transfers between devices, from_behind(): return lax.ppermute(value, axis, pairs)  11.3 us
    another operation x3, other arithmetic  10.8 us
    reshape x1, local copies, waits for them, and re-layouts, per_device(): dep = dep.reshape(count_q, width_x, width_y, NZ)  10.2 us
  transfers between devices with their start and end apart: 12, of which 6 were waited for; matrix products, arithmetic and copies ran while one was open for 13% of the time, Pallas kernels for 0%

commit v1 on v0

v1 whole, which is shorter than its diff:
```python
import functools

import jax
import jax.numpy as jnp
from jax import lax
from jax.experimental import pallas as pl
from jax.experimental.pallas import tpu as pltpu
from jax.sharding import PartitionSpec as P

MAT = 8
NZ = 64
BLK = 128
CAP = 2
HALF = BLK // 2
PAD = 8
ROWS = 16
UNROLL = 8
MIB = 2**20

time_step = 0.8
F32 = jnp.float32
BF16 = jnp.bfloat16

SMEM = pl.BlockSpec(memory_space=pltpu.SMEM)
VMEM = pl.BlockSpec(memory_space=pltpu.VMEM)
ANY = pl.BlockSpec(memory_space=pl.ANY)


def partner(index, size, which):
    if which == 1:
        return index ^ 1
    return (index + 1 if index % 2 else index - 1) % size


def swap(value, axis, which, wrap=True):
    size = lax.axis_size(axis)
    pairs = [(i, partner(i, size, which)) for i in range(size)]
    if not wrap:
        pairs = [(i, j) for i, j in pairs if abs(i - j) == 1]
    return lax.ppermute(value, axis, pairs)


def code_of(index, mine):
    return jnp.where(index == mine, 0, jnp.where(index == (mine ^ 1), 1, 2))


def split_device(device, size):
    if size & (size - 1) == 0:
        return device >> (size.bit_length() - 1), device & (size - 1)
    return lax.div(device, size), lax.rem(device, size)


def payload_kernel(dest, props, volume, velocity, energy, mat, own, first, second, place, seen, packed, *, size_y):
    pos_x, pos_y = lax.axis_index("gx"), lax.axis_index("gy")
    n_blocks = volume.shape[0]
    kinds = mat[...]
    density = jnp.zeros(kinds.shape, F32)
    for m in range(MAT):
        density = jnp.where(kinds == m, props[0, m], density)
    mass = volume[...] * density
    heat = mass * energy[...]
    level = lax.broadcasted_iota(jnp.int32, (MAT, BLK), 0)
    for k in range(9):
        seen[k] = 0
    for b in range(n_blocks):
        at_x, at_y = split_device(dest[b], size_y)
        near = code_of(at_x, pos_x) * 3 + code_of(at_y, pos_y)
        rank = seen[near]
        seen[near] = rank + 1
        slot = near * CAP + rank
        place[b] = slot
        volumes = jnp.where(kinds[b : b + 1] == level, volume[b : b + 1, :], 0.0)
        momentum = mass[b : b + 1] * velocity[:, b * BLK : (b + 1) * BLK]
        rows = jnp.concatenate([volumes, momentum, heat[b : b + 1], jnp.zeros((4, BLK), F32)], axis=0)
        packed[slot] = rows.astype(BF16)
    for k, out in enumerate((own, first, second)):
        for s in range(3 * CAP):
            out[s] = packed[k * 3 * CAP + s]


def payload(dest, props, volume, velocity, energy, mat, size_y):
    n_blocks = volume.shape[0]
    parcel = pltpu.VMEM((3 * CAP, ROWS, BLK), BF16)
    return pl.pallas_call(
        functools.partial(payload_kernel, size_y=size_y),
        name="payload",
        out_shape=(parcel, parcel, parcel, jax.ShapeDtypeStruct((n_blocks,), jnp.int32)),
        in_specs=[SMEM, SMEM, VMEM, VMEM, VMEM, VMEM],
        out_specs=(VMEM, VMEM, VMEM, SMEM),
        scratch_shapes=[pltpu.SMEM((9,), jnp.int32), pltpu.VMEM((9 * CAP, ROWS, BLK), BF16)],
        compiler_params=pltpu.CompilerParams(vmem_limit_bytes=4 * MIB),
    )(dest, props, volume, velocity, energy, mat)


def stage_kernel(cell, state, sem):
    columns = state.shape[0] - 2
    width = state.shape[2] - 2 * PAD
    copies = [
        pltpu.make_async_copy(
            cell.at[:, :, pl.ds(j * BLK, BLK)], state.at[j + 1, :, pl.ds(PAD, width)], sem.at[j]
        )
        for j in range(columns)
    ]
    for copy in copies:
        copy.start()
    for copy in copies:
        copy.wait()


def stage(cell):
    count, width, lanes = cell.shape
    columns = lanes // BLK
    return pl.pallas_call(
        stage_kernel,
        name="stage",
        out_shape=pltpu.VMEM((columns + 2, count, width + 2 * PAD, BLK), F32),
        in_specs=[ANY],
        out_specs=VMEM,
        scratch_shapes=[pltpu.SemaphoreType.DMA((columns,))],
        compiler_params=pltpu.CompilerParams(vmem_limit_bytes=2 * MIB),
        cost_estimate=pl.CostEstimate(flops=0, bytes_accessed=2 * cell.size * 4, transcendentals=0),
    )(cell)


def local_slot(slot, pos_x, pos_y, size_y):
    at_x, at_y = split_device(slot >> 1, size_y)
    return code_of(at_y, pos_y) * (3 * CAP) + code_of(at_x, pos_x) * CAP + (slot & 1)


def low_lanes():
    return lax.broadcasted_iota(jnp.int32, (1, BLK), 1) < HALF


def turn(value):
    return pltpu.roll(value, HALF, value.ndim - 1)


def deposit_kernel(
    tile_slot, tile_cell, tile_count, own, first, second, north, south, weight, state_in,
    state, edge_x1, edge_x2, edge_y1, edge_y2, rows, *, size_y
):
    pos_x, pos_y = lax.axis_index("gx"), lax.axis_index("gy")
    n_tiles = weight.shape[0]
    columns, count, tall = state.shape[0] - 2, state.shape[1], state.shape[2]
    flat = state.reshape(columns + 2, count * tall, BLK)
    for k, part in enumerate((own, first, second)):
        for r in range(CAP):
            rows[k * CAP + r] = part[r]
    for k, part in enumerate((north, south)):
        for r in range(3 * CAP):
            rows[(k + 1) * 3 * CAP + r] = part[r]
    counted = tile_count[0]

    def add_tiles(step, carry):
        for k in range(UNROLL):
            t = step * UNROLL + k
            slot = local_slot(tile_slot[t], pos_x, pos_y, size_y)
            contrib = jnp.dot(rows[slot], weight[t], preferred_element_type=F32)[:count]
            contrib = jnp.where(t < counted, contrib, 0.0)
            x, j = split_device(tile_cell[t], columns)
            at = pl.ds(x + PAD, count, stride=tall)
            flat[j + 1, at, :] = flat[j + 1, at, :] + contrib
        return carry

    lax.fori_loop(0, n_tiles // UNROLL, add_tiles, 0)

    even_x, even_y = (pos_x & 1) == 0, (pos_y & 1) == 0
    top, bottom = tall - PAD - 1, PAD
    line = state.reshape((columns + 2) * count * tall, BLK)
    for edge, row in (
        (edge_x1, jnp.where(even_x, top, bottom)),
        (edge_x2, jnp.where(even_x, bottom, top)),
    ):
        for q in range(count):
            at = pl.ds(count * tall + q * tall + row, columns, stride=count * tall)
            edge[q * columns : (q + 1) * columns, :] = line[at, :].astype(BF16)
    low = low_lanes()
    width = tall - 2 * PAD
    for edge, upper in ((edge_y1, even_y), (edge_y2, jnp.logical_not(even_y))):
        column = jnp.where(upper, columns, 1)
        for q in range(count // 2):
            for i in range(width // ROWS):
                here = slice(PAD + i * ROWS, PAD + (i + 1) * ROWS)
                a = state[column, q, here, :]
                b = state[column, q + count // 2, here, :]
                both = jnp.where(low, jnp.where(upper, turn(a), a), jnp.where(upper, b, turn(b)))
                edge[q * width + i * ROWS : q * width + (i + 1) * ROWS, :] = both.astype(BF16)


def deposit(tile_slot, tile_cell, tile_count, parts, weight, state, size_y):
    columns, count, tall = state.shape[0] - 2, state.shape[1], state.shape[2]
    edge_x = pltpu.VMEM((count * columns, BLK), BF16)
    edge_y = pltpu.VMEM((count // 2 * (tall - 2 * PAD), BLK), BF16)
    return pl.pallas_call(
        functools.partial(deposit_kernel, size_y=size_y),
        name="deposit",
        out_shape=(pltpu.VMEM(state.shape, F32), edge_x, edge_x, edge_y, edge_y),
        in_specs=[SMEM] * 3 + [VMEM] * 7,
        out_specs=(VMEM,) * 5,
        input_output_aliases={9: 0},
        scratch_shapes=[pltpu.VMEM((9 * CAP, ROWS, BLK), BF16)],
        compiler_params=pltpu.CompilerParams(vmem_limit_bytes=4 * MIB),
    )(tile_slot, tile_cell, tile_count, *parts, weight, state)


def speeds_at(props, state, speed, j, here, parts):
    mass = 1.0 + props[0, 0] * state[j, 0, here, :]
    for m in range(1, MAT):
        mass = mass + props[0, m] * state[j, m, here, :]
    share = 1.0 / mass
    for k in parts:
        speed[j, k, here, :] = state[j, MAT + k, here, :] * share


def remap_at(props, state, speed, press, fresh, j, first_row):
    count = state.shape[1]
    low = low_lanes()
    here = slice(first_row, first_row + 8)
    before = slice(first_row - 1, first_row + 7)
    after = slice(first_row + 1, first_row + 9)
    inside = slice(first_row - PAD, first_row - PAD + 8)
    scale = 0.5 * time_step
    ux = speed[j, 0, here, :]
    lower = scale * (speed[j, 0, before, :] + ux)
    upper = scale * (ux + speed[j, 0, after, :])
    uy = speed[j, 1, here, :]
    left = scale * (turn(jnp.where(low, uy, speed[j - 1, 1, here, :])) + uy)
    right = scale * (uy + turn(jnp.where(low, speed[j + 1, 1, here, :], uy)))
    keep = 1.0 - (
        jnp.maximum(upper, 0.0) + jnp.maximum(-lower, 0.0) + jnp.maximum(right, 0.0) + jnp.maximum(-left, 0.0)
    )
    take_before = jnp.maximum(lower, 0.0)
    take_after = jnp.maximum(-upper, 0.0)
    take_left = turn(jnp.maximum(left, 0.0))
    take_right = turn(jnp.maximum(-right, 0.0))
    same = jnp.where(low, take_left, take_right)
    other = jnp.where(low, take_right, take_left)
    total = None
    for q in range(count):
        mid = state[j, q, here, :]
        beside = jnp.where(low, state[j + 1, q, here, :], state[j - 1, q, here, :])
        value = keep * mid + take_before * state[j, q, before, :]
        value = value + take_after * state[j, q, after, :]
        value = value + turn(same * mid + other * beside)
        fresh[j - 1, q, inside, :] = value
        if q < MAT:
            term = value * (props[1, q] + (0.5 * props[1, q]) * value)
            total = term if total is None else total + term
        elif q == count - 1:
            total = total + 0.4 * value
    press[j - 1, inside, :] = total


def inner_kernel(props, state, remapped, press, speed, fresh, sem):
    columns, tall = state.shape[0] - 2, state.shape[2]
    tiles = (tall - 2 * PAD) // 8

    def speeds(j, carry):
        for i in range(tiles):
            speeds_at(props, state, speed, j, slice(PAD + 8 * i, PAD + 8 * i + 8), (0, 1))
        return carry

    lax.fori_loop(1, columns + 1, speeds, 0)

    def write(j):
        rows = pl.ds(8, 8 * (tiles - 2))
        lanes = pl.ds(pl.multiple_of((j - 1) * BLK, BLK), BLK)
        return pltpu.make_async_copy(fresh.at[j - 1, :, rows], remapped.at[:, rows, lanes], sem.at[j - 1])

    def remap(j, carry):
        for i in range(1, tiles - 1):
            remap_at(props, state, speed, press, fresh, j, PAD + 8 * i)
        write(j).start()
        return carry

    lax.fori_loop(2, columns, remap, 0)

    def finish(j, carry):
        write(j).wait()
        return carry

    lax.fori_loop(2, columns, finish, 0)


def inner(props, state, width):
    columns, count, tall = state.shape[0] - 2, state.shape[1], state.shape[2]
    return pl.pallas_call(
        inner_kernel,
        name="inner",
        out_shape=(
            jax.ShapeDtypeStruct((count, width, columns * BLK), F32),
            pltpu.VMEM((columns, width, BLK), F32),
            pltpu.VMEM((columns + 2, 2, tall, BLK), F32),
        ),
        in_specs=[SMEM, VMEM],
        out_specs=(ANY, VMEM, VMEM),
        scratch_shapes=[pltpu.VMEM((columns, count, width, BLK), F32), pltpu.SemaphoreType.DMA((columns,))],
        compiler_params=pltpu.CompilerParams(vmem_limit_bytes=10 * MIB),
        cost_estimate=pl.CostEstimate(flops=20 * state.size, bytes_accessed=2 * state.size * 4, transcendentals=0),
    )(props, state)


def outer_kernel(
    props, tile_slot, tile_cell, tile_count, edge_x1, edge_x2, edge_y1, edge_y2, weight, state_in, speed_in, press_in,
    remapped_in, remapped, state, speed, press, own, first, second, fresh, sums, sem, *, size_y
):
    pos_x, pos_y = lax.axis_index("gx"), lax.axis_index("gy")
    n_tiles = weight.shape[0]
    columns, count, tall = state.shape[0] - 2, state.shape[1], state.shape[2]
    width = tall - 2 * PAD
    tiles = width // 8
    even_x, even_y = (pos_x & 1) == 0, (pos_y & 1) == 0
    line = state.reshape((columns + 2) * count * tall, BLK)
    above, below = tall - PAD, PAD - 1
    for edge, row in (
        (edge_x1, jnp.where(even_x, above, below)),
        (edge_x2, jnp.where(even_x, below, above)),
    ):
        for q in range(count):
            at = pl.ds(count * tall + q * tall + row, columns, stride=count * tall)
            line[at, :] = edge[q * columns : (q + 1) * columns, :].astype(F32)
    low = low_lanes()
    for edge, column in (
        (edge_y1, jnp.where(even_y, columns + 1, 0)),
        (edge_y2, jnp.where(even_y, 0, columns + 1)),
    ):
        for q in range(count // 2):
            for i in range(width // ROWS):
                here = slice(PAD + i * ROWS, PAD + (i + 1) * ROWS)
                both = edge[q * width + i * ROWS : q * width + (i + 1) * ROWS, :].astype(F32)
                turned = turn(both)
                state[column, q, here, :] = jnp.where(low, both, turned)
                state[column, q + count // 2, here, :] = jnp.where(low, turned, both)

    def side_speeds(j, carry):
        speeds_at(props, state, speed, j, slice(0, PAD), (0,))
        speeds_at(props, state, speed, j, slice(tall - PAD, tall), (0,))
        return carry

    lax.fori_loop(1, columns + 1, side_speeds, 0)
    for j in (0, columns + 1):
        for i in range(tiles):
            speeds_at(props, state, speed, j, slice(PAD + 8 * i, PAD + 8 * i + 8), (1,))

    def write(j, first_row, rows, which):
        rows = pl.ds(first_row, rows)
        lanes = pl.ds(pl.multiple_of((j - 1) * BLK, BLK), BLK)
        return pltpu.make_async_copy(fresh.at[j - 1, :, rows], remapped.at[:, rows, lanes], sem.at[which, j - 1])

    def sides(j, carry):
        for which, i in enumerate((0, tiles - 1)):
            remap_at(props, state, speed, press, fresh, j, PAD + 8 * i)
            write(j, 8 * i, 8, which).start()
        return carry

    lax.fori_loop(1, columns + 1, sides, 0)
    for j in (1, columns):
        for i in range(1, tiles - 1):
            remap_at(props, state, speed, press, fresh, j, PAD + 8 * i)
        write(j, 8, 8 * (tiles - 2), 2).start()

    sums[...] = jnp.zeros(sums.shape, F32)
    counted = tile_count[0]
    head = lax.broadcasted_iota(jnp.int32, (ROWS, BLK), 0) == 0

    def sample(step, carry):
        for k in range(UNROLL):
            t = step * UNROLL + k
            slot = local_slot(tile_slot[t], pos_x, pos_y, size_y)
            x, j = split_device(tile_cell[t], columns)
            probe = jnp.where(head, press[j, pl.ds(x, 1), :], 1.0).astype(BF16)
            both = lax.dot_general(probe, weight[t], (((1,), (1,)), ((), ())), preferred_element_type=F32)[:8]
            sums[slot] = sums[slot] + jnp.where(t < counted, both, 0.0)
        return carry

    lax.fori_loop(0, n_tiles // UNROLL, sample, 0)
    table = sums.reshape(sums.shape[0] * 8, BLK)
    for k, out in enumerate((own, first, second)):
        top = table[pl.ds(k * 3 * CAP * 8, 3 * CAP, stride=8), :]
        under = table[pl.ds(k * 3 * CAP * 8 + 1, 3 * CAP, stride=8), :]
        out[...] = top / jnp.maximum(under, 1.0)

    def finish(j, carry):
        write(j, 0, 8, 0).wait()
        write(j, 8 * (tiles - 1), 8, 1).wait()
        return carry

    lax.fori_loop(1, columns + 1, finish, 0)
    for j in (1, columns):
        write(j, 8, 8 * (tiles - 2), 2).wait()


def outer(props, tile_slot, tile_cell, tile_count, edges, weight, state, speed, press, remapped, size_y):
    columns, count = state.shape[0] - 2, state.shape[1]
    answer = pltpu.VMEM((3 * CAP, BLK), F32)
    outs = pl.pallas_call(
        functools.partial(outer_kernel, size_y=size_y),
        name="outer",
        out_shape=(
            jax.ShapeDtypeStruct(remapped.shape, F32),
            pltpu.VMEM(state.shape, F32),
            pltpu.VMEM(speed.shape, F32),
            pltpu.VMEM(press.shape, F32),
            answer,
            answer,
            answer,
        ),
        in_specs=[SMEM] * 4 + [VMEM] * 8 + [ANY],
        out_specs=(ANY,) + (VMEM,) * 6,
        input_output_aliases={12: 0, 9: 1, 10: 2, 11: 3},
        scratch_shapes=[
            pltpu.VMEM((columns, count, remapped.shape[1], BLK), F32),
            pltpu.VMEM((9 * CAP, 8, BLK), F32),
            pltpu.SemaphoreType.DMA((3, columns)),
        ],
        compiler_params=pltpu.CompilerParams(vmem_limit_bytes=10 * MIB),
    )(props, tile_slot, tile_cell, tile_count, *edges, weight, state, speed, press, remapped)
    return outs[0], outs[4], outs[5], outs[6]


def pick_kernel(place, own, first, second, out, table):
    for k, part in enumerate((own, first, second)):
        table[k * 3 * CAP : (k + 1) * 3 * CAP, :] = part[...]
    for b in range(out.shape[0]):
        out[b : b + 1, :] = table[pl.ds(place[b], 1), :]


def pick(place, own, first, second):
    return pl.pallas_call(
        pick_kernel,
        name="pick",
        out_shape=pltpu.VMEM((place.shape[0], BLK), F32),
        in_specs=[SMEM, VMEM, VMEM, VMEM],
        out_specs=VMEM,
        scratch_shapes=[pltpu.VMEM((9 * CAP, BLK), F32)],
        compiler_params=pltpu.CompilerParams(vmem_limit_bytes=2 * MIB),
    )(place, own, first, second)


def per_device(
    elem_volume,
    elem_velocity,
    elem_energy,
    elem_mat,
    elem_dest,
    tile_slot,
    tile_cell,
    tile_weight,
    tile_count,
    cell_state,
    mat_props,
):
    size_y = lax.axis_size("gy")
    n_blocks = elem_dest.shape[0]
    shape = (n_blocks, BLK)
    own, first, second, place = payload(
        elem_dest,
        mat_props,
        elem_volume.reshape(shape),
        elem_velocity,
        elem_energy.reshape(shape),
        elem_mat.reshape(shape),
        size_y,
    )
    state = stage(cell_state)
    weight = pltpu.with_memory_space_constraint(tile_weight, pltpu.VMEM)

    first = swap(first, "gx", 1)
    second = swap(second, "gx", 2)

    def along_y(which):
        rows = slice(which * CAP, (which + 1) * CAP)
        return jnp.concatenate([own[rows], first[rows], second[rows]], axis=0)

    north = swap(along_y(1), "gy", 1)
    south = swap(along_y(2), "gy", 2)
    state, *edges = deposit(
        tile_slot, tile_cell, tile_count, (own, first, second, north, south), weight, state, size_y
    )
    edges = (
        swap(edges[0], "gx", 1, wrap=False),
        swap(edges[1], "gx", 2, wrap=False),
        swap(edges[2], "gy", 1, wrap=False),
        swap(edges[3], "gy", 2, wrap=False),
    )
    remapped, press, speed = inner(mat_props, state, cell_state.shape[1])
    remapped, own, first, second = outer(
        mat_props, tile_slot, tile_cell, tile_count, edges, weight, state, speed, press, remapped, size_y
    )
    first = swap(first, "gy", 1)
    second = swap(second, "gy", 2)

    def along_x(which):
        rows = slice(which * CAP, (which + 1) * CAP)
        return jnp.concatenate([own[rows], first[rows], second[rows]], axis=0)

    back = pick(place, along_x(0), swap(along_x(1), "gx", 1), swap(along_x(2), "gx", 2))
    return remapped, back.astype(BF16).reshape(n_blocks * BLK)


def solution(mesh):
    placed = (
        P(("gx", "gy")),
        P(None, ("gx", "gy")),
        P(("gx", "gy")),
        P(("gx", "gy")),
        P(("gx", "gy")),
        P(("gx", "gy")),
        P(("gx", "gy")),
        P(("gx", "gy"), None, None),
        P(("gx", "gy")),
        P(None, "gx", "gy"),
        P(),
    )
    return jax.shard_map(
        per_device,
        mesh=mesh,
        in_specs=placed,
        out_specs=(P(None, "gx", "gy"), P(("gx", "gy"))),
        check_vma=False,
    )
```

time: 188 us -> 60.6 us (0.32)
  other arithmetic: 84.1 us -> 0.64 us
  local copies, waits for them, and re-layouts: 45 us -> 8.09 us
  Pallas kernels: 0 us -> 23.5 us
  waiting for transfers between devices: 20.6 us -> 7.21 us
  matrix products: 12.7 us -> 0 us
  starting transfers between devices: 22.6 us -> 19.2 us
    reshape x5 -> x0, local copies, waits for them, and re-layouts: 33.4 us -> none  [the longest x1 11.8 us: per_device(): remapped = fresh.reshape(count_q, width_x, width_y * NZ)]
    sub x1 -> x0, other arithmetic: 27.3 us -> none  [per_device(): state - time_step * (flux_x[:, 1:] - flux_x[:, :-1] + flux_y[:, :, 1:] -...]
    pallas_call x0 -> x6, Pallas kernels: none -> 23.5 us  [the longest x1 10.3 us: outer(): pl.pallas_call(functools.partial(outer_kernel, size_y=size_y), name='oute...]
    mul x5 -> x0, other arithmetic: 18.8 us -> none  [the longest x4 17.5 us: face_flux(): return 0.5 * (speed * (q_lo + q_hi) - jnp.abs(speed) * (q_hi - q_lo))]
    ppermute x12, waiting for transfers between devices: 20.6 us -> 7.21 us  [swap(): return lax.ppermute(value, axis, pairs)]
    convert_element_type x3 -> x0, other arithmetic: 13.2 us -> none  [the longest x1 13.2 us: per_device(): with_halo(packed.astype(jnp.bfloat16), (('gx', 1), ('gy', 2)), 1)]
    dot_general x4 -> x0, matrix products: 12.7 us -> none  [the longest x1 4.64 us: per_device(): jnp.einsum('kt,rtc->rkc', cell_pick, contrib, precision=lax.Precision.HIG...]
    another operation x7 -> x0, other arithmetic: 11 us -> none
  transfers between devices with their start and end apart: 12 -> 12, of which waited for: 6 -> 3; matrix products, arithmetic and copies ran while one was open for 13% -> 0% of each run, Pallas kernels for 0% -> 12%
where the time goes in v1:
time: 60.6 us; the launch traced here: 60.1 us
  Pallas kernels  23.5 us (39%)
  starting transfers between devices  19.2 us (32%)
  local copies, waits for them, and re-layouts  8.09 us (13%)
  waiting for transfers between devices  7.21 us (12%)
  between operations  1.46 us (2%)
  other arithmetic  0.64 us (1%)
    ppermute x12, starting transfers between devices, swap(): return lax.ppermute(value, axis, pairs)  19.2 us
    pallas_call x1, Pallas kernels, outer(): pl.pallas_call(functools.partial(outer_kernel, size_y=size_y), name='oute...  10.3 us
    unnamed x22, local copies, waits for them, and re-layouts  8.07 us
    ppermute x12, waiting for transfers between devices, swap(): return lax.ppermute(value, axis, pairs)  7.21 us
    pallas_call x1, Pallas kernels, inner(): pl.pallas_call(inner_kernel, name='inner', out_shape=(jax.ShapeDtypeStruc...  6.34 us
    pallas_call x1, Pallas kernels, deposit(): pl.pallas_call(functools.partial(deposit_kernel, size_y=size_y), name='de...  3.95 us
    pallas_call x1, Pallas kernels, payload(): pl.pallas_call(functools.partial(payload_kernel, size_y=size_y), name='pa...  1.27 us
  transfers between devices with their start and end apart: 12, of which 3 were waited for; matrix products, arithmetic and copies ran while one was open for 0% of the time, Pallas kernels for 12%

profile of v1, /device:TPU:0, one launch (start us, length us, event | category | flops | bytes accessed | tf_op | source)
XLA Modules:
  0.0 60.1 jit_solution(6137112412753119526)
XLA Ops:
  0.6 0.0 copy-start.2
  0.6 0.8 %copy-done.2 = f32[3,2304]{1,0:T(4,128)S(1)} copy-done((f32[3,2304]{1,0:T(4,128)S(1)}, f32[3,2304]{1,0:T(4,128)}, u32[]{:S(2)}) %copy-start.2) | copy-done | bytes 27672
  1.4 0.0 copy-start.3
  1.4 0.7 %copy-done.3 = f32[2304]{0:T(1024)S(1)} copy-done((f32[2304]{0:T(1024)S(1)}, f32[2304]{0:T(1024)}, u32[]{:S(2)}) %copy-start.3) | copy-done | bytes 9240
  2.1 0.0 copy-start.4
  2.1 0.7 %copy-done.4 = f32[2304]{0:T(1024)S(1)} copy-done((f32[2304]{0:T(1024)S(1)}, f32[2304]{0:T(1024)}, u32[]{:S(2)}) %copy-start.4) | copy-done | bytes 9240
  2.8 0.0 copy-start.5
  2.8 0.7 %copy-done.5 = s32[2304]{0:T(1024)S(1)} copy-done((s32[2304]{0:T(1024)S(1)}, s32[2304]{0:T(1024)}, u32[]{:S(2)}) %copy-start.5) | copy-done | bytes 9240
  3.5 0.0 copy-start.6
  3.5 0.7 %copy-done.6 = f32[2,8]{1,0:T(2,128)S(1)} copy-done((f32[2,8]{1,0:T(2,128)S(1)}, f32[2,8]{1,0:T(2,128)}, u32[]{:S(2)}) %copy-start.6) | copy-done | bytes 88
  4.2 0.0 copy-start.10
  4.2 0.7 %copy-done.10 = s32[18]{0:T(128)S(1)} copy-done((s32[18]{0:T(128)S(1)}, s32[18]{0:T(128)}, u32[]{:S(2)}) %copy-start.10) | copy-done | bytes 96
  4.9 1.3 %payload.1 = (bf16[6,16,128]{2,1,0:T(8,128)(2,1)S(1)}, bf16[6,16,128]{2,1,0:T(8,128)(2,1)S(1)}, bf16[6,16,128]{2,1,0:T(8,128)(2,1)S(1)}, s32[18]{0:T(128)S(1)}) custom-call(s32[18]{0:T(128)S(1)} %copy-done.10, f32[2,8]{1,0:T(2,128)S(1)} %copy-done.6, f32[18,128]{1,0:T(8,128)S(1)} %bitcast.5, f32[3,2304]{1,0:T(4,128)S(1)} %copy-done.2, ...), custom_call_target="tpu_custom_call" | custom-call | tf_op jit(solution)/shard_map/payload/pallas_call | solution.py:84
  6.1 0.5 collective-permute-start
  6.7 2.6 %collective-permute-start.1 = (bf16[6,16,128]{2,1,0:T(8,128)(2,1)S(1)}, bf16[6,16,128]{2,1,0:T(8,128)(2,1)S(1)}, u32[]{:S(2)}, u32[]{:S(2)}) collective-permute-start(bf16[6,16,128]{2,1,0:T(8,128)(2,1)S(1)} %get-tuple-element.20), channel_id=1, source_target_pairs={{0,24},{8,16},{16,8},{24,0},{1,25},{9,17},{17,9},{25,1},{2,26},{10... | collective-permute-start | bytes 73736 | tf_op jit(solution)/shard_map/ppermute | solution.py:40
  9.3 0.0 collective-permute-done.first
  9.3 1.5 %collective-permute-done.1.second = bf16[6,16,128]{2,1,0:T(8,128)(2,1)S(1)} collective-permute-done((bf16[6,16,128]{2,1,0:T(8,128)(2,1)S(1)}, bf16[6,16,128]{2,1,0:T(8,128)(2,1)S(1)}, u32[]{:S(2)}, u32[]{:S(2)}) %collective-permute-start.1) | collective-permute-done | bytes 24608 | tf_op jit(solution)/shard_map/ppermute | solution.py:40
  10.8 1.7 %collective-permute-start.2 = (bf16[6,16,128]{2,1,0:T(8,128)(2,1)S(1)}, bf16[6,16,128]{2,1,0:T(8,128)(2,1)S(1)}, u32[]{:S(2)}, u32[]{:S(2)}) collective-permute-start(bf16[6,16,128]{2,1,0:T(8,128)(2,1)S(1)} %pad_maximum_fusion), channel_id=1, source_target_pairs={{0,1},{1,0},{2,3},{3,2},{4,5},{5,4},{6,7},{7,6},{8,9},{9,8},{10,11... | collective-permute-start | bytes 73736 | tf_op jit(solution)/shard_map/ppermute | solution.py:40
  12.6 3.6 %collective-permute-start.3 = (bf16[6,16,128]{2,1,0:T(8,128)(2,1)S(1)}, bf16[6,16,128]{2,1,0:T(8,128)(2,1)S(1)}, u32[]{:S(2)}, u32[]{:S(2)}) collective-permute-start(bf16[6,16,128]{2,1,0:T(8,128)(2,1)S(1)} %pad_maximum_fusion.1), channel_id=1, source_target_pairs={{0,7},{1,2},{2,1},{3,4},{4,3},{5,6},{6,5},{7,0},{8,15},{9,10},{10,... | collective-permute-start | bytes 73736 | tf_op jit(solution)/shard_map/ppermute | solution.py:40
  16.8 0.0 copy-start.1
  16.8 2.8 %copy-done.1 = f32[12,64,2048]{2,1,0:T(8,128)S(1)} copy-done((f32[12,64,2048]{2,1,0:T(8,128)S(1)}, f32[12,64,2048]{2,1,0:T(8,128)}, u32[]{:S(2)}) %copy-start.1) | copy-done | bytes 6291480
  19.6 0.0 copy-start
  19.6 0.0 copy-start.8
  19.6 0.0 copy-start.9
  19.6 1.1 %stage.1.state_in = f32[18,12,80,128]{3,2,1,0:T(8,128)S(1)} custom-call(f32[12,64,2048]{2,1,0:T(8,128)S(1)} %copy-done.1), custom_call_target="tpu_custom_call" | custom-call | bytes 12582912 | tf_op jit(solution)/shard_map/stage/pallas_call | solution.py:113
  20.7 0.0 copy-start.7
  20.7 0.0 collective-permute-done.2.north
  20.7 0.0 collective-permute-done.3.south
  20.7 1.1 %copy-done = bf16[128,128,128]{2,1,0:T(8,128)(2,1)S(1)} copy-done((bf16[128,128,128]{2,1,0:T(8,128)(2,1)S(1)}, bf16[128,128,128]{2,1,0:T(8,128)(2,1)}, u32[]{:S(2)}) %copy-start) | copy-done | bytes 4194328
  21.8 0.0 copy-done.8
  21.8 0.0 copy-done.9
  21.8 3.9 %deposit.1 = (f32[18,12,80,128]{3,2,1,0:T(8,128)S(1)}, bf16[192,128]{1,0:T(8,128)(2,1)S(1)}, bf16[192,128]{1,0:T(8,128)(2,1)S(1)}, bf16[384,128]{1,0:T(8,128)(2,1)S(1)}, bf16[384,128]{1,0:T(8,128)(2,1)S(1)}) custom-call(s32[128]{0:T(128)S(1)} %copy-done.8, s32[128]{0:T(128)S(1)} %copy-done.9, ...), custom_call_target="tpu_custom_call", output_to_operand_aliasing={{0}: (9, {})} | custom-call | tf_op jit(solution)/shard_map/deposit/pallas_call | solution.py:194
  25.7 0.1 collective-permute-start.6
  25.8 0.7 %collective-permute-start.7 = (bf16[384,128]{1,0:T(8,128)(2,1)S(1)}, bf16[384,128]{1,0:T(8,128)(2,1)S(1)}, u32[]{:S(2)}, u32[]{:S(2)}) collective-permute-start(bf16[384,128]{1,0:T(8,128)(2,1)S(1)} %get-tuple-element.24), channel_id=1, source_target_pairs={{1,2},{2,1},{3,4},{4,3},{5,6},{6,5},{9,10},{10,9},{11,12},{12,11},... | collective-permute-start | bytes 294920 | tf_op jit(solution)/shard_map/ppermute | solution.py:40
  26.5 0.1 collective-permute-start.4
  26.5 0.7 %collective-permute-start.5 = (bf16[192,128]{1,0:T(8,128)(2,1)S(1)}, bf16[192,128]{1,0:T(8,128)(2,1)S(1)}, u32[]{:S(2)}, u32[]{:S(2)}) collective-permute-start(bf16[192,128]{1,0:T(8,128)(2,1)S(1)} %get-tuple-element.22), channel_id=1, source_target_pairs={{8,16},{16,8},{9,17},{17,9},{10,18},{18,10},{11,19},{19,11},{12,20... | collective-permute-start | bytes 147464 | tf_op jit(solution)/shard_map/ppermute | solution.py:40
  27.2 0.0 copy-done.7
  27.2 6.3 %inner.1 = (f32[12,64,2048]{2,1,0:T(8,128)}, f32[16,64,128]{2,1,0:T(8,128)S(1)}, f32[18,2,80,128]{3,2,1,0:T(8,128)S(1)}) custom-call(f32[2,8]{1,0:T(2,128)S(1)} %copy-done.7, f32[18,12,80,128]{3,2,1,0:T(8,128)S(1)} %get-tuple-element.25.state.state_in), custom_call_target="tpu_custom_call" | custom-call | flops 44236800 | bytes 17694720 | tf_op jit(solution)/shard_map/inner/pallas_call | solution.py:287
  33.6 0.0 collective-permute-done.4.edge_x1
  33.6 0.0 collective-permute-done.5.edge_x2
  33.6 0.0 collective-permute-done.6.edge_y1
  33.6 0.0 collective-permute-done.7.edge_y2
  33.6 10.3 %outer.1 = (f32[12,64,2048]{2,1,0:T(8,128)}, f32[18,12,80,128]{3,2,1,0:T(8,128)S(1)}, f32[18,2,80,128]{3,2,1,0:T(8,128)S(1)}, f32[16,64,128]{2,1,0:T(8,128)S(1)}...) custom-call(f32[2,8]{1,0:T(2,128)S(1)} %copy-done.7, ...), custom_call_target="tpu_custom_call", output_to_operand_aliasing={{0}: (12, {}), {1}: (9, {}), {2}: (10, {}), {3}: (11, {})} | custom-call | tf_op jit(solution)/shard_map/outer/pallas_call | solution.py:396
  43.9 3.8 %collective-permute-start.8 = (f32[6,128]{1,0:T(8,128)S(1)}, f32[6,128]{1,0:T(8,128)S(1)}, u32[]{:S(2)}, u32[]{:S(2)}) collective-permute-start(f32[6,128]{1,0:T(8,128)S(1)} %get-tuple-element.32), channel_id=1, source_target_pairs={{0,1},{1,0},{2,3},{3,2},{4,5},{5,4},{6,7},{7,6},{8,9},{9,8},{10,11... | collective-permute-start | bytes 9224 | tf_op jit(solution)/shard_map/ppermute | solution.py:40
  47.7 1.9 %collective-permute-start.9 = (f32[6,128]{1,0:T(8,128)S(1)}, f32[6,128]{1,0:T(8,128)S(1)}, u32[]{:S(2)}, u32[]{:S(2)}) collective-permute-start(f32[6,128]{1,0:T(8,128)S(1)} %get-tuple-element.33), channel_id=1, source_target_pairs={{0,7},{1,2},{2,1},{3,4},{4,3},{5,6},{6,5},{7,0},{8,15},{9,10},{10,... | collective-permute-start | bytes 9224 | tf_op jit(solution)/shard_map/ppermute | solution.py:40
  49.7 0.0 collective-permute-done.8
  49.7 4.4 %collective-permute-done.9 = f32[6,128]{1,0:T(8,128)S(1)} collective-permute-done((f32[6,128]{1,0:T(8,128)S(1)}, f32[6,128]{1,0:T(8,128)S(1)}, u32[]{:S(2)}, u32[]{:S(2)}) %collective-permute-start.9) | collective-permute-done | bytes 3104 | tf_op jit(solution)/shard_map/ppermute | solution.py:40
  54.1 1.5 %collective-permute-start.10 = (f32[6,128]{1,0:T(8,128)S(1)}, f32[6,128]{1,0:T(8,128)S(1)}, u32[]{:S(2)}, u32[]{:S(2)}) collective-permute-start(f32[6,128]{1,0:T(8,128)S(1)} %pad_maximum_fusion.3), channel_id=1, source_target_pairs={{0,8},{8,0},{16,24},{24,16},{1,9},{9,1},{17,25},{25,17},{2,10},{10... | collective-permute-start | bytes 9224 | tf_op jit(solution)/shard_map/ppermute | solution.py:40
  55.6 2.1 %collective-permute-start.11 = (f32[6,128]{1,0:T(8,128)S(1)}, f32[6,128]{1,0:T(8,128)S(1)}, u32[]{:S(2)}, u32[]{:S(2)}) collective-permute-start(f32[6,128]{1,0:T(8,128)S(1)} %pad_maximum_fusion.4), channel_id=1, source_target_pairs={{0,24},{8,16},{16,8},{24,0},{1,25},{9,17},{17,9},{25,1},{2,26},{10... | collective-permute-start | bytes 9224 | tf_op jit(solution)/shard_map/ppermute | solution.py:40
  57.7 0.0 collective-permute-done.10.first
  57.7 1.3 %collective-permute-done.11.second = f32[6,128]{1,0:T(8,128)S(1)} collective-permute-done((f32[6,128]{1,0:T(8,128)S(1)}, f32[6,128]{1,0:T(8,128)S(1)}, u32[]{:S(2)}, u32[]{:S(2)}) %collective-permute-start.11) | collective-permute-done | bytes 3104 | tf_op jit(solution)/shard_map/ppermute | solution.py:40
  59.0 0.6 pick.1
  59.6 0.6 convert_bitcast_fusion
  (11 shorter events, 0.1 us)
Async XLA Ops:
  0.6 0.8 %copy-start.2 = (f32[3,2304]{1,0:T(4,128)S(1)}, f32[3,2304]{1,0:T(4,128)}, u32[]{:S(2)}) copy-start(f32[3,2304]{1,0:T(4,128)} %velocity.1) | copy-start | bytes 82948
  1.4 0.7 %copy-start.3 = (f32[2304]{0:T(1024)S(1)}, f32[2304]{0:T(1024)}, u32[]{:S(2)}) copy-start(f32[2304]{0:T(1024)} %param.11) | copy-start | bytes 27652
  2.1 0.7 %copy-start.4 = (f32[2304]{0:T(1024)S(1)}, f32[2304]{0:T(1024)}, u32[]{:S(2)}) copy-start(f32[2304]{0:T(1024)} %param.13) | copy-start | bytes 27652
  2.8 0.7 %copy-start.5 = (s32[2304]{0:T(1024)S(1)}, s32[2304]{0:T(1024)}, u32[]{:S(2)}) copy-start(s32[2304]{0:T(1024)} %param.14) | copy-start | bytes 27652
  3.5 0.7 %copy-start.6 = (f32[2,8]{1,0:T(2,128)S(1)}, f32[2,8]{1,0:T(2,128)}, u32[]{:S(2)}) copy-start(f32[2,8]{1,0:T(2,128)} %props.5) | copy-start | bytes 196
  4.2 0.7 %copy-start.10 = (s32[18]{0:T(128)S(1)}, s32[18]{0:T(128)}, u32[]{:S(2)}) copy-start(s32[18]{0:T(128)} %dest.1) | copy-start | bytes 220
  6.1 3.2 %collective-permute-start = (bf16[6,16,128]{2,1,0:T(8,128)(2,1)S(1)}, bf16[6,16,128]{2,1,0:T(8,128)(2,1)S(1)}, u32[]{:S(2)}, u32[]{:S(2)}) collective-permute-start(bf16[6,16,128]{2,1,0:T(8,128)(2,1)S(1)} %get-tuple-element.19), channel_id=1, source_target_pairs={{0,8},{8,0},{16,24},{24,16},{1,9},{9,1},{17,25},{25,17},{2,10},{10... | collective-permute-start | bytes 73736 | tf_op jit(solution)/shard_map/ppermute | solution.py:40
  6.7 4.2 %collective-permute-start.1 = (bf16[6,16,128]{2,1,0:T(8,128)(2,1)S(1)}, bf16[6,16,128]{2,1,0:T(8,128)(2,1)S(1)}, u32[]{:S(2)}, u32[]{:S(2)}) collective-permute-start(bf16[6,16,128]{2,1,0:T(8,128)(2,1)S(1)} %get-tuple-element.20), channel_id=1, source_target_pairs={{0,24},{8,16},{16,8},{24,0},{1,25},{9,17},{17,9},{25,1},{2,26},{10... | collective-permute-start | bytes 73736 | tf_op jit(solution)/shard_map/ppermute | solution.py:40
  10.8 9.8 %collective-permute-start.2 = (bf16[6,16,128]{2,1,0:T(8,128)(2,1)S(1)}, bf16[6,16,128]{2,1,0:T(8,128)(2,1)S(1)}, u32[]{:S(2)}, u32[]{:S(2)}) collective-permute-start(bf16[6,16,128]{2,1,0:T(8,128)(2,1)S(1)} %pad_maximum_fusion), channel_id=1, source_target_pairs={{0,1},{1,0},{2,3},{3,2},{4,5},{5,4},{6,7},{7,6},{8,9},{9,8},{10,11... | collective-permute-start | bytes 73736 | tf_op jit(solution)/shard_map/ppermute | solution.py:40
  12.6 8.1 %collective-permute-start.3 = (bf16[6,16,128]{2,1,0:T(8,128)(2,1)S(1)}, bf16[6,16,128]{2,1,0:T(8,128)(2,1)S(1)}, u32[]{:S(2)}, u32[]{:S(2)}) collective-permute-start(bf16[6,16,128]{2,1,0:T(8,128)(2,1)S(1)} %pad_maximum_fusion.1), channel_id=1, source_target_pairs={{0,7},{1,2},{2,1},{3,4},{4,3},{5,6},{6,5},{7,0},{8,15},{9,10},{10,... | collective-permute-start | bytes 73736 | tf_op jit(solution)/shard_map/ppermute | solution.py:40
  16.8 2.8 %copy-start.1 = (f32[12,64,2048]{2,1,0:T(8,128)S(1)}, f32[12,64,2048]{2,1,0:T(8,128)}, u32[]{:S(2)}) copy-start(f32[12,64,2048]{2,1,0:T(8,128)} %cell.1) | copy-start | bytes 18874372
  19.6 2.2 %copy-start = (bf16[128,128,128]{2,1,0:T(8,128)(2,1)S(1)}, bf16[128,128,128]{2,1,0:T(8,128)(2,1)}, u32[]{:S(2)}) copy-start(bf16[128,128,128]{2,1,0:T(8,128)(2,1)} %weight.3) | copy-start | bytes 12582916
  19.6 2.2 %copy-start.8 = (s32[128]{0:T(128)S(1)}, s32[128]{0:T(128)}, u32[]{:S(2)}) copy-start(s32[128]{0:T(128)} %tile_slot.3) | copy-start | bytes 1540
  19.6 2.2 %copy-start.9 = (s32[128]{0:T(128)S(1)}, s32[128]{0:T(128)}, u32[]{:S(2)}) copy-start(s32[128]{0:T(128)} %tile_cell.3) | copy-start | bytes 1540
  20.7 6.6 %copy-start.7 = (f32[2,8]{1,0:T(2,128)S(1)}, f32[2,8]{1,0:T(2,128)}, u32[]{:S(2)}) copy-start(f32[2,8]{1,0:T(2,128)} %props.5) | copy-start | bytes 196
  25.7 7.9 %collective-permute-start.6 = (bf16[384,128]{1,0:T(8,128)(2,1)S(1)}, bf16[384,128]{1,0:T(8,128)(2,1)S(1)}, u32[]{:S(2)}, u32[]{:S(2)}) collective-permute-start(bf16[384,128]{1,0:T(8,128)(2,1)S(1)} %get-tuple-element.23), channel_id=1, source_target_pairs={{0,1},{1,0},{2,3},{3,2},{4,5},{5,4},{6,7},{7,6},{8,9},{9,8},{10,11... | collective-permute-start | bytes 294920 | tf_op jit(solution)/shard_map/ppermute | solution.py:40
  25.8 7.8 %collective-permute-start.7 = (bf16[384,128]{1,0:T(8,128)(2,1)S(1)}, bf16[384,128]{1,0:T(8,128)(2,1)S(1)}, u32[]{:S(2)}, u32[]{:S(2)}) collective-permute-start(bf16[384,128]{1,0:T(8,128)(2,1)S(1)} %get-tuple-element.24), channel_id=1, source_target_pairs={{1,2},{2,1},{3,4},{4,3},{5,6},{6,5},{9,10},{10,9},{11,12},{12,11},... | collective-permute-start | bytes 294920 | tf_op jit(solution)/shard_map/ppermute | solution.py:40
  26.5 7.1 %collective-permute-start.4 = (bf16[192,128]{1,0:T(8,128)(2,1)S(1)}, bf16[192,128]{1,0:T(8,128)(2,1)S(1)}, u32[]{:S(2)}, u32[]{:S(2)}) collective-permute-start(bf16[192,128]{1,0:T(8,128)(2,1)S(1)} %get-tuple-element.21), channel_id=1, source_target_pairs={{0,8},{8,0},{16,24},{24,16},{1,9},{9,1},{17,25},{25,17},{2,10},{10... | collective-permute-start | bytes 147464 | tf_op jit(solution)/shard_map/ppermute | solution.py:40
  26.5 7.0 %collective-permute-start.5 = (bf16[192,128]{1,0:T(8,128)(2,1)S(1)}, bf16[192,128]{1,0:T(8,128)(2,1)S(1)}, u32[]{:S(2)}, u32[]{:S(2)}) collective-permute-start(bf16[192,128]{1,0:T(8,128)(2,1)S(1)} %get-tuple-element.22), channel_id=1, source_target_pairs={{8,16},{16,8},{9,17},{17,9},{10,18},{18,10},{11,19},{19,11},{12,20... | collective-permute-start | bytes 147464 | tf_op jit(solution)/shard_map/ppermute | solution.py:40
  43.9 5.7 %collective-permute-start.8 = (f32[6,128]{1,0:T(8,128)S(1)}, f32[6,128]{1,0:T(8,128)S(1)}, u32[]{:S(2)}, u32[]{:S(2)}) collective-permute-start(f32[6,128]{1,0:T(8,128)S(1)} %get-tuple-element.32), channel_id=1, source_target_pairs={{0,1},{1,0},{2,3},{3,2},{4,5},{5,4},{6,7},{7,6},{8,9},{9,8},{10,11... | collective-permute-start | bytes 9224 | tf_op jit(solution)/shard_map/ppermute | solution.py:40
  47.7 6.3 %collective-permute-start.9 = (f32[6,128]{1,0:T(8,128)S(1)}, f32[6,128]{1,0:T(8,128)S(1)}, u32[]{:S(2)}, u32[]{:S(2)}) collective-permute-start(f32[6,128]{1,0:T(8,128)S(1)} %get-tuple-element.33), channel_id=1, source_target_pairs={{0,7},{1,2},{2,1},{3,4},{4,3},{5,6},{6,5},{7,0},{8,15},{9,10},{10,... | collective-permute-start | bytes 9224 | tf_op jit(solution)/shard_map/ppermute | solution.py:40
  54.1 3.6 %collective-permute-start.10 = (f32[6,128]{1,0:T(8,128)S(1)}, f32[6,128]{1,0:T(8,128)S(1)}, u32[]{:S(2)}, u32[]{:S(2)}) collective-permute-start(f32[6,128]{1,0:T(8,128)S(1)} %pad_maximum_fusion.3), channel_id=1, source_target_pairs={{0,8},{8,0},{16,24},{24,16},{1,9},{9,1},{17,25},{25,17},{2,10},{10... | collective-permute-start | bytes 9224 | tf_op jit(solution)/shard_map/ppermute | solution.py:40
  55.6 3.4 %collective-permute-start.11 = (f32[6,128]{1,0:T(8,128)S(1)}, f32[6,128]{1,0:T(8,128)S(1)}, u32[]{:S(2)}, u32[]{:S(2)}) collective-permute-start(f32[6,128]{1,0:T(8,128)S(1)} %pad_maximum_fusion.4), channel_id=1, source_target_pairs={{0,24},{8,16},{16,8},{24,0},{1,25},{9,17},{17,9},{25,1},{2,26},{10... | collective-permute-start | bytes 9224 | tf_op jit(solution)/shard_map/ppermute | solution.py:40

commit v2 on v1

--- a/solution.py
+++ b/solution.py
@@ -14,7 +14,7 @@
 HALF = BLK // 2
 PAD = 8
 ROWS = 16
-UNROLL = 8
+UNROLL = 32
 MIB = 2**20
 
 time_step = 0.8
@@ -50,7 +50,23 @@
     return lax.div(device, size), lax.rem(device, size)
 
 
-def payload_kernel(dest, props, volume, velocity, energy, mat, own, first, second, place, seen, packed, *, size_y):
+def in_hbm(value):
+    return pltpu.with_memory_space_constraint(value, pltpu.HBM)
+
+
+def payload_kernel(
+    dest_hbm, props_hbm, volume_hbm, velocity_hbm, energy_hbm, mat_hbm, own, first, second, place,
+    dest, props, volume, velocity, energy, mat, seen, packed, sem, *, size_y
+):
+    moves = (
+        (dest_hbm, dest), (props_hbm, props), (mat_hbm, mat),
+        (volume_hbm, volume), (velocity_hbm, velocity), (energy_hbm, energy),
+    )
+    copies = [pltpu.make_async_copy(src, dst, sem.at[k]) for k, (src, dst) in enumerate(moves)]
+    for copy in copies:
+        copy.start()
+    for copy in copies:
+        copy.wait()
     pos_x, pos_y = lax.axis_index("gx"), lax.axis_index("gy")
     n_blocks = volume.shape[0]
     kinds = mat[...]
@@ -85,11 +101,21 @@
         functools.partial(payload_kernel, size_y=size_y),
         name="payload",
         out_shape=(parcel, parcel, parcel, jax.ShapeDtypeStruct((n_blocks,), jnp.int32)),
-        in_specs=[SMEM, SMEM, VMEM, VMEM, VMEM, VMEM],
+        in_specs=[ANY] * 6,
         out_specs=(VMEM, VMEM, VMEM, SMEM),
-        scratch_shapes=[pltpu.SMEM((9,), jnp.int32), pltpu.VMEM((9 * CAP, ROWS, BLK), BF16)],
+        scratch_shapes=[
+            pltpu.SMEM(dest.shape, jnp.int32),
+            pltpu.SMEM(props.shape, F32),
+            pltpu.VMEM(volume.shape, F32),
+            pltpu.VMEM(velocity.shape, F32),
+            pltpu.VMEM(energy.shape, F32),
+            pltpu.VMEM(mat.shape, jnp.int32),
+            pltpu.SMEM((9,), jnp.int32),
+            pltpu.VMEM((9 * CAP, ROWS, BLK), BF16),
+            pltpu.SemaphoreType.DMA((6,)),
+        ],
         compiler_params=pltpu.CompilerParams(vmem_limit_bytes=4 * MIB),
-    )(dest, props, volume, velocity, energy, mat)
+    )(*(in_hbm(value) for value in (dest, props, volume, velocity, energy, mat)))
 
 
 def stage_kernel(cell, state, sem):
@@ -119,7 +145,26 @@
         scratch_shapes=[pltpu.SemaphoreType.DMA((columns,))],
         compiler_params=pltpu.CompilerParams(vmem_limit_bytes=2 * MIB),
         cost_estimate=pl.CostEstimate(flops=0, bytes_accessed=2 * cell.size * 4, transcendentals=0),
-    )(cell)
+    )(in_hbm(cell))
+
+
+def fetch_kernel(source, target, sem):
+    copy = pltpu.make_async_copy(source, target, sem)
+    copy.start()
+    copy.wait()
+
+
+def fetch(value):
+    return pl.pallas_call(
+        fetch_kernel,
+        name="fetch",
+        out_shape=pltpu.VMEM(value.shape, value.dtype),
+        in_specs=[ANY],
+        out_specs=VMEM,
+        scratch_shapes=[pltpu.SemaphoreType.DMA],
+        compiler_params=pltpu.CompilerParams(vmem_limit_bytes=2 * MIB),
+        cost_estimate=pl.CostEstimate(flops=0, bytes_accessed=2 * value.size * 2, transcendentals=0),
+    )(in_hbm(value))
 
 
 def local_slot(slot, pos_x, pos_y, size_y):
@@ -203,52 +248,86 @@
     )(tile_slot, tile_cell, tile_count, *parts, weight, state)
 
 
-def speeds_at(props, state, speed, j, here, parts):
-    mass = 1.0 + props[0, 0] * state[j, 0, here, :]
-    for m in range(1, MAT):
-        mass = mass + props[0, m] * state[j, m, here, :]
-    share = 1.0 / mass
-    for k in parts:
-        speed[j, k, here, :] = state[j, MAT + k, here, :] * share
-
-
-def remap_at(props, state, speed, press, fresh, j, first_row):
+def speeds_at(props, state, j, here, parts):
+    terms = [props[0, m] * state[j, m, here, :] for m in range(MAT)]
+    while len(terms) > 1:
+        terms = [a + b for a, b in zip(terms[::2], terms[1::2], strict=True)]
+    share = 1.0 / (1.0 + terms[0])
+    found = []
+    if 0 in parts:
+        found.append((0, state[j, MAT, here, :] * share))
+    if 1 in parts:
+        along = state[j, MAT + 1, here, :] * share
+        found += [(1, along), (2, turn(along))]
+    return found
+
+
+def store_speeds(props, state, speed, j, first_rows, parts):
+    rows = [slice(first, first + 8) for first in first_rows]
+    found = [speeds_at(props, state, j, here, parts) for here in rows]
+    for here, planes in zip(rows, found, strict=True):
+        for plane, value in planes:
+            speed[j, plane, here, :] = value
+
+
+def weights_at(speed, j, first_row):
+    low = low_lanes()
+    here = slice(first_row, first_row + 8)
+    scale = 0.5 * time_step
+    ux = speed[j, 0, here, :]
+    lower = scale * (speed[j, 0, slice(first_row - 1, first_row + 7), :] + ux)
+    upper = scale * (ux + speed[j, 0, slice(first_row + 1, first_row + 9), :])
+    uy, before, after = (speed[k, 1, here, :] for k in (j, j - 1, j + 1))
+    turned, turned_before, turned_after = (speed[k, 2, here, :] for k in (j, j - 1, j + 1))
+    left = scale * (jnp.where(low, turned_before, turned) + uy)
+    right = scale * (uy + jnp.where(low, turned, turned_after))
+    keep = 1.0 - (
+        (jnp.maximum(upper, 0.0) + jnp.maximum(-lower, 0.0)) + (jnp.maximum(right, 0.0) + jnp.maximum(-left, 0.0))
+    )
+    take_left = jnp.maximum(scale * (jnp.where(low, uy, before) + turned), 0.0)
+    take_right = jnp.maximum(-scale * (turned + jnp.where(low, after, uy)), 0.0)
+    same = jnp.where(low, take_left, take_right)
+    other = jnp.where(low, take_right, take_left)
+    return keep, jnp.maximum(lower, 0.0), jnp.maximum(-upper, 0.0), same, other
+
+
+def remap_at(props, state, weights, j, first_row):
     count = state.shape[1]
     low = low_lanes()
     here = slice(first_row, first_row + 8)
     before = slice(first_row - 1, first_row + 7)
     after = slice(first_row + 1, first_row + 9)
-    inside = slice(first_row - PAD, first_row - PAD + 8)
-    scale = 0.5 * time_step
-    ux = speed[j, 0, here, :]
-    lower = scale * (speed[j, 0, before, :] + ux)
-    upper = scale * (ux + speed[j, 0, after, :])
-    uy = speed[j, 1, here, :]
-    left = scale * (turn(jnp.where(low, uy, speed[j - 1, 1, here, :])) + uy)
-    right = scale * (uy + turn(jnp.where(low, speed[j + 1, 1, here, :], uy)))
-    keep = 1.0 - (
-        jnp.maximum(upper, 0.0) + jnp.maximum(-lower, 0.0) + jnp.maximum(right, 0.0) + jnp.maximum(-left, 0.0)
-    )
-    take_before = jnp.maximum(lower, 0.0)
-    take_after = jnp.maximum(-upper, 0.0)
-    take_left = turn(jnp.maximum(left, 0.0))
-    take_right = turn(jnp.maximum(-right, 0.0))
-    same = jnp.where(low, take_left, take_right)
-    other = jnp.where(low, take_right, take_left)
+    keep, take_before, take_after, same, other = weights
+    values = []
     total = None
     for q in range(count):
         mid = state[j, q, here, :]
         beside = jnp.where(low, state[j + 1, q, here, :], state[j - 1, q, here, :])
-        value = keep * mid + take_before * state[j, q, before, :]
-        value = value + take_after * state[j, q, after, :]
+        value = (keep * mid + take_before * state[j, q, before, :]) + take_after * state[j, q, after, :]
         value = value + turn(same * mid + other * beside)
-        fresh[j - 1, q, inside, :] = value
+        values.append(value)
         if q < MAT:
             term = value * (props[1, q] + (0.5 * props[1, q]) * value)
             total = term if total is None else total + term
         elif q == count - 1:
             total = total + 0.4 * value
-    press[j - 1, inside, :] = total
+    return values, total
+
+
+def remap_tiles(props, state, speed, press, fresh, j, first_rows):
+    def store(first_row, values, total):
+        inside = slice(first_row - PAD, first_row - PAD + 8)
+        for q, value in enumerate(values):
+            fresh[j - 1, q, inside, :] = value
+        press[j - 1, inside, :] = total
+
+    waiting = None
+    for first_row in first_rows:
+        found = (first_row, *remap_at(props, state, weights_at(speed, j, first_row), j, first_row))
+        if waiting is not None:
+            store(*waiting)
+        waiting = found
+    store(*waiting)
 
 
 def inner_kernel(props, state, remapped, press, speed, fresh, sem):
@@ -256,8 +335,7 @@
     tiles = (tall - 2 * PAD) // 8
 
     def speeds(j, carry):
-        for i in range(tiles):
-            speeds_at(props, state, speed, j, slice(PAD + 8 * i, PAD + 8 * i + 8), (0, 1))
+        store_speeds(props, state, speed, j, range(PAD, tall - PAD, 8), (0, 1))
         return carry
 
     lax.fori_loop(1, columns + 1, speeds, 0)
@@ -268,8 +346,7 @@
         return pltpu.make_async_copy(fresh.at[j - 1, :, rows], remapped.at[:, rows, lanes], sem.at[j - 1])
 
     def remap(j, carry):
-        for i in range(1, tiles - 1):
-            remap_at(props, state, speed, press, fresh, j, PAD + 8 * i)
+        remap_tiles(props, state, speed, press, fresh, j, range(PAD + 8, tall - PAD - 8, 8))
         write(j).start()
         return carry
 
@@ -290,7 +367,7 @@
         out_shape=(
             jax.ShapeDtypeStruct((count, width, columns * BLK), F32),
             pltpu.VMEM((columns, width, BLK), F32),
-            pltpu.VMEM((columns + 2, 2, tall, BLK), F32),
+            pltpu.VMEM((columns + 2, 3, tall, BLK), F32),
         ),
         in_specs=[SMEM, VMEM],
         out_specs=(ANY, VMEM, VMEM),
@@ -333,14 +410,12 @@
                 state[column, q + count // 2, here, :] = jnp.where(low, turned, both)
 
     def side_speeds(j, carry):
-        speeds_at(props, state, speed, j, slice(0, PAD), (0,))
-        speeds_at(props, state, speed, j, slice(tall - PAD, tall), (0,))
+        store_speeds(props, state, speed, j, (0, tall - PAD), (0,))
         return carry
 
     lax.fori_loop(1, columns + 1, side_speeds, 0)
     for j in (0, columns + 1):
-        for i in range(tiles):
-            speeds_at(props, state, speed, j, slice(PAD + 8 * i, PAD + 8 * i + 8), (1,))
+        store_speeds(props, state, speed, j, range(PAD, tall - PAD, 8), (1,))
 
     def write(j, first_row, rows, which):
         rows = pl.ds(first_row, rows)
@@ -348,15 +423,14 @@
         return pltpu.make_async_copy(fresh.at[j - 1, :, rows], remapped.at[:, rows, lanes], sem.at[which, j - 1])
 
     def sides(j, carry):
+        remap_tiles(props, state, speed, press, fresh, j, (PAD, tall - PAD - 8))
         for which, i in enumerate((0, tiles - 1)):
-            remap_at(props, state, speed, press, fresh, j, PAD + 8 * i)
             write(j, 8 * i, 8, which).start()
         return carry
 
     lax.fori_loop(1, columns + 1, sides, 0)
     for j in (1, columns):
-        for i in range(1, tiles - 1):
-            remap_at(props, state, speed, press, fresh, j, PAD + 8 * i)
+        remap_tiles(props, state, speed, press, fresh, j, range(PAD + 8, tall - PAD - 8, 8))
         write(j, 8, 8 * (tiles - 2), 2).start()
 
     sums[...] = jnp.zeros(sums.shape, F32)
@@ -463,17 +537,17 @@
         size_y,
     )
     state = stage(cell_state)
-    weight = pltpu.with_memory_space_constraint(tile_weight, pltpu.VMEM)
-
+    weight = fetch(tile_weight)
+
+    second = swap(second, "gx", 2)
     first = swap(first, "gx", 1)
-    second = swap(second, "gx", 2)
 
     def along_y(which):
         rows = slice(which * CAP, (which + 1) * CAP)
         return jnp.concatenate([own[rows], first[rows], second[rows]], axis=0)
 
+    south = swap(along_y(2), "gy", 2)
     north = swap(along_y(1), "gy", 1)
-    south = swap(along_y(2), "gy", 2)
     state, *edges = deposit(
         tile_slot, tile_cell, tile_count, (own, first, second, north, south), weight, state, size_y
     )
@@ -487,8 +561,8 @@
     remapped, own, first, second = outer(
         mat_props, tile_slot, tile_cell, tile_count, edges, weight, state, speed, press, remapped, size_y
     )
+    second = swap(second, "gy", 2)
     first = swap(first, "gy", 1)
-    second = swap(second, "gy", 2)
 
     def along_x(which):
         rows = slice(which * CAP, (which + 1) * CAP)

time: 60.6 us -> 50.8 us (0.84)
  local copies, waits for them, and re-layouts: 8.09 us -> 0.04 us
  Pallas kernels: 23.5 us -> 22 us
    unnamed x22 -> x6, local copies, waits for them, and re-layouts: 8.07 us -> 0.02 us
    pallas_call x1, Pallas kernels: 10.3 us -> 6.56 us  [outer(): pl.pallas_call(functools.partial(outer_kernel, size_y=size_y), name='oute...]
    pallas_call x0 -> x1, Pallas kernels: none -> 2.2 us  [fetch(): pl.pallas_call(fetch_kernel, name='fetch', out_shape=pltpu.VMEM(value.sha...]
    pallas_call x1, Pallas kernels: 1.08 us -> 3.03 us  [stage(): pl.pallas_call(stage_kernel, name='stage', out_shape=pltpu.VMEM((columns...]
    pallas_call x1, Pallas kernels: 3.95 us -> 2.53 us  [deposit(): pl.pallas_call(functools.partial(deposit_kernel, size_y=size_y), name='de...]
    pallas_call x1, Pallas kernels: 6.34 us -> 5.51 us  [inner(): pl.pallas_call(inner_kernel, name='inner', out_shape=(jax.ShapeDtypeStruc...]
  transfers between devices with their start and end apart: 12 -> 12, of which waited for: 3 -> 3; matrix products, arithmetic and copies ran while one was open for 0% -> 0% of each run, Pallas kernels for 12% -> 21%
where the time goes in v2:
time: 50.8 us; the launch traced here: 50.6 us
  Pallas kernels  22 us (43%)
  starting transfers between devices  19.2 us (38%)
  waiting for transfers between devices  7.21 us (14%)
  between operations  1.48 us (3%)
  other arithmetic  0.64 us (1%)
    ppermute x12, starting transfers between devices, swap(): return lax.ppermute(value, axis, pairs)  19.2 us
    ppermute x12, waiting for transfers between devices, swap(): return lax.ppermute(value, axis, pairs)  7.21 us
    pallas_call x1, Pallas kernels, outer(): pl.pallas_call(functools.partial(outer_kernel, size_y=size_y), name='oute...  6.56 us
    pallas_call x1, Pallas kernels, inner(): pl.pallas_call(inner_kernel, name='inner', out_shape=(jax.ShapeDtypeStruc...  5.51 us
    pallas_call x1, Pallas kernels, stage(): pl.pallas_call(stage_kernel, name='stage', out_shape=pltpu.VMEM((columns...  3.03 us
    pallas_call x1, Pallas kernels, deposit(): pl.pallas_call(functools.partial(deposit_kernel, size_y=size_y), name='de...  2.53 us
    pallas_call x1, Pallas kernels, fetch(): pl.pallas_call(fetch_kernel, name='fetch', out_shape=pltpu.VMEM(value.sha...  2.2 us
    pallas_call x1, Pallas kernels, payload(): pl.pallas_call(functools.partial(payload_kernel, size_y=size_y), name='pa...  1.57 us
  transfers between devices with their start and end apart: 12, of which 3 were waited for; matrix products, arithmetic and copies ran while one was open for 0% of the time, Pallas kernels for 21%

profile of v2, /device:TPU:0, one launch (start us, length us, event | category | flops | bytes accessed | tf_op | source)
XLA Modules:
  0.0 50.6 jit_solution(8894078924719028226)
XLA Ops:
  0.6 1.6 %payload.1 = (bf16[6,16,128]{2,1,0:T(8,128)(2,1)S(1)}, bf16[6,16,128]{2,1,0:T(8,128)(2,1)S(1)}, bf16[6,16,128]{2,1,0:T(8,128)(2,1)S(1)}, s32[18]{0:T(128)S(1)}) custom-call(s32[18]{0:T(128)} %dest_hbm.1, f32[2,8]{1,0:T(2,128)} %props.3, f32[18,128]{1,0:T(8,128)} %bitcast.5, f32[3,2304]{1,0:T(4,128)} %velocity_hbm.1, f32[18,128]{1,0:T(8,128)} %bitcast.6, ...), custom_call_target="tpu_custom_call" | custom-call | tf_op jit(solution)/shard_map/payload/pallas_call | solution.py:100
  2.2 0.5 %collective-permute-start = (bf16[6,16,128]{2,1,0:T(8,128)(2,1)S(1)}, bf16[6,16,128]{2,1,0:T(8,128)(2,1)S(1)}, u32[]{:S(2)}, u32[]{:S(2)}) collective-permute-start(bf16[6,16,128]{2,1,0:T(8,128)(2,1)S(1)} %get-tuple-element.19), channel_id=1, source_target_pairs={{0,8},{8,0},{16,24},{24,16},{1,9},{9,1},{17,25},{25,17},{2,10},{10... | collective-permute-start | bytes 73736 | tf_op jit(solution)/shard_map/ppermute | solution.py:40
  2.7 2.6 %collective-permute-start.1 = (bf16[6,16,128]{2,1,0:T(8,128)(2,1)S(1)}, bf16[6,16,128]{2,1,0:T(8,128)(2,1)S(1)}, u32[]{:S(2)}, u32[]{:S(2)}) collective-permute-start(bf16[6,16,128]{2,1,0:T(8,128)(2,1)S(1)} %get-tuple-element.20), channel_id=1, source_target_pairs={{0,24},{8,16},{16,8},{24,0},{1,25},{9,17},{17,9},{25,1},{2,26},{10... | collective-permute-start | bytes 73736 | tf_op jit(solution)/shard_map/ppermute | solution.py:40
  5.4 0.0 collective-permute-done.first
  5.4 1.5 %collective-permute-done.1.second = bf16[6,16,128]{2,1,0:T(8,128)(2,1)S(1)} collective-permute-done((bf16[6,16,128]{2,1,0:T(8,128)(2,1)S(1)}, bf16[6,16,128]{2,1,0:T(8,128)(2,1)S(1)}, u32[]{:S(2)}, u32[]{:S(2)}) %collective-permute-start.1) | collective-permute-done | bytes 24608 | tf_op jit(solution)/shard_map/ppermute | solution.py:40
  6.9 1.7 %collective-permute-start.2 = (bf16[6,16,128]{2,1,0:T(8,128)(2,1)S(1)}, bf16[6,16,128]{2,1,0:T(8,128)(2,1)S(1)}, u32[]{:S(2)}, u32[]{:S(2)}) collective-permute-start(bf16[6,16,128]{2,1,0:T(8,128)(2,1)S(1)} %pad_maximum_fusion), channel_id=1, source_target_pairs={{0,1},{1,0},{2,3},{3,2},{4,5},{5,4},{6,7},{7,6},{8,9},{9,8},{10,11... | collective-permute-start | bytes 73736 | tf_op jit(solution)/shard_map/ppermute | solution.py:40
  8.6 3.6 %collective-permute-start.3 = (bf16[6,16,128]{2,1,0:T(8,128)(2,1)S(1)}, bf16[6,16,128]{2,1,0:T(8,128)(2,1)S(1)}, u32[]{:S(2)}, u32[]{:S(2)}) collective-permute-start(bf16[6,16,128]{2,1,0:T(8,128)(2,1)S(1)} %pad_maximum_fusion.1), channel_id=1, source_target_pairs={{0,7},{1,2},{2,1},{3,4},{4,3},{5,6},{6,5},{7,0},{8,15},{9,10},{10,... | collective-permute-start | bytes 73736 | tf_op jit(solution)/shard_map/ppermute | solution.py:40
  12.9 2.2 %fetch.1.weight = bf16[128,128,128]{2,1,0:T(8,128)(2,1)S(1)} custom-call(bf16[128,128,128]{2,1,0:T(8,128)(2,1)} %source.1), custom_call_target="tpu_custom_call" | custom-call | bytes 8388608 | tf_op jit(solution)/shard_map/fetch/pallas_call | solution.py:158
  15.1 0.0 copy-start.1
  15.1 0.0 copy-start.2
  15.1 3.0 %stage.1.state_in = f32[18,12,80,128]{3,2,1,0:T(8,128)S(1)} custom-call(f32[12,64,2048]{2,1,0:T(8,128)} %cell.1), custom_call_target="tpu_custom_call" | custom-call | bytes 12582912 | tf_op jit(solution)/shard_map/stage/pallas_call | solution.py:139
  18.1 0.0 copy-start
  18.1 0.0 collective-permute-done.2.north
  18.1 0.0 collective-permute-done.3.south
  18.2 0.0 copy-done.1
  18.2 0.0 copy-done.2
  18.2 2.5 %deposit.1 = (f32[18,12,80,128]{3,2,1,0:T(8,128)S(1)}, bf16[192,128]{1,0:T(8,128)(2,1)S(1)}, bf16[192,128]{1,0:T(8,128)(2,1)S(1)}, bf16[384,128]{1,0:T(8,128)(2,1)S(1)}, bf16[384,128]{1,0:T(8,128)(2,1)S(1)}) custom-call(s32[128]{0:T(128)S(1)} %copy-done.1, s32[128]{0:T(128)S(1)} %copy-done.2, ...), custom_call_target="tpu_custom_call", output_to_operand_aliasing={{0}: (9, {})} | custom-call | tf_op jit(solution)/shard_map/deposit/pallas_call | solution.py:239
  20.7 0.1 collective-permute-start.6
  20.8 0.7 %collective-permute-start.7 = (bf16[384,128]{1,0:T(8,128)(2,1)S(1)}, bf16[384,128]{1,0:T(8,128)(2,1)S(1)}, u32[]{:S(2)}, u32[]{:S(2)}) collective-permute-start(bf16[384,128]{1,0:T(8,128)(2,1)S(1)} %get-tuple-element.24), channel_id=1, source_target_pairs={{1,2},{2,1},{3,4},{4,3},{5,6},{6,5},{9,10},{10,9},{11,12},{12,11},... | collective-permute-start | bytes 294920 | tf_op jit(solution)/shard_map/ppermute | solution.py:40
  21.5 0.1 collective-permute-start.4
  21.5 0.7 %collective-permute-start.5 = (bf16[192,128]{1,0:T(8,128)(2,1)S(1)}, bf16[192,128]{1,0:T(8,128)(2,1)S(1)}, u32[]{:S(2)}, u32[]{:S(2)}) collective-permute-start(bf16[192,128]{1,0:T(8,128)(2,1)S(1)} %get-tuple-element.22), channel_id=1, source_target_pairs={{8,16},{16,8},{9,17},{17,9},{10,18},{18,10},{11,19},{19,11},{12,20... | collective-permute-start | bytes 147464 | tf_op jit(solution)/shard_map/ppermute | solution.py:40
  22.2 0.0 copy-done
  22.2 5.5 %inner.1 = (f32[12,64,2048]{2,1,0:T(8,128)}, f32[16,64,128]{2,1,0:T(8,128)S(1)}, f32[18,3,80,128]{3,2,1,0:T(8,128)S(1)}) custom-call(f32[2,8]{1,0:T(2,128)S(1)} %copy-done, f32[18,12,80,128]{3,2,1,0:T(8,128)S(1)} %get-tuple-element.25.state.state_in), custom_call_target="tpu_custom_call" | custom-call | flops 44236800 | bytes 17694720 | tf_op jit(solution)/shard_map/inner/pallas_call | solution.py:364
  27.7 0.0 collective-permute-done.4.edge_x1
  27.8 0.0 collective-permute-done.5.edge_x2
  27.8 0.0 collective-permute-done.6.edge_y1
  27.8 0.0 collective-permute-done.7.edge_y2
  27.8 6.6 %outer.1 = (f32[12,64,2048]{2,1,0:T(8,128)}, f32[18,12,80,128]{3,2,1,0:T(8,128)S(1)}, f32[18,3,80,128]{3,2,1,0:T(8,128)S(1)}, f32[16,64,128]{2,1,0:T(8,128)S(1)}...) custom-call(f32[2,8]{1,0:T(2,128)S(1)} %copy-done, ...), custom_call_target="tpu_custom_call", output_to_operand_aliasing={{0}: (12, {}), {1}: (9, {}), {2}: (10, {}), {3}: (11, {})} | custom-call | tf_op jit(solution)/shard_map/outer/pallas_call | solution.py:470
  34.4 3.8 %collective-permute-start.8 = (f32[6,128]{1,0:T(8,128)S(1)}, f32[6,128]{1,0:T(8,128)S(1)}, u32[]{:S(2)}, u32[]{:S(2)}) collective-permute-start(f32[6,128]{1,0:T(8,128)S(1)} %get-tuple-element.32), channel_id=1, source_target_pairs={{0,1},{1,0},{2,3},{3,2},{4,5},{5,4},{6,7},{7,6},{8,9},{9,8},{10,11... | collective-permute-start | bytes 9224 | tf_op jit(solution)/shard_map/ppermute | solution.py:40
  38.1 1.9 %collective-permute-start.9 = (f32[6,128]{1,0:T(8,128)S(1)}, f32[6,128]{1,0:T(8,128)S(1)}, u32[]{:S(2)}, u32[]{:S(2)}) collective-permute-start(f32[6,128]{1,0:T(8,128)S(1)} %get-tuple-element.33), channel_id=1, source_target_pairs={{0,7},{1,2},{2,1},{3,4},{4,3},{5,6},{6,5},{7,0},{8,15},{9,10},{10,... | collective-permute-start | bytes 9224 | tf_op jit(solution)/shard_map/ppermute | solution.py:40
  40.1 0.0 collective-permute-done.8
  40.1 4.4 %collective-permute-done.9 = f32[6,128]{1,0:T(8,128)S(1)} collective-permute-done((f32[6,128]{1,0:T(8,128)S(1)}, f32[6,128]{1,0:T(8,128)S(1)}, u32[]{:S(2)}, u32[]{:S(2)}) %collective-permute-start.9) | collective-permute-done | bytes 3104 | tf_op jit(solution)/shard_map/ppermute | solution.py:40
  44.5 1.5 %collective-permute-start.10 = (f32[6,128]{1,0:T(8,128)S(1)}, f32[6,128]{1,0:T(8,128)S(1)}, u32[]{:S(2)}, u32[]{:S(2)}) collective-permute-start(f32[6,128]{1,0:T(8,128)S(1)} %pad_maximum_fusion.3), channel_id=1, source_target_pairs={{0,8},{8,0},{16,24},{24,16},{1,9},{9,1},{17,25},{25,17},{2,10},{10... | collective-permute-start | bytes 9224 | tf_op jit(solution)/shard_map/ppermute | solution.py:40
  46.0 2.1 %collective-permute-start.11 = (f32[6,128]{1,0:T(8,128)S(1)}, f32[6,128]{1,0:T(8,128)S(1)}, u32[]{:S(2)}, u32[]{:S(2)}) collective-permute-start(f32[6,128]{1,0:T(8,128)S(1)} %pad_maximum_fusion.4), channel_id=1, source_target_pairs={{0,24},{8,16},{16,8},{24,0},{1,25},{9,17},{17,9},{25,1},{2,26},{10... | collective-permute-start | bytes 9224 | tf_op jit(solution)/shard_map/ppermute | solution.py:40
  48.1 0.0 collective-permute-done.10.first
  48.1 1.3 %collective-permute-done.11.second = f32[6,128]{1,0:T(8,128)S(1)} collective-permute-done((f32[6,128]{1,0:T(8,128)S(1)}, f32[6,128]{1,0:T(8,128)S(1)}, u32[]{:S(2)}, u32[]{:S(2)}) %collective-permute-start.11) | collective-permute-done | bytes 3104 | tf_op jit(solution)/shard_map/ppermute | solution.py:40
  49.4 0.6 %pick.1 = f32[18,128]{1,0:T(8,128)S(1)} custom-call(s32[18]{0:T(128)S(1)} %get-tuple-element.30.place, f32[6,128]{1,0:T(8,128)S(1)} %pad_maximum_fusion.2.own, f32[6,128]{1,0:T(8,128)S(1)} %collective-permute-done.10.first, f32[6,128]{1,0:T(8,128)S(1)} %collective-permute-done.11.second), custom_call_target="tpu_custom_call" | custom-call | tf_op jit(solution)/shard_map/pick/pallas_call | solution.py:503
  50.0 0.6 %convert_bitcast_fusion = bf16[2304]{0:T(1024)(128)(2,1)} fusion(f32[18,128]{1,0:T(8,128)S(1)} %pick.1), kind=kLoop, calls=%fused_computation.2 | loop fusion | flops 2304 | bytes 13824 | tf_op jit(solution)/shard_map/reshape | solution.py:572
  (11 shorter events, 0.1 us)
Async XLA Ops:
  2.2 3.2 %collective-permute-start = (bf16[6,16,128]{2,1,0:T(8,128)(2,1)S(1)}, bf16[6,16,128]{2,1,0:T(8,128)(2,1)S(1)}, u32[]{:S(2)}, u32[]{:S(2)}) collective-permute-start(bf16[6,16,128]{2,1,0:T(8,128)(2,1)S(1)} %get-tuple-element.19), channel_id=1, source_target_pairs={{0,8},{8,0},{16,24},{24,16},{1,9},{9,1},{17,25},{25,17},{2,10},{10... | collective-permute-start | bytes 73736 | tf_op jit(solution)/shard_map/ppermute | solution.py:40
  2.7 4.2 %collective-permute-start.1 = (bf16[6,16,128]{2,1,0:T(8,128)(2,1)S(1)}, bf16[6,16,128]{2,1,0:T(8,128)(2,1)S(1)}, u32[]{:S(2)}, u32[]{:S(2)}) collective-permute-start(bf16[6,16,128]{2,1,0:T(8,128)(2,1)S(1)} %get-tuple-element.20), channel_id=1, source_target_pairs={{0,24},{8,16},{16,8},{24,0},{1,25},{9,17},{17,9},{25,1},{2,26},{10... | collective-permute-start | bytes 73736 | tf_op jit(solution)/shard_map/ppermute | solution.py:40
  6.9 11.2 %collective-permute-start.2 = (bf16[6,16,128]{2,1,0:T(8,128)(2,1)S(1)}, bf16[6,16,128]{2,1,0:T(8,128)(2,1)S(1)}, u32[]{:S(2)}, u32[]{:S(2)}) collective-permute-start(bf16[6,16,128]{2,1,0:T(8,128)(2,1)S(1)} %pad_maximum_fusion), channel_id=1, source_target_pairs={{0,1},{1,0},{2,3},{3,2},{4,5},{5,4},{6,7},{7,6},{8,9},{9,8},{10,11... | collective-permute-start | bytes 73736 | tf_op jit(solution)/shard_map/ppermute | solution.py:40
  8.6 9.5 %collective-permute-start.3 = (bf16[6,16,128]{2,1,0:T(8,128)(2,1)S(1)}, bf16[6,16,128]{2,1,0:T(8,128)(2,1)S(1)}, u32[]{:S(2)}, u32[]{:S(2)}) collective-permute-start(bf16[6,16,128]{2,1,0:T(8,128)(2,1)S(1)} %pad_maximum_fusion.1), channel_id=1, source_target_pairs={{0,7},{1,2},{2,1},{3,4},{4,3},{5,6},{6,5},{7,0},{8,15},{9,10},{10,... | collective-permute-start | bytes 73736 | tf_op jit(solution)/shard_map/ppermute | solution.py:40
  15.1 3.1 %copy-start.1 = (s32[128]{0:T(128)S(1)}, s32[128]{0:T(128)}, u32[]{:S(2)}) copy-start(s32[128]{0:T(128)} %tile_slot.3) | copy-start | bytes 1540
  15.1 3.1 %copy-start.2 = (s32[128]{0:T(128)S(1)}, s32[128]{0:T(128)}, u32[]{:S(2)}) copy-start(s32[128]{0:T(128)} %tile_cell.3) | copy-start | bytes 1540
  18.1 4.1 %copy-start = (f32[2,8]{1,0:T(2,128)S(1)}, f32[2,8]{1,0:T(2,128)}, u32[]{:S(2)}) copy-start(f32[2,8]{1,0:T(2,128)} %props.3) | copy-start | bytes 196
  20.7 7.1 %collective-permute-start.6 = (bf16[384,128]{1,0:T(8,128)(2,1)S(1)}, bf16[384,128]{1,0:T(8,128)(2,1)S(1)}, u32[]{:S(2)}, u32[]{:S(2)}) collective-permute-start(bf16[384,128]{1,0:T(8,128)(2,1)S(1)} %get-tuple-element.23), channel_id=1, source_target_pairs={{0,1},{1,0},{2,3},{3,2},{4,5},{5,4},{6,7},{7,6},{8,9},{9,8},{10,11... | collective-permute-start | bytes 294920 | tf_op jit(solution)/shard_map/ppermute | solution.py:40
  20.8 7.0 %collective-permute-start.7 = (bf16[384,128]{1,0:T(8,128)(2,1)S(1)}, bf16[384,128]{1,0:T(8,128)(2,1)S(1)}, u32[]{:S(2)}, u32[]{:S(2)}) collective-permute-start(bf16[384,128]{1,0:T(8,128)(2,1)S(1)} %get-tuple-element.24), channel_id=1, source_target_pairs={{1,2},{2,1},{3,4},{4,3},{5,6},{6,5},{9,10},{10,9},{11,12},{12,11},... | collective-permute-start | bytes 294920 | tf_op jit(solution)/shard_map/ppermute | solution.py:40
  21.5 6.3 %collective-permute-start.4 = (bf16[192,128]{1,0:T(8,128)(2,1)S(1)}, bf16[192,128]{1,0:T(8,128)(2,1)S(1)}, u32[]{:S(2)}, u32[]{:S(2)}) collective-permute-start(bf16[192,128]{1,0:T(8,128)(2,1)S(1)} %get-tuple-element.21), channel_id=1, source_target_pairs={{0,8},{8,0},{16,24},{24,16},{1,9},{9,1},{17,25},{25,17},{2,10},{10... | collective-permute-start | bytes 147464 | tf_op jit(solution)/shard_map/ppermute | solution.py:40
  21.5 6.2 %collective-permute-start.5 = (bf16[192,128]{1,0:T(8,128)(2,1)S(1)}, bf16[192,128]{1,0:T(8,128)(2,1)S(1)}, u32[]{:S(2)}, u32[]{:S(2)}) collective-permute-start(bf16[192,128]{1,0:T(8,128)(2,1)S(1)} %get-tuple-element.22), channel_id=1, source_target_pairs={{8,16},{16,8},{9,17},{17,9},{10,18},{18,10},{11,19},{19,11},{12,20... | collective-permute-start | bytes 147464 | tf_op jit(solution)/shard_map/ppermute | solution.py:40
  34.4 5.7 %collective-permute-start.8 = (f32[6,128]{1,0:T(8,128)S(1)}, f32[6,128]{1,0:T(8,128)S(1)}, u32[]{:S(2)}, u32[]{:S(2)}) collective-permute-start(f32[6,128]{1,0:T(8,128)S(1)} %get-tuple-element.32), channel_id=1, source_target_pairs={{0,1},{1,0},{2,3},{3,2},{4,5},{5,4},{6,7},{7,6},{8,9},{9,8},{10,11... | collective-permute-start | bytes 9224 | tf_op jit(solution)/shard_map/ppermute | solution.py:40
  38.1 6.3 %collective-permute-start.9 = (f32[6,128]{1,0:T(8,128)S(1)}, f32[6,128]{1,0:T(8,128)S(1)}, u32[]{:S(2)}, u32[]{:S(2)}) collective-permute-start(f32[6,128]{1,0:T(8,128)S(1)} %get-tuple-element.33), channel_id=1, source_target_pairs={{0,7},{1,2},{2,1},{3,4},{4,3},{5,6},{6,5},{7,0},{8,15},{9,10},{10,... | collective-permute-start | bytes 9224 | tf_op jit(solution)/shard_map/ppermute | solution.py:40
  44.5 3.6 %collective-permute-start.10 = (f32[6,128]{1,0:T(8,128)S(1)}, f32[6,128]{1,0:T(8,128)S(1)}, u32[]{:S(2)}, u32[]{:S(2)}) collective-permute-start(f32[6,128]{1,0:T(8,128)S(1)} %pad_maximum_fusion.3), channel_id=1, source_target_pairs={{0,8},{8,0},{16,24},{24,16},{1,9},{9,1},{17,25},{25,17},{2,10},{10... | collective-permute-start | bytes 9224 | tf_op jit(solution)/shard_map/ppermute | solution.py:40
  46.0 3.4 %collective-permute-start.11 = (f32[6,128]{1,0:T(8,128)S(1)}, f32[6,128]{1,0:T(8,128)S(1)}, u32[]{:S(2)}, u32[]{:S(2)}) collective-permute-start(f32[6,128]{1,0:T(8,128)S(1)} %pad_maximum_fusion.4), channel_id=1, source_target_pairs={{0,24},{8,16},{16,8},{24,0},{1,25},{9,17},{17,9},{25,1},{2,26},{10... | collective-permute-start | bytes 9224 | tf_op jit(solution)/shard_map/ppermute | solution.py:40

commit v3 on v2

--- a/solution.py
+++ b/solution.py
@@ -14,7 +14,10 @@
 HALF = BLK // 2
 PAD = 8
 ROWS = 16
-UNROLL = 32
+UNROLL = 128
+PAIR = 2
+GROUP = 8
+DELAY = 4
 MIB = 2**20
 
 time_step = 0.8
@@ -27,7 +30,7 @@
 
 
 def partner(index, size, which):
-    if which == 1:
+    if which == 2:
         return index ^ 1
     return (index + 1 if index % 2 else index - 1) % size
 
@@ -41,7 +44,7 @@
 
 
 def code_of(index, mine):
-    return jnp.where(index == mine, 0, jnp.where(index == (mine ^ 1), 1, 2))
+    return jnp.where(index == mine, 0, jnp.where(index == (mine ^ 1), 2, 1))
 
 
 def split_device(device, size):
@@ -181,7 +184,7 @@
 
 
 def deposit_kernel(
-    tile_slot, tile_cell, tile_count, own, first, second, north, south, weight, state_in,
+    tile_slot, tile_cell, tile_count, own, first, second, south, north, weight, state_in,
     state, edge_x1, edge_x2, edge_y1, edge_y2, rows, *, size_y
 ):
     pos_x, pos_y = lax.axis_index("gx"), lax.axis_index("gy")
@@ -191,7 +194,7 @@
     for k, part in enumerate((own, first, second)):
         for r in range(CAP):
             rows[k * CAP + r] = part[r]
-    for k, part in enumerate((north, south)):
+    for k, part in enumerate((south, north)):
         for r in range(3 * CAP):
             rows[(k + 1) * 3 * CAP + r] = part[r]
     counted = tile_count[0]
@@ -213,15 +216,15 @@
     top, bottom = tall - PAD - 1, PAD
     line = state.reshape((columns + 2) * count * tall, BLK)
     for edge, row in (
-        (edge_x1, jnp.where(even_x, top, bottom)),
-        (edge_x2, jnp.where(even_x, bottom, top)),
+        (edge_x1, jnp.where(even_x, bottom, top)),
+        (edge_x2, jnp.where(even_x, top, bottom)),
     ):
         for q in range(count):
             at = pl.ds(count * tall + q * tall + row, columns, stride=count * tall)
             edge[q * columns : (q + 1) * columns, :] = line[at, :].astype(BF16)
     low = low_lanes()
     width = tall - 2 * PAD
-    for edge, upper in ((edge_y1, even_y), (edge_y2, jnp.logical_not(even_y))):
+    for edge, upper in ((edge_y1, jnp.logical_not(even_y)), (edge_y2, even_y)):
         column = jnp.where(upper, columns, 1)
         for q in range(count // 2):
             for i in range(width // ROWS):
@@ -248,11 +251,14 @@
     )(tile_slot, tile_cell, tile_count, *parts, weight, state)
 
 
-def speeds_at(props, state, j, here, parts):
-    terms = [props[0, m] * state[j, m, here, :] for m in range(MAT)]
+def total(terms):
     while len(terms) > 1:
         terms = [a + b for a, b in zip(terms[::2], terms[1::2], strict=True)]
-    share = 1.0 / (1.0 + terms[0])
+    return terms[0]
+
+
+def speeds_at(props, state, j, here, parts):
+    share = 1.0 / (1.0 + total([props[0, m] * state[j, m, here, :] for m in range(MAT)]))
     found = []
     if 0 in parts:
         found.append((0, state[j, MAT, here, :] * share))
@@ -262,12 +268,16 @@
     return found
 
 
-def store_speeds(props, state, speed, j, first_rows, parts):
-    rows = [slice(first, first + 8) for first in first_rows]
-    found = [speeds_at(props, state, j, here, parts) for here in rows]
-    for here, planes in zip(rows, found, strict=True):
-        for plane, value in planes:
-            speed[j, plane, here, :] = value
+def store_speeds(props, state, speed, places, parts):
+    waiting = []
+    for step in range(len(places) + DELAY):
+        if step < len(places):
+            j, first_row = places[step]
+            waiting.append(speeds_at(props, state, j, slice(first_row, first_row + 8), parts))
+        if step >= DELAY:
+            j, first_row = places[step - DELAY]
+            for plane, value in waiting.pop(0):
+                speed[j, plane, first_row : first_row + 8, :] = value
 
 
 def weights_at(speed, j, first_row):
@@ -291,72 +301,69 @@
     return keep, jnp.maximum(lower, 0.0), jnp.maximum(-upper, 0.0), same, other
 
 
-def remap_at(props, state, weights, j, first_row):
-    count = state.shape[1]
+def values_at(state, weights, j, first_row):
     low = low_lanes()
     here = slice(first_row, first_row + 8)
     before = slice(first_row - 1, first_row + 7)
     after = slice(first_row + 1, first_row + 9)
     keep, take_before, take_after, same, other = weights
     values = []
-    total = None
-    for q in range(count):
+    for q in range(state.shape[1]):
         mid = state[j, q, here, :]
         beside = jnp.where(low, state[j + 1, q, here, :], state[j - 1, q, here, :])
         value = (keep * mid + take_before * state[j, q, before, :]) + take_after * state[j, q, after, :]
-        value = value + turn(same * mid + other * beside)
-        values.append(value)
-        if q < MAT:
-            term = value * (props[1, q] + (0.5 * props[1, q]) * value)
-            total = term if total is None else total + term
-        elif q == count - 1:
-            total = total + 0.4 * value
-    return values, total
-
-
-def remap_tiles(props, state, speed, press, fresh, j, first_rows):
-    def store(first_row, values, total):
-        inside = slice(first_row - PAD, first_row - PAD + 8)
-        for q, value in enumerate(values):
-            fresh[j - 1, q, inside, :] = value
-        press[j - 1, inside, :] = total
-
-    waiting = None
-    for first_row in first_rows:
-        found = (first_row, *remap_at(props, state, weights_at(speed, j, first_row), j, first_row))
-        if waiting is not None:
-            store(*waiting)
-        waiting = found
-    store(*waiting)
-
-
-def inner_kernel(props, state, remapped, press, speed, fresh, sem):
+        values.append(value + turn(same * mid + other * beside))
+    return values
+
+
+def pressure_of(props, values):
+    terms = [value * (props[1, m] + (0.5 * props[1, m]) * value) for m, value in enumerate(values[:MAT])]
+    return total(terms) + 0.4 * values[-1]
+
+
+def remap_tiles(props, state, speed, press, fresh, places):
+    weights, values = {}, {}
+    for step in range(len(places) + 2):
+        if step < len(places):
+            weights[step] = weights_at(speed, *places[step])
+        k = step - 1
+        if 0 <= k < len(places):
+            values[k] = values_at(state, weights.pop(k), *places[k])
+        k = step - 2
+        if k >= 0:
+            found = values.pop(k)
+            j, first_row = places[k]
+            inside = slice(first_row - PAD, first_row - PAD + 8)
+            lanes = column_lanes(j)
+            for q, value in enumerate(found):
+                fresh[q, inside, lanes] = value
+            press[j - 1, inside, :] = pressure_of(props, found)
+
+
+def column_lanes(j):
+    if isinstance(j, int):
+        return slice((j - 1) * BLK, j * BLK)
+    return pl.ds(pl.multiple_of((j - 1) * BLK, BLK), BLK)
+
+
+def inner_kernel(props, state, fresh, press, speed):
     columns, tall = state.shape[0] - 2, state.shape[2]
-    tiles = (tall - 2 * PAD) // 8
-
-    def speeds(j, carry):
-        store_speeds(props, state, speed, j, range(PAD, tall - PAD, 8), (0, 1))
+
+    def speeds(step, carry):
+        rows = range(PAD, tall - PAD, 8)
+        places = [(1 + step * GROUP + k, row) for k in range(GROUP) for row in rows]
+        store_speeds(props, state, speed, places, (0, 1))
         return carry
 
-    lax.fori_loop(1, columns + 1, speeds, 0)
-
-    def write(j):
-        rows = pl.ds(8, 8 * (tiles - 2))
-        lanes = pl.ds(pl.multiple_of((j - 1) * BLK, BLK), BLK)
-        return pltpu.make_async_copy(fresh.at[j - 1, :, rows], remapped.at[:, rows, lanes], sem.at[j - 1])
-
-    def remap(j, carry):
-        remap_tiles(props, state, speed, press, fresh, j, range(PAD + 8, tall - PAD - 8, 8))
-        write(j).start()
+    lax.fori_loop(0, columns // GROUP, speeds, 0)
+
+    def remap(step, carry):
+        rows = range(PAD + 8, tall - PAD - 8, 8)
+        places = [(2 + step * PAIR + k, row) for k in range(PAIR) for row in rows]
+        remap_tiles(props, state, speed, press, fresh, places)
         return carry
 
-    lax.fori_loop(2, columns, remap, 0)
-
-    def finish(j, carry):
-        write(j).wait()
-        return carry
-
-    lax.fori_loop(2, columns, finish, 0)
+    lax.fori_loop(0, (columns - 2) // PAIR, remap, 0)
 
 
 def inner(props, state, width):
@@ -365,41 +372,52 @@
         inner_kernel,
         name="inner",
         out_shape=(
-            jax.ShapeDtypeStruct((count, width, columns * BLK), F32),
+            pltpu.VMEM((count, width, columns * BLK), F32),
             pltpu.VMEM((columns, width, BLK), F32),
             pltpu.VMEM((columns + 2, 3, tall, BLK), F32),
         ),
         in_specs=[SMEM, VMEM],
-        out_specs=(ANY, VMEM, VMEM),
-        scratch_shapes=[pltpu.VMEM((columns, count, width, BLK), F32), pltpu.SemaphoreType.DMA((columns,))],
-        compiler_params=pltpu.CompilerParams(vmem_limit_bytes=10 * MIB),
+        out_specs=(VMEM, VMEM, VMEM),
+        compiler_params=pltpu.CompilerParams(vmem_limit_bytes=4 * MIB),
         cost_estimate=pl.CostEstimate(flops=20 * state.size, bytes_accessed=2 * state.size * 4, transcendentals=0),
     )(props, state)
 
 
 def outer_kernel(
     props, tile_slot, tile_cell, tile_count, edge_x1, edge_x2, edge_y1, edge_y2, weight, state_in, speed_in, press_in,
-    remapped_in, remapped, state, speed, press, own, first, second, fresh, sums, sem, *, size_y
+    fresh_in, remapped, state, speed, press, fresh, own, first, second, sums, sem, *, size_y
 ):
     pos_x, pos_y = lax.axis_index("gx"), lax.axis_index("gy")
     n_tiles = weight.shape[0]
     columns, count, tall = state.shape[0] - 2, state.shape[1], state.shape[2]
     width = tall - 2 * PAD
-    tiles = width // 8
+    middle = pl.ds(8, width - 16)
+    areas = (
+        (middle, pl.ds(BLK, (columns - 2) * BLK)),
+        (pl.ds(0, 8), pl.ds(0, columns * BLK)),
+        (pl.ds(width - 8, 8), pl.ds(0, columns * BLK)),
+        (middle, pl.ds(0, BLK)),
+        (middle, pl.ds((columns - 1) * BLK, BLK)),
+    )
+    copies = [
+        pltpu.make_async_copy(fresh.at[:, rows, lanes], remapped.at[:, rows, lanes], sem.at[k])
+        for k, (rows, lanes) in enumerate(areas)
+    ]
+    copies[0].start()
     even_x, even_y = (pos_x & 1) == 0, (pos_y & 1) == 0
     line = state.reshape((columns + 2) * count * tall, BLK)
     above, below = tall - PAD, PAD - 1
     for edge, row in (
-        (edge_x1, jnp.where(even_x, above, below)),
-        (edge_x2, jnp.where(even_x, below, above)),
+        (edge_x1, jnp.where(even_x, below, above)),
+        (edge_x2, jnp.where(even_x, above, below)),
     ):
         for q in range(count):
             at = pl.ds(count * tall + q * tall + row, columns, stride=count * tall)
             line[at, :] = edge[q * columns : (q + 1) * columns, :].astype(F32)
     low = low_lanes()
     for edge, column in (
-        (edge_y1, jnp.where(even_y, columns + 1, 0)),
-        (edge_y2, jnp.where(even_y, 0, columns + 1)),
+        (edge_y1, jnp.where(even_y, 0, columns + 1)),
+        (edge_y2, jnp.where(even_y, columns + 1, 0)),
     ):
         for q in range(count // 2):
             for i in range(width // ROWS):
@@ -409,29 +427,23 @@
                 state[column, q, here, :] = jnp.where(low, both, turned)
                 state[column, q + count // 2, here, :] = jnp.where(low, turned, both)
 
-    def side_speeds(j, carry):
-        store_speeds(props, state, speed, j, (0, tall - PAD), (0,))
+    places = [(j, row) for j in range(1, columns + 1) for row in (0, tall - PAD)]
+    store_speeds(props, state, speed, places, (0,))
+    places = [(j, row) for j in (0, columns + 1) for row in range(PAD, tall - PAD, 8)]
+    store_speeds(props, state, speed, places, (1,))
+
+    def sides(step, carry):
+        places = [(1 + step * 2 * PAIR + k, row) for k in range(2 * PAIR) for row in (PAD, tall - PAD - 8)]
+        remap_tiles(props, state, speed, press, fresh, places)
         return carry
 
-    lax.fori_loop(1, columns + 1, side_speeds, 0)
-    for j in (0, columns + 1):
-        store_speeds(props, state, speed, j, range(PAD, tall - PAD, 8), (1,))
-
-    def write(j, first_row, rows, which):
-        rows = pl.ds(first_row, rows)
-        lanes = pl.ds(pl.multiple_of((j - 1) * BLK, BLK), BLK)
-        return pltpu.make_async_copy(fresh.at[j - 1, :, rows], remapped.at[:, rows, lanes], sem.at[which, j - 1])
-
-    def sides(j, carry):
-        remap_tiles(props, state, speed, press, fresh, j, (PAD, tall - PAD - 8))
-        for which, i in enumerate((0, tiles - 1)):
-            write(j, 8 * i, 8, which).start()
-        return carry
-
-    lax.fori_loop(1, columns + 1, sides, 0)
-    for j in (1, columns):
-        remap_tiles(props, state, speed, press, fresh, j, range(PAD + 8, tall - PAD - 8, 8))
-        write(j, 8, 8 * (tiles - 2), 2).start()
+    lax.fori_loop(0, columns // (2 * PAIR), sides, 0)
+    copies[1].start()
+    copies[2].start()
+    places = [(j, row) for j in (1, columns) for row in range(PAD + 8, tall - PAD - 8, 8)]
+    remap_tiles(props, state, speed, press, fresh, places)
+    copies[3].start()
+    copies[4].start()
 
     sums[...] = jnp.zeros(sums.shape, F32)
     counted = tile_count[0]
@@ -454,42 +466,32 @@
         under = table[pl.ds(k * 3 * CAP * 8 + 1, 3 * CAP, stride=8), :]
         out[...] = top / jnp.maximum(under, 1.0)
 
-    def finish(j, carry):
-        write(j, 0, 8, 0).wait()
-        write(j, 8 * (tiles - 1), 8, 1).wait()
-        return carry
-
-    lax.fori_loop(1, columns + 1, finish, 0)
-    for j in (1, columns):
-        write(j, 8, 8 * (tiles - 2), 2).wait()
-
-
-def outer(props, tile_slot, tile_cell, tile_count, edges, weight, state, speed, press, remapped, size_y):
-    columns, count = state.shape[0] - 2, state.shape[1]
+    for copy in copies:
+        copy.wait()
+
+
+def outer(props, tile_slot, tile_cell, tile_count, edges, weight, state, speed, press, fresh, size_y):
     answer = pltpu.VMEM((3 * CAP, BLK), F32)
     outs = pl.pallas_call(
         functools.partial(outer_kernel, size_y=size_y),
         name="outer",
         out_shape=(
-            jax.ShapeDtypeStruct(remapped.shape, F32),
+            jax.ShapeDtypeStruct(fresh.shape, F32),
             pltpu.VMEM(state.shape, F32),
             pltpu.VMEM(speed.shape, F32),
             pltpu.VMEM(press.shape, F32),
+            pltpu.VMEM(fresh.shape, F32),
             answer,
             answer,
             answer,
         ),
-        in_specs=[SMEM] * 4 + [VMEM] * 8 + [ANY],
-        out_specs=(ANY,) + (VMEM,) * 6,
-        input_output_aliases={12: 0, 9: 1, 10: 2, 11: 3},
-        scratch_shapes=[
-            pltpu.VMEM((columns, count, remapped.shape[1], BLK), F32),
-            pltpu.VMEM((9 * CAP, 8, BLK), F32),
-            pltpu.SemaphoreType.DMA((3, columns)),
-        ],
-        compiler_params=pltpu.CompilerParams(vmem_limit_bytes=10 * MIB),
-    )(props, tile_slot, tile_cell, tile_count, *edges, weight, state, speed, press, remapped)
-    return outs[0], outs[4], outs[5], outs[6]
+        in_specs=[SMEM] * 4 + [VMEM] * 9,
+        out_specs=(ANY,) + (VMEM,) * 7,
+        input_output_aliases={9: 1, 10: 2, 11: 3, 12: 4},
+        scratch_shapes=[pltpu.VMEM((9 * CAP, 8, BLK), F32), pltpu.SemaphoreType.DMA((5,))],
+        compiler_params=pltpu.CompilerParams(vmem_limit_bytes=4 * MIB),
+    )(props, tile_slot, tile_cell, tile_count, *edges, weight, state, speed, press, fresh)
+    return outs[0], outs[5], outs[6], outs[7]
 
 
 def pick_kernel(place, own, first, second, out, table):
@@ -539,17 +541,18 @@
     state = stage(cell_state)
     weight = fetch(tile_weight)
 
+    first = swap(first, "gx", 1)
     second = swap(second, "gx", 2)
-    first = swap(first, "gx", 1)
+    weight, own = lax.optimization_barrier((weight, own))
 
     def along_y(which):
         rows = slice(which * CAP, (which + 1) * CAP)
         return jnp.concatenate([own[rows], first[rows], second[rows]], axis=0)
 
-    south = swap(along_y(2), "gy", 2)
-    north = swap(along_y(1), "gy", 1)
+    south = swap(along_y(1), "gy", 1)
+    north = swap(along_y(2), "gy", 2)
     state, *edges = deposit(
-        tile_slot, tile_cell, tile_count, (own, first, second, north, south), weight, state, size_y
+        tile_slot, tile_cell, tile_count, (own, first, second, south, north), weight, state, size_y
     )
     edges = (
         swap(edges[0], "gx", 1, wrap=False),
@@ -557,12 +560,12 @@
         swap(edges[2], "gy", 1, wrap=False),
         swap(edges[3], "gy", 2, wrap=False),
     )
-    remapped, press, speed = inner(mat_props, state, cell_state.shape[1])
+    fresh, press, speed = inner(mat_props, state, cell_state.shape[1])
     remapped, own, first, second = outer(
-        mat_props, tile_slot, tile_cell, tile_count, edges, weight, state, speed, press, remapped, size_y
-    )
+        mat_props, tile_slot, tile_cell, tile_count, edges, weight, state, speed, press, fresh, size_y
+    )
+    first = swap(first, "gy", 1)
     second = swap(second, "gy", 2)
-    first = swap(first, "gy", 1)
 
     def along_x(which):
         rows = slice(which * CAP, (which + 1) * CAP)

time: 50.8 us -> 44.6 us (0.88)
  Pallas kernels: 22 us -> 17.7 us
  starting transfers between devices: 19.2 us -> 18.1 us
  waiting for transfers between devices: 7.21 us -> 6.37 us
    pallas_call x1, Pallas kernels: 5.51 us -> 3.45 us  [inner(): pl.pallas_call(inner_kernel, name='inner', out_shape=(pltpu.VMEM((count,...]
    pallas_call x1, Pallas kernels: 6.56 us -> 4.8 us  [outer(): pl.pallas_call(functools.partial(outer_kernel, size_y=size_y), name='oute...]
    ppermute x12, starting transfers between devices: 19.2 us -> 18.1 us  [swap(): return lax.ppermute(value, axis, pairs)]
    ppermute x12, waiting for transfers between devices: 7.21 us -> 6.37 us  [swap(): return lax.ppermute(value, axis, pairs)]
  transfers between devices with their start and end apart: 12 -> 12, of which waited for: 3 -> 3; matrix products, arithmetic and copies ran while one was open for 0% -> 0% of each run, Pallas kernels for 21% -> 20%
where the time goes in v3:
time: 44.6 us; the launch traced here: 44.4 us
  starting transfers between devices  18.1 us (41%)
  Pallas kernels  17.7 us (40%)
  waiting for transfers between devices  6.37 us (14%)
  between operations  1.51 us (3%)
  other arithmetic  0.64 us (1%)
    ppermute x12, starting transfers between devices, swap(): return lax.ppermute(value, axis, pairs)  18.1 us
    ppermute x12, waiting for transfers between devices, swap(): return lax.ppermute(value, axis, pairs)  6.37 us
    pallas_call x1, Pallas kernels, outer(): pl.pallas_call(functools.partial(outer_kernel, size_y=size_y), name='oute...  4.8 us
    pallas_call x1, Pallas kernels, inner(): pl.pallas_call(inner_kernel, name='inner', out_shape=(pltpu.VMEM((count,...  3.45 us
    pallas_call x1, Pallas kernels, stage(): pl.pallas_call(stage_kernel, name='stage', out_shape=pltpu.VMEM((columns...  3.03 us
    pallas_call x1, Pallas kernels, fetch(): pl.pallas_call(fetch_kernel, name='fetch', out_shape=pltpu.VMEM(value.sha...  2.2 us
    pallas_call x1, Pallas kernels, deposit(): pl.pallas_call(functools.partial(deposit_kernel, size_y=size_y), name='de...  2.13 us
    pallas_call x1, Pallas kernels, payload(): pl.pallas_call(functools.partial(payload_kernel, size_y=size_y), name='pa...  1.57 us
  transfers between devices with their start and end apart: 12, of which 3 were waited for; matrix products, arithmetic and copies ran while one was open for 0% of the time, Pallas kernels for 20%

profile of v3, /device:TPU:0, one launch (start us, length us, event | category | flops | bytes accessed | tf_op | source)
XLA Modules:
  0.0 44.4 jit_solution(7817147834413788635)
XLA Ops:
  0.6 1.6 %payload.1 = (bf16[6,16,128]{2,1,0:T(8,128)(2,1)S(1)}, bf16[6,16,128]{2,1,0:T(8,128)(2,1)S(1)}, bf16[6,16,128]{2,1,0:T(8,128)(2,1)S(1)}, s32[18]{0:T(128)S(1)}) custom-call(s32[18]{0:T(128)} %dest_hbm.1, f32[2,8]{1,0:T(2,128)} %props.3, f32[18,128]{1,0:T(8,128)} %bitcast.5, f32[3,2304]{1,0:T(4,128)} %velocity_hbm.1, f32[18,128]{1,0:T(8,128)} %bitcast.6, ...), custom_call_target="tpu_custom_call" | custom-call | tf_op jit(solution)/shard_map/payload/pallas_call | solution.py:103
  2.2 2.5 %collective-permute-start = (bf16[6,16,128]{2,1,0:T(8,128)(2,1)S(1)}, bf16[6,16,128]{2,1,0:T(8,128)(2,1)S(1)}, u32[]{:S(2)}, u32[]{:S(2)}) collective-permute-start(bf16[6,16,128]{2,1,0:T(8,128)(2,1)S(1)} %get-tuple-element.22), channel_id=1, source_target_pairs={{0,24},{8,16},{16,8},{24,0},{1,25},{9,17},{17,9},{25,1},{2,26},{10... | collective-permute-start | bytes 73736 | tf_op jit(solution)/shard_map/ppermute | solution.py:43
  4.7 0.7 %collective-permute-start.1 = (bf16[6,16,128]{2,1,0:T(8,128)(2,1)S(1)}, bf16[6,16,128]{2,1,0:T(8,128)(2,1)S(1)}, u32[]{:S(2)}, u32[]{:S(2)}) collective-permute-start(bf16[6,16,128]{2,1,0:T(8,128)(2,1)S(1)} %get-tuple-element.23), channel_id=1, source_target_pairs={{0,8},{8,0},{16,24},{24,16},{1,9},{9,1},{17,25},{25,17},{2,10},{10... | collective-permute-start | bytes 73736 | tf_op jit(solution)/shard_map/ppermute | solution.py:43
  5.4 2.2 %fetch.1.weight = bf16[128,128,128]{2,1,0:T(8,128)(2,1)S(1)} custom-call(bf16[128,128,128]{2,1,0:T(8,128)(2,1)} %source.1), custom_call_target="tpu_custom_call" | custom-call | bytes 8388608 | tf_op jit(solution)/shard_map/fetch/pallas_call | solution.py:161
  7.6 0.0 collective-permute-done.first
  7.6 0.0 collective-permute-done.1.second
  7.6 4.6 %collective-permute-start.2 = (bf16[6,16,128]{2,1,0:T(8,128)(2,1)S(1)}, bf16[6,16,128]{2,1,0:T(8,128)(2,1)S(1)}, u32[]{:S(2)}, u32[]{:S(2)}) collective-permute-start(bf16[6,16,128]{2,1,0:T(8,128)(2,1)S(1)} %pad_maximum_fusion), channel_id=1, source_target_pairs={{0,7},{1,2},{2,1},{3,4},{4,3},{5,6},{6,5},{7,0},{8,15},{9,10},{10,... | collective-permute-start | bytes 73736 | tf_op jit(solution)/shard_map/ppermute | solution.py:43
  12.2 0.0 collective-permute-start.3
  12.9 0.0 copy-start.1
  12.9 0.0 copy-start.2
  12.9 3.0 %stage.1.state_in = f32[18,12,80,128]{3,2,1,0:T(8,128)S(1)} custom-call(f32[12,64,2048]{2,1,0:T(8,128)} %cell.1), custom_call_target="tpu_custom_call" | custom-call | bytes 12582912 | tf_op jit(solution)/shard_map/stage/pallas_call | solution.py:142
  16.0 0.0 copy-start
  16.0 0.0 collective-permute-done.2.south
  16.0 0.1 collective-permute-done.3.north
  16.1 0.0 copy-done.1
  16.1 0.0 copy-done.2
  16.1 2.1 %deposit.1 = (f32[18,12,80,128]{3,2,1,0:T(8,128)S(1)}, bf16[192,128]{1,0:T(8,128)(2,1)S(1)}, bf16[192,128]{1,0:T(8,128)(2,1)S(1)}, bf16[384,128]{1,0:T(8,128)(2,1)S(1)}, bf16[384,128]{1,0:T(8,128)(2,1)S(1)}) custom-call(s32[128]{0:T(128)S(1)} %copy-done.1, s32[128]{0:T(128)S(1)} %copy-done.2, ...), custom_call_target="tpu_custom_call", output_to_operand_aliasing={{0}: (9, {})} | custom-call | tf_op jit(solution)/shard_map/deposit/pallas_call | solution.py:242
  18.2 0.7 %collective-permute-start.6 = (bf16[384,128]{1,0:T(8,128)(2,1)S(1)}, bf16[384,128]{1,0:T(8,128)(2,1)S(1)}, u32[]{:S(2)}, u32[]{:S(2)}) collective-permute-start(bf16[384,128]{1,0:T(8,128)(2,1)S(1)} %get-tuple-element.27), channel_id=1, source_target_pairs={{1,2},{2,1},{3,4},{4,3},{5,6},{6,5},{9,10},{10,9},{11,12},{12,11},... | collective-permute-start | bytes 294920 | tf_op jit(solution)/shard_map/ppermute | solution.py:43
  18.9 3.3 %collective-permute-start.7 = (bf16[384,128]{1,0:T(8,128)(2,1)S(1)}, bf16[384,128]{1,0:T(8,128)(2,1)S(1)}, u32[]{:S(2)}, u32[]{:S(2)}) collective-permute-start(bf16[384,128]{1,0:T(8,128)(2,1)S(1)} %get-tuple-element.28), channel_id=1, source_target_pairs={{0,1},{1,0},{2,3},{3,2},{4,5},{5,4},{6,7},{7,6},{8,9},{9,8},{10,11... | collective-permute-start | bytes 294920 | tf_op jit(solution)/shard_map/ppermute | solution.py:43
  22.2 0.7 %collective-permute-start.4 = (bf16[192,128]{1,0:T(8,128)(2,1)S(1)}, bf16[192,128]{1,0:T(8,128)(2,1)S(1)}, u32[]{:S(2)}, u32[]{:S(2)}) collective-permute-start(bf16[192,128]{1,0:T(8,128)(2,1)S(1)} %get-tuple-element.25), channel_id=1, source_target_pairs={{8,16},{16,8},{9,17},{17,9},{10,18},{18,10},{11,19},{19,11},{12,20... | collective-permute-start | bytes 147464 | tf_op jit(solution)/shard_map/ppermute | solution.py:43
  22.8 2.6 %collective-permute-start.5 = (bf16[192,128]{1,0:T(8,128)(2,1)S(1)}, bf16[192,128]{1,0:T(8,128)(2,1)S(1)}, u32[]{:S(2)}, u32[]{:S(2)}) collective-permute-start(bf16[192,128]{1,0:T(8,128)(2,1)S(1)} %get-tuple-element.26), channel_id=1, source_target_pairs={{0,8},{8,0},{16,24},{24,16},{1,9},{9,1},{17,25},{25,17},{2,10},{10... | collective-permute-start | bytes 147464 | tf_op jit(solution)/shard_map/ppermute | solution.py:43
  25.4 0.0 copy-done
  25.4 3.4 %inner.1 = (f32[12,64,2048]{2,1,0:T(8,128)S(1)}, f32[16,64,128]{2,1,0:T(8,128)S(1)}, f32[18,3,80,128]{3,2,1,0:T(8,128)S(1)}) custom-call(f32[2,8]{1,0:T(2,128)S(1)} %copy-done, f32[18,12,80,128]{3,2,1,0:T(8,128)S(1)} %get-tuple-element.29.state.state_in), custom_call_target="tpu_custom_call" | custom-call | flops 44236800 | bytes 17694720 | tf_op jit(solution)/shard_map/inner/pallas_call | solution.py:371
  28.8 0.0 collective-permute-done.4.edge_x1
  28.9 0.0 collective-permute-done.5.edge_x2
  28.9 0.0 collective-permute-done.6.edge_y1
  28.9 0.0 collective-permute-done.7.edge_y2
  28.9 4.8 %outer.1 = (f32[12,64,2048]{2,1,0:T(8,128)}, f32[18,12,80,128]{3,2,1,0:T(8,128)S(1)}, f32[18,3,80,128]{3,2,1,0:T(8,128)S(1)}, f32[16,64,128]{2,1,0:T(8,128)S(1)}...) custom-call(f32[2,8]{1,0:T(2,128)S(1)} %copy-done, ...), custom_call_target="tpu_custom_call", output_to_operand_aliasing={{1}: (9, {}), {2}: (10, {}), {3}: (11, {}), {4}: (12, {})} | custom-call | tf_op jit(solution)/shard_map/outer/pallas_call | solution.py:475
  33.7 1.9 %collective-permute-start.8 = (f32[6,128]{1,0:T(8,128)S(1)}, f32[6,128]{1,0:T(8,128)S(1)}, u32[]{:S(2)}, u32[]{:S(2)}) collective-permute-start(f32[6,128]{1,0:T(8,128)S(1)} %get-tuple-element.36), channel_id=1, source_target_pairs={{0,7},{1,2},{2,1},{3,4},{4,3},{5,6},{6,5},{7,0},{8,15},{9,10},{10,... | collective-permute-start | bytes 9224 | tf_op jit(solution)/shard_map/ppermute | solution.py:43
  35.6 1.2 %collective-permute-start.9 = (f32[6,128]{1,0:T(8,128)S(1)}, f32[6,128]{1,0:T(8,128)S(1)}, u32[]{:S(2)}, u32[]{:S(2)}) collective-permute-start(f32[6,128]{1,0:T(8,128)S(1)} %get-tuple-element.37), channel_id=1, source_target_pairs={{0,1},{1,0},{2,3},{3,2},{4,5},{5,4},{6,7},{7,6},{8,9},{9,8},{10,11... | collective-permute-start | bytes 9224 | tf_op jit(solution)/shard_map/ppermute | solution.py:43
  36.7 3.4 %collective-permute-done.8 = f32[6,128]{1,0:T(8,128)S(1)} collective-permute-done((f32[6,128]{1,0:T(8,128)S(1)}, f32[6,128]{1,0:T(8,128)S(1)}, u32[]{:S(2)}, u32[]{:S(2)}) %collective-permute-start.8) | collective-permute-done | bytes 3104 | tf_op jit(solution)/shard_map/ppermute | solution.py:43
  40.1 0.0 collective-permute-done.9
  40.1 0.1 collective-permute-start.10
  40.2 0.1 collective-permute-start.11
  40.3 2.9 %collective-permute-done.10.first = f32[6,128]{1,0:T(8,128)S(1)} collective-permute-done((f32[6,128]{1,0:T(8,128)S(1)}, f32[6,128]{1,0:T(8,128)S(1)}, u32[]{:S(2)}, u32[]{:S(2)}) %collective-permute-start.10) | collective-permute-done | bytes 3104 | tf_op jit(solution)/shard_map/ppermute | solution.py:43
  43.2 0.0 collective-permute-done.11.second
  43.2 0.6 %pick.1 = f32[18,128]{1,0:T(8,128)S(1)} custom-call(s32[18]{0:T(128)S(1)} %get-tuple-element.34.place, f32[6,128]{1,0:T(8,128)S(1)} %pad_maximum_fusion.2.own, f32[6,128]{1,0:T(8,128)S(1)} %collective-permute-done.10.first, f32[6,128]{1,0:T(8,128)S(1)} %collective-permute-done.11.second), custom_call_target="tpu_custom_call" | custom-call | tf_op jit(solution)/shard_map/pick/pallas_call | solution.py:505
  43.8 0.6 %convert_bitcast_fusion = bf16[2304]{0:T(1024)(128)(2,1)} fusion(f32[18,128]{1,0:T(8,128)S(1)} %pick.1), kind=kLoop, calls=%fused_computation.2 | loop fusion | flops 2304 | bytes 13824 | tf_op jit(solution)/shard_map/reshape | solution.py:575
  (11 shorter events, 0.1 us)
Async XLA Ops:
  2.2 5.4 %collective-permute-start = (bf16[6,16,128]{2,1,0:T(8,128)(2,1)S(1)}, bf16[6,16,128]{2,1,0:T(8,128)(2,1)S(1)}, u32[]{:S(2)}, u32[]{:S(2)}) collective-permute-start(bf16[6,16,128]{2,1,0:T(8,128)(2,1)S(1)} %get-tuple-element.22), channel_id=1, source_target_pairs={{0,24},{8,16},{16,8},{24,0},{1,25},{9,17},{17,9},{25,1},{2,26},{10... | collective-permute-start | bytes 73736 | tf_op jit(solution)/shard_map/ppermute | solution.py:43
  4.7 2.9 %collective-permute-start.1 = (bf16[6,16,128]{2,1,0:T(8,128)(2,1)S(1)}, bf16[6,16,128]{2,1,0:T(8,128)(2,1)S(1)}, u32[]{:S(2)}, u32[]{:S(2)}) collective-permute-start(bf16[6,16,128]{2,1,0:T(8,128)(2,1)S(1)} %get-tuple-element.23), channel_id=1, source_target_pairs={{0,8},{8,0},{16,24},{24,16},{1,9},{9,1},{17,25},{25,17},{2,10},{10... | collective-permute-start | bytes 73736 | tf_op jit(solution)/shard_map/ppermute | solution.py:43
  7.6 8.3 %collective-permute-start.2 = (bf16[6,16,128]{2,1,0:T(8,128)(2,1)S(1)}, bf16[6,16,128]{2,1,0:T(8,128)(2,1)S(1)}, u32[]{:S(2)}, u32[]{:S(2)}) collective-permute-start(bf16[6,16,128]{2,1,0:T(8,128)(2,1)S(1)} %pad_maximum_fusion), channel_id=1, source_target_pairs={{0,7},{1,2},{2,1},{3,4},{4,3},{5,6},{6,5},{7,0},{8,15},{9,10},{10,... | collective-permute-start | bytes 73736 | tf_op jit(solution)/shard_map/ppermute | solution.py:43
  12.2 3.8 %collective-permute-start.3 = (bf16[6,16,128]{2,1,0:T(8,128)(2,1)S(1)}, bf16[6,16,128]{2,1,0:T(8,128)(2,1)S(1)}, u32[]{:S(2)}, u32[]{:S(2)}) collective-permute-start(bf16[6,16,128]{2,1,0:T(8,128)(2,1)S(1)} %pad_maximum_fusion.1), channel_id=1, source_target_pairs={{0,1},{1,0},{2,3},{3,2},{4,5},{5,4},{6,7},{7,6},{8,9},{9,8},{10,11... | collective-permute-start | bytes 73736 | tf_op jit(solution)/shard_map/ppermute | solution.py:43
  12.9 3.2 %copy-start.1 = (s32[128]{0:T(128)S(1)}, s32[128]{0:T(128)}, u32[]{:S(2)}) copy-start(s32[128]{0:T(128)} %tile_slot.3) | copy-start | bytes 1540
  12.9 3.2 %copy-start.2 = (s32[128]{0:T(128)S(1)}, s32[128]{0:T(128)}, u32[]{:S(2)}) copy-start(s32[128]{0:T(128)} %tile_cell.3) | copy-start | bytes 1540
  16.0 9.4 %copy-start = (f32[2,8]{1,0:T(2,128)S(1)}, f32[2,8]{1,0:T(2,128)}, u32[]{:S(2)}) copy-start(f32[2,8]{1,0:T(2,128)} %props.3) | copy-start | bytes 196
  18.2 10.7 %collective-permute-start.6 = (bf16[384,128]{1,0:T(8,128)(2,1)S(1)}, bf16[384,128]{1,0:T(8,128)(2,1)S(1)}, u32[]{:S(2)}, u32[]{:S(2)}) collective-permute-start(bf16[384,128]{1,0:T(8,128)(2,1)S(1)} %get-tuple-element.27), channel_id=1, source_target_pairs={{1,2},{2,1},{3,4},{4,3},{5,6},{6,5},{9,10},{10,9},{11,12},{12,11},... | collective-permute-start | bytes 294920 | tf_op jit(solution)/shard_map/ppermute | solution.py:43
  18.9 10.0 %collective-permute-start.7 = (bf16[384,128]{1,0:T(8,128)(2,1)S(1)}, bf16[384,128]{1,0:T(8,128)(2,1)S(1)}, u32[]{:S(2)}, u32[]{:S(2)}) collective-permute-start(bf16[384,128]{1,0:T(8,128)(2,1)S(1)} %get-tuple-element.28), channel_id=1, source_target_pairs={{0,1},{1,0},{2,3},{3,2},{4,5},{5,4},{6,7},{7,6},{8,9},{9,8},{10,11... | collective-permute-start | bytes 294920 | tf_op jit(solution)/shard_map/ppermute | solution.py:43
  22.2 6.7 %collective-permute-start.4 = (bf16[192,128]{1,0:T(8,128)(2,1)S(1)}, bf16[192,128]{1,0:T(8,128)(2,1)S(1)}, u32[]{:S(2)}, u32[]{:S(2)}) collective-permute-start(bf16[192,128]{1,0:T(8,128)(2,1)S(1)} %get-tuple-element.25), channel_id=1, source_target_pairs={{8,16},{16,8},{9,17},{17,9},{10,18},{18,10},{11,19},{19,11},{12,20... | collective-permute-start | bytes 147464 | tf_op jit(solution)/shard_map/ppermute | solution.py:43
  22.8 6.0 %collective-permute-start.5 = (bf16[192,128]{1,0:T(8,128)(2,1)S(1)}, bf16[192,128]{1,0:T(8,128)(2,1)S(1)}, u32[]{:S(2)}, u32[]{:S(2)}) collective-permute-start(bf16[192,128]{1,0:T(8,128)(2,1)S(1)} %get-tuple-element.26), channel_id=1, source_target_pairs={{0,8},{8,0},{16,24},{24,16},{1,9},{9,1},{17,25},{25,17},{2,10},{10... | collective-permute-start | bytes 147464 | tf_op jit(solution)/shard_map/ppermute | solution.py:43
  33.7 6.4 %collective-permute-start.8 = (f32[6,128]{1,0:T(8,128)S(1)}, f32[6,128]{1,0:T(8,128)S(1)}, u32[]{:S(2)}, u32[]{:S(2)}) collective-permute-start(f32[6,128]{1,0:T(8,128)S(1)} %get-tuple-element.36), channel_id=1, source_target_pairs={{0,7},{1,2},{2,1},{3,4},{4,3},{5,6},{6,5},{7,0},{8,15},{9,10},{10,... | collective-permute-start | bytes 9224 | tf_op jit(solution)/shard_map/ppermute | solution.py:43
  35.6 4.5 %collective-permute-start.9 = (f32[6,128]{1,0:T(8,128)S(1)}, f32[6,128]{1,0:T(8,128)S(1)}, u32[]{:S(2)}, u32[]{:S(2)}) collective-permute-start(f32[6,128]{1,0:T(8,128)S(1)} %get-tuple-element.37), channel_id=1, source_target_pairs={{0,1},{1,0},{2,3},{3,2},{4,5},{5,4},{6,7},{7,6},{8,9},{9,8},{10,11... | collective-permute-start | bytes 9224 | tf_op jit(solution)/shard_map/ppermute | solution.py:43
  40.1 3.1 %collective-permute-start.10 = (f32[6,128]{1,0:T(8,128)S(1)}, f32[6,128]{1,0:T(8,128)S(1)}, u32[]{:S(2)}, u32[]{:S(2)}) collective-permute-start(f32[6,128]{1,0:T(8,128)S(1)} %pad_maximum_fusion.3), channel_id=1, source_target_pairs={{0,24},{8,16},{16,8},{24,0},{1,25},{9,17},{17,9},{25,1},{2,26},{10... | collective-permute-start | bytes 9224 | tf_op jit(solution)/shard_map/ppermute | solution.py:43
  40.2 3.0 %collective-permute-start.11 = (f32[6,128]{1,0:T(8,128)S(1)}, f32[6,128]{1,0:T(8,128)S(1)}, u32[]{:S(2)}, u32[]{:S(2)}) collective-permute-start(f32[6,128]{1,0:T(8,128)S(1)} %pad_maximum_fusion.4), channel_id=1, source_target_pairs={{0,8},{8,0},{16,24},{24,16},{1,9},{9,1},{17,25},{25,17},{2,10},{10... | collective-permute-start | bytes 9224 | tf_op jit(solution)/shard_map/ppermute | solution.py:43

commit v4 on v3

--- a/solution.py
+++ b/solution.py
@@ -16,6 +16,7 @@
 ROWS = 16
 UNROLL = 128
 PAIR = 2
+TURN = 16
 GROUP = 8
 DELAY = 4
 MIB = 2**20
@@ -39,8 +40,12 @@
     size = lax.axis_size(axis)
     pairs = [(i, partner(i, size, which)) for i in range(size)]
     if not wrap:
-        pairs = [(i, j) for i, j in pairs if abs(i - j) == 1]
+        pairs = [(i, j if abs(i - j) == 1 else i) for i, j in pairs]
     return lax.ppermute(value, axis, pairs)
+
+
+def has_far(index, size):
+    return (index > 0) & (index < size - 1)
 
 
 def code_of(index, mine):
@@ -121,7 +126,7 @@
     )(*(in_hbm(value) for value in (dest, props, volume, velocity, energy, mat)))
 
 
-def stage_kernel(cell, state, sem):
+def stage_kernel(cell, weight, state, turned, sem):
     columns = state.shape[0] - 2
     width = state.shape[2] - 2 * PAD
     copies = [
@@ -132,23 +137,33 @@
     ]
     for copy in copies:
         copy.start()
+
+    def transpose(step, carry):
+        for k in range(TURN):
+            turned[step * TURN + k] = weight[step * TURN + k].T
+        return carry
+
+    lax.fori_loop(0, weight.shape[0] // TURN, transpose, 0)
     for copy in copies:
         copy.wait()
 
 
-def stage(cell):
+def stage(cell, weight):
     count, width, lanes = cell.shape
     columns = lanes // BLK
     return pl.pallas_call(
         stage_kernel,
         name="stage",
-        out_shape=pltpu.VMEM((columns + 2, count, width + 2 * PAD, BLK), F32),
-        in_specs=[ANY],
-        out_specs=VMEM,
+        out_shape=(
+            pltpu.VMEM((columns + 2, count, width + 2 * PAD, BLK), F32),
+            pltpu.VMEM(weight.shape, weight.dtype),
+        ),
+        in_specs=[ANY, VMEM],
+        out_specs=(VMEM, VMEM),
         scratch_shapes=[pltpu.SemaphoreType.DMA((columns,))],
         compiler_params=pltpu.CompilerParams(vmem_limit_bytes=2 * MIB),
         cost_estimate=pl.CostEstimate(flops=0, bytes_accessed=2 * cell.size * 4, transcendentals=0),
-    )(in_hbm(cell))
+    )(in_hbm(cell), weight)
 
 
 def fetch_kernel(source, target, sem):
@@ -301,14 +316,14 @@
     return keep, jnp.maximum(lower, 0.0), jnp.maximum(-upper, 0.0), same, other
 
 
-def values_at(state, weights, j, first_row):
+def values_at(state, weights, j, first_row, wanted):
     low = low_lanes()
     here = slice(first_row, first_row + 8)
     before = slice(first_row - 1, first_row + 7)
     after = slice(first_row + 1, first_row + 9)
     keep, take_before, take_after, same, other = weights
     values = []
-    for q in range(state.shape[1]):
+    for q in wanted:
         mid = state[j, q, here, :]
         beside = jnp.where(low, state[j + 1, q, here, :], state[j - 1, q, here, :])
         value = (keep * mid + take_before * state[j, q, before, :]) + take_after * state[j, q, after, :]
@@ -321,23 +336,28 @@
     return total(terms) + 0.4 * values[-1]
 
 
-def remap_tiles(props, state, speed, press, fresh, places):
+def remap_tiles(props, state, speed, press, fresh, places, wanted):
     weights, values = {}, {}
     for step in range(len(places) + 2):
         if step < len(places):
             weights[step] = weights_at(speed, *places[step])
         k = step - 1
         if 0 <= k < len(places):
-            values[k] = values_at(state, weights.pop(k), *places[k])
+            values[k] = values_at(state, weights.pop(k), *places[k], wanted)
         k = step - 2
         if k >= 0:
             found = values.pop(k)
             j, first_row = places[k]
             inside = slice(first_row - PAD, first_row - PAD + 8)
             lanes = column_lanes(j)
-            for q, value in enumerate(found):
+            for q, value in zip(wanted, found, strict=True):
                 fresh[q, inside, lanes] = value
-            press[j - 1, inside, :] = pressure_of(props, found)
+            if press is not None:
+                press[j - 1, inside, :] = pressure_of(props, found)
+
+
+def scalars(count):
+    return [*range(MAT), count - 1]
 
 
 def column_lanes(j):
@@ -360,7 +380,7 @@
     def remap(step, carry):
         rows = range(PAD + 8, tall - PAD - 8, 8)
         places = [(2 + step * PAIR + k, row) for k in range(PAIR) for row in rows]
-        remap_tiles(props, state, speed, press, fresh, places)
+        remap_tiles(props, state, speed, press, fresh, places, scalars(state.shape[1]))
         return carry
 
     lax.fori_loop(0, (columns - 2) // PAIR, remap, 0)
@@ -385,44 +405,32 @@
 
 def outer_kernel(
     props, tile_slot, tile_cell, tile_count, edge_x1, edge_x2, edge_y1, edge_y2, weight, state_in, speed_in, press_in,
-    fresh_in, remapped, state, speed, press, fresh, own, first, second, sums, sem, *, size_y
+    fresh_in, state, speed, press, fresh, own, first, second, sums, *, size_x, size_y
 ):
     pos_x, pos_y = lax.axis_index("gx"), lax.axis_index("gy")
     n_tiles = weight.shape[0]
     columns, count, tall = state.shape[0] - 2, state.shape[1], state.shape[2]
     width = tall - 2 * PAD
-    middle = pl.ds(8, width - 16)
-    areas = (
-        (middle, pl.ds(BLK, (columns - 2) * BLK)),
-        (pl.ds(0, 8), pl.ds(0, columns * BLK)),
-        (pl.ds(width - 8, 8), pl.ds(0, columns * BLK)),
-        (middle, pl.ds(0, BLK)),
-        (middle, pl.ds((columns - 1) * BLK, BLK)),
-    )
-    copies = [
-        pltpu.make_async_copy(fresh.at[:, rows, lanes], remapped.at[:, rows, lanes], sem.at[k])
-        for k, (rows, lanes) in enumerate(areas)
-    ]
-    copies[0].start()
     even_x, even_y = (pos_x & 1) == 0, (pos_y & 1) == 0
     line = state.reshape((columns + 2) * count * tall, BLK)
     above, below = tall - PAD, PAD - 1
-    for edge, row in (
-        (edge_x1, jnp.where(even_x, below, above)),
-        (edge_x2, jnp.where(even_x, above, below)),
+    for edge, row, there in (
+        (edge_x1, jnp.where(even_x, below, above), has_far(pos_x, size_x)),
+        (edge_x2, jnp.where(even_x, above, below), True),
     ):
         for q in range(count):
             at = pl.ds(count * tall + q * tall + row, columns, stride=count * tall)
-            line[at, :] = edge[q * columns : (q + 1) * columns, :].astype(F32)
+            line[at, :] = jnp.where(there, edge[q * columns : (q + 1) * columns, :].astype(F32), 0.0)
     low = low_lanes()
-    for edge, column in (
-        (edge_y1, jnp.where(even_y, 0, columns + 1)),
-        (edge_y2, jnp.where(even_y, columns + 1, 0)),
+    for edge, column, there in (
+        (edge_y1, jnp.where(even_y, 0, columns + 1), has_far(pos_y, size_y)),
+        (edge_y2, jnp.where(even_y, columns + 1, 0), True),
     ):
         for q in range(count // 2):
             for i in range(width // ROWS):
                 here = slice(PAD + i * ROWS, PAD + (i + 1) * ROWS)
                 both = edge[q * width + i * ROWS : q * width + (i + 1) * ROWS, :].astype(F32)
+                both = jnp.where(there, both, 0.0)
                 turned = turn(both)
                 state[column, q, here, :] = jnp.where(low, both, turned)
                 state[column, q + count // 2, here, :] = jnp.where(low, turned, both)
@@ -434,16 +442,12 @@
 
     def sides(step, carry):
         places = [(1 + step * 2 * PAIR + k, row) for k in range(2 * PAIR) for row in (PAD, tall - PAD - 8)]
-        remap_tiles(props, state, speed, press, fresh, places)
+        remap_tiles(props, state, speed, press, fresh, places, scalars(state.shape[1]))
         return carry
 
     lax.fori_loop(0, columns // (2 * PAIR), sides, 0)
-    copies[1].start()
-    copies[2].start()
     places = [(j, row) for j in (1, columns) for row in range(PAD + 8, tall - PAD - 8, 8)]
-    remap_tiles(props, state, speed, press, fresh, places)
-    copies[3].start()
-    copies[4].start()
+    remap_tiles(props, state, speed, press, fresh, places, scalars(state.shape[1]))
 
     sums[...] = jnp.zeros(sums.shape, F32)
     counted = tile_count[0]
@@ -455,7 +459,7 @@
             slot = local_slot(tile_slot[t], pos_x, pos_y, size_y)
             x, j = split_device(tile_cell[t], columns)
             probe = jnp.where(head, press[j, pl.ds(x, 1), :], 1.0).astype(BF16)
-            both = lax.dot_general(probe, weight[t], (((1,), (1,)), ((), ())), preferred_element_type=F32)[:8]
+            both = jnp.dot(probe, weight[t], preferred_element_type=F32)[:8]
             sums[slot] = sums[slot] + jnp.where(t < counted, both, 0.0)
         return carry
 
@@ -466,17 +470,13 @@
         under = table[pl.ds(k * 3 * CAP * 8 + 1, 3 * CAP, stride=8), :]
         out[...] = top / jnp.maximum(under, 1.0)
 
-    for copy in copies:
-        copy.wait()
-
-
-def outer(props, tile_slot, tile_cell, tile_count, edges, weight, state, speed, press, fresh, size_y):
+
+def outer(props, tile_slot, tile_cell, tile_count, edges, weight, state, speed, press, fresh, size_x, size_y):
     answer = pltpu.VMEM((3 * CAP, BLK), F32)
     outs = pl.pallas_call(
-        functools.partial(outer_kernel, size_y=size_y),
+        functools.partial(outer_kernel, size_x=size_x, size_y=size_y),
         name="outer",
         out_shape=(
-            jax.ShapeDtypeStruct(fresh.shape, F32),
             pltpu.VMEM(state.shape, F32),
             pltpu.VMEM(speed.shape, F32),
             pltpu.VMEM(press.shape, F32),
@@ -486,29 +486,67 @@
             answer,
         ),
         in_specs=[SMEM] * 4 + [VMEM] * 9,
-        out_specs=(ANY,) + (VMEM,) * 7,
-        input_output_aliases={9: 1, 10: 2, 11: 3, 12: 4},
-        scratch_shapes=[pltpu.VMEM((9 * CAP, 8, BLK), F32), pltpu.SemaphoreType.DMA((5,))],
+        out_specs=(VMEM,) * 7,
+        input_output_aliases={9: 0, 10: 1, 11: 2, 12: 3},
+        scratch_shapes=[pltpu.VMEM((9 * CAP, 8, BLK), F32)],
         compiler_params=pltpu.CompilerParams(vmem_limit_bytes=4 * MIB),
     )(props, tile_slot, tile_cell, tile_count, *edges, weight, state, speed, press, fresh)
-    return outs[0], outs[5], outs[6], outs[7]
-
-
-def pick_kernel(place, own, first, second, out, table):
+    return outs[0], outs[1], outs[3], outs[4], outs[5], outs[6]
+
+
+def late_kernel(state, speed, fresh_in, remapped, fresh, sem):
+    columns, count, tall = state.shape[0] - 2, state.shape[1], state.shape[2]
+    moving = range(MAT, count - 1)
+    copies = [
+        pltpu.make_async_copy(fresh.at[rows], remapped.at[rows], sem.at[k])
+        for k, rows in enumerate((pl.ds(0, MAT), pl.ds(count - 1, 1), pl.ds(MAT, count - 1 - MAT)))
+    ]
+    copies[0].start()
+    copies[1].start()
+
+    def remap(step, carry):
+        rows = range(PAD, tall - PAD, 8)
+        places = [(1 + step * PAIR + k, row) for k in range(PAIR) for row in rows]
+        remap_tiles(None, state, speed, None, fresh, places, moving)
+        return carry
+
+    lax.fori_loop(0, columns // PAIR, remap, 0)
+    copies[2].start()
+    for copy in copies:
+        copy.wait()
+
+
+def late(state, speed, fresh):
+    return pl.pallas_call(
+        late_kernel,
+        name="late",
+        out_shape=(jax.ShapeDtypeStruct(fresh.shape, F32), pltpu.VMEM(fresh.shape, F32)),
+        in_specs=[VMEM] * 3,
+        out_specs=(ANY, VMEM),
+        input_output_aliases={2: 1},
+        scratch_shapes=[pltpu.SemaphoreType.DMA((3,))],
+        compiler_params=pltpu.CompilerParams(vmem_limit_bytes=4 * MIB),
+        cost_estimate=pl.CostEstimate(flops=5 * state.size, bytes_accessed=2 * state.size * 4, transcendentals=0),
+    )(state, speed, fresh)[0]
+
+
+def pick_kernel(place, own, first, second, out, table, lines):
     for k, part in enumerate((own, first, second)):
         table[k * 3 * CAP : (k + 1) * 3 * CAP, :] = part[...]
     for b in range(out.shape[0]):
-        out[b : b + 1, :] = table[pl.ds(place[b], 1), :]
+        lines[b : b + 1, :] = table[pl.ds(place[b], 1), :]
+    out[...] = lines[...].astype(BF16)
 
 
 def pick(place, own, first, second):
+    n_blocks = place.shape[0]
     return pl.pallas_call(
         pick_kernel,
         name="pick",
-        out_shape=pltpu.VMEM((place.shape[0], BLK), F32),
+        out_shape=jax.ShapeDtypeStruct((n_blocks, BLK), BF16),
         in_specs=[SMEM, VMEM, VMEM, VMEM],
         out_specs=VMEM,
-        scratch_shapes=[pltpu.VMEM((9 * CAP, BLK), F32)],
+        scratch_shapes=[pltpu.VMEM((9 * CAP, BLK), F32), pltpu.VMEM((n_blocks, BLK), F32)],
         compiler_params=pltpu.CompilerParams(vmem_limit_bytes=2 * MIB),
     )(place, own, first, second)
 
@@ -526,7 +564,7 @@
     cell_state,
     mat_props,
 ):
-    size_y = lax.axis_size("gy")
+    size_x, size_y = lax.axis_size("gx"), lax.axis_size("gy")
     n_blocks = elem_dest.shape[0]
     shape = (n_blocks, BLK)
     own, first, second, place = payload(
@@ -538,12 +576,12 @@
         elem_mat.reshape(shape),
         size_y,
     )
-    state = stage(cell_state)
     weight = fetch(tile_weight)
 
     first = swap(first, "gx", 1)
     second = swap(second, "gx", 2)
     weight, own = lax.optimization_barrier((weight, own))
+    state, turned = stage(cell_state, weight)
 
     def along_y(which):
         rows = slice(which * CAP, (which + 1) * CAP)
@@ -555,15 +593,16 @@
         tile_slot, tile_cell, tile_count, (own, first, second, south, north), weight, state, size_y
     )
     edges = (
-        swap(edges[0], "gx", 1, wrap=False),
-        swap(edges[1], "gx", 2, wrap=False),
+        swap(edges[0], "gx", 1),
+        swap(edges[1], "gx", 2),
         swap(edges[2], "gy", 1, wrap=False),
-        swap(edges[3], "gy", 2, wrap=False),
+        swap(edges[3], "gy", 2),
     )
     fresh, press, speed = inner(mat_props, state, cell_state.shape[1])
-    remapped, own, first, second = outer(
-        mat_props, tile_slot, tile_cell, tile_count, edges, weight, state, speed, press, fresh, size_y
-    )
+    state, speed, fresh, own, first, second = outer(
+        mat_props, tile_slot, tile_cell, tile_count, edges, turned, state, speed, press, fresh, size_x, size_y
+    )
+    remapped = late(state, speed, fresh)
     first = swap(first, "gy", 1)
     second = swap(second, "gy", 2)
 
@@ -572,7 +611,7 @@
         return jnp.concatenate([own[rows], first[rows], second[rows]], axis=0)
 
     back = pick(place, along_x(0), swap(along_x(1), "gx", 1), swap(along_x(2), "gx", 2))
-    return remapped, back.astype(BF16).reshape(n_blocks * BLK)
+    return remapped, back.reshape(n_blocks * BLK)
 
 
 def solution(mesh):

time: 44.6 us -> 40.9 us (0.917)
  waiting for transfers between devices: 6.37 us -> 2.58 us
  Pallas kernels: 17.7 us -> 19.4 us
  starting transfers between devices: 18.1 us -> 17.2 us
  other arithmetic: 0.64 us -> 0.04 us
    ppermute x12, waiting for transfers between devices: 6.37 us -> 2.58 us  [swap(): return lax.ppermute(value, axis, pairs)]
    pallas_call x3 -> x4, Pallas kernels: 8.38 us -> 10.3 us  [the longest x1 3.43 us: outer(): pl.pallas_call(functools.partial(outer_kernel, size_x=size_x, size_y=size...]
    ppermute x12, starting transfers between devices: 18.1 us -> 17.2 us  [swap(): return lax.ppermute(value, axis, pairs)]
    reshape x1 -> x0, other arithmetic: 0.6 us -> none  [per_device(): return (remapped, back.astype(BF16).reshape(n_blocks * BLK))]
  transfers between devices with their start and end apart: 12 -> 12, of which waited for: 3 -> 3; matrix products, arithmetic and copies ran while one was open for 0% -> 0% of each run, Pallas kernels for 20% -> 27%
where the time goes in v4:
time: 40.9 us; the launch traced here: 40.7 us
  Pallas kernels  19.4 us (47%)
  starting transfers between devices  17.2 us (42%)
  waiting for transfers between devices  2.58 us (6%)
  between operations  1.47 us (4%)
    ppermute x12, starting transfers between devices, swap(): return lax.ppermute(value, axis, pairs)  17.2 us
    pallas_call x1, Pallas kernels, outer(): pl.pallas_call(functools.partial(outer_kernel, size_x=size_x, size_y=size...  3.43 us
    pallas_call x1, Pallas kernels, inner(): pl.pallas_call(inner_kernel, name='inner', out_shape=(pltpu.VMEM((count,...  3.16 us
    pallas_call x1, Pallas kernels, stage(): pl.pallas_call(stage_kernel, name='stage', out_shape=(pltpu.VMEM((columns...  3.03 us
    pallas_call x1, Pallas kernels, late(): pl.pallas_call(late_kernel, name='late', out_shape=(jax.ShapeDtypeStruct(...  2.7 us
    ppermute x12, waiting for transfers between devices, swap(): return lax.ppermute(value, axis, pairs)  2.58 us
    pallas_call x1, Pallas kernels, fetch(): pl.pallas_call(fetch_kernel, name='fetch', out_shape=pltpu.VMEM(value.sha...  2.2 us
    pallas_call x1, Pallas kernels, deposit(): pl.pallas_call(functools.partial(deposit_kernel, size_y=size_y), name='de...  2.13 us
  transfers between devices with their start and end apart: 12, of which 3 were waited for; matrix products, arithmetic and copies ran while one was open for 0% of the time, Pallas kernels for 27%

profile of v4, /device:TPU:0, one launch (start us, length us, event | category | flops | bytes accessed | tf_op | source)
XLA Modules:
  0.0 40.7 jit_solution(10893555479633788435)
XLA Ops:
  0.6 1.6 %payload.1 = (bf16[6,16,128]{2,1,0:T(8,128)(2,1)S(1)}, bf16[6,16,128]{2,1,0:T(8,128)(2,1)S(1)}, bf16[6,16,128]{2,1,0:T(8,128)(2,1)S(1)}, s32[18]{0:T(128)S(1)}) custom-call(s32[18]{0:T(128)} %dest_hbm.1, f32[2,8]{1,0:T(2,128)} %props.3, f32[18,128]{1,0:T(8,128)} %bitcast.4, f32[3,2304]{1,0:T(4,128)} %velocity_hbm.1, f32[18,128]{1,0:T(8,128)} %bitcast.5, ...), custom_call_target="tpu_custom_call" | custom-call | tf_op jit(solution)/shard_map/payload/pallas_call | solution.py:108
  2.2 2.5 %collective-permute-start = (bf16[6,16,128]{2,1,0:T(8,128)(2,1)S(1)}, bf16[6,16,128]{2,1,0:T(8,128)(2,1)S(1)}, u32[]{:S(2)}, u32[]{:S(2)}) collective-permute-start(bf16[6,16,128]{2,1,0:T(8,128)(2,1)S(1)} %get-tuple-element.27), channel_id=1, source_target_pairs={{0,24},{8,16},{16,8},{24,0},{1,25},{9,17},{17,9},{25,1},{2,26},{10... | collective-permute-start | bytes 73736 | tf_op jit(solution)/shard_map/ppermute | solution.py:44
  4.7 0.7 %collective-permute-start.1 = (bf16[6,16,128]{2,1,0:T(8,128)(2,1)S(1)}, bf16[6,16,128]{2,1,0:T(8,128)(2,1)S(1)}, u32[]{:S(2)}, u32[]{:S(2)}) collective-permute-start(bf16[6,16,128]{2,1,0:T(8,128)(2,1)S(1)} %get-tuple-element.28), channel_id=1, source_target_pairs={{0,8},{8,0},{16,24},{24,16},{1,9},{9,1},{17,25},{25,17},{2,10},{10... | collective-permute-start | bytes 73736 | tf_op jit(solution)/shard_map/ppermute | solution.py:44
  5.4 2.2 %fetch.1.weight = bf16[128,128,128]{2,1,0:T(8,128)(2,1)S(1)} custom-call(bf16[128,128,128]{2,1,0:T(8,128)(2,1)} %source.1), custom_call_target="tpu_custom_call" | custom-call | bytes 8388608 | tf_op jit(solution)/shard_map/fetch/pallas_call | solution.py:176
  7.6 0.0 copy-start.1
  7.6 0.0 copy-start.2
  7.6 0.0 collective-permute-done.first
  7.6 0.0 collective-permute-done.1.second
  7.7 4.6 %collective-permute-start.2 = (bf16[6,16,128]{2,1,0:T(8,128)(2,1)S(1)}, bf16[6,16,128]{2,1,0:T(8,128)(2,1)S(1)}, u32[]{:S(2)}, u32[]{:S(2)}) collective-permute-start(bf16[6,16,128]{2,1,0:T(8,128)(2,1)S(1)} %pad_maximum_fusion), channel_id=1, source_target_pairs={{0,7},{1,2},{2,1},{3,4},{4,3},{5,6},{6,5},{7,0},{8,15},{9,10},{10,... | collective-permute-start | bytes 73736 | tf_op jit(solution)/shard_map/ppermute | solution.py:44
  12.3 0.0 collective-permute-start.3
  12.9 3.0 %stage.1 = (f32[18,12,80,128]{3,2,1,0:T(8,128)S(1)}, bf16[128,128,128]{2,1,0:T(8,128)(2,1)S(1)}) custom-call(f32[12,64,2048]{2,1,0:T(8,128)} %cell.1, bf16[128,128,128]{2,1,0:T(8,128)(2,1)S(1)} %fetch.1.weight), custom_call_target="tpu_custom_call" | custom-call | bytes 12582912 | tf_op jit(solution)/shard_map/stage/pallas_call | solution.py:154
  16.0 0.0 collective-permute-done.2.south
  16.0 0.1 collective-permute-done.3.north
  16.1 0.0 copy-done.1
  16.1 0.0 copy-done.2
  16.1 0.0 copy-start
  16.1 2.1 %deposit.1 = (f32[18,12,80,128]{3,2,1,0:T(8,128)S(1)}, bf16[192,128]{1,0:T(8,128)(2,1)S(1)}, bf16[192,128]{1,0:T(8,128)(2,1)S(1)}, bf16[384,128]{1,0:T(8,128)(2,1)S(1)}, bf16[384,128]{1,0:T(8,128)(2,1)S(1)}) custom-call(s32[128]{0:T(128)S(1)} %copy-done.1, s32[128]{0:T(128)S(1)} %copy-done.2, ...), custom_call_target="tpu_custom_call", output_to_operand_aliasing={{0}: (9, {})} | custom-call | tf_op jit(solution)/shard_map/deposit/pallas_call | solution.py:257
  18.2 0.7 %collective-permute-start.6 = (bf16[384,128]{1,0:T(8,128)(2,1)S(1)}, bf16[384,128]{1,0:T(8,128)(2,1)S(1)}, u32[]{:S(2)}, u32[]{:S(2)}) collective-permute-start(bf16[384,128]{1,0:T(8,128)(2,1)S(1)} %get-tuple-element.33), channel_id=1, source_target_pairs={{0,0},{1,2},{2,1},{3,4},{4,3},{5,6},{6,5},{7,7},{8,8},{9,10},{10,9... | collective-permute-start | bytes 294920 | tf_op jit(solution)/shard_map/ppermute | solution.py:44
  18.9 3.3 %collective-permute-start.7 = (bf16[384,128]{1,0:T(8,128)(2,1)S(1)}, bf16[384,128]{1,0:T(8,128)(2,1)S(1)}, u32[]{:S(2)}, u32[]{:S(2)}) collective-permute-start(bf16[384,128]{1,0:T(8,128)(2,1)S(1)} %get-tuple-element.34), channel_id=1, source_target_pairs={{0,1},{1,0},{2,3},{3,2},{4,5},{5,4},{6,7},{7,6},{8,9},{9,8},{10,11... | collective-permute-start | bytes 294920 | tf_op jit(solution)/shard_map/ppermute | solution.py:44
  22.2 0.0 collective-permute-start.4
  22.2 1.2 %collective-permute-start.5 = (bf16[192,128]{1,0:T(8,128)(2,1)S(1)}, bf16[192,128]{1,0:T(8,128)(2,1)S(1)}, u32[]{:S(2)}, u32[]{:S(2)}) collective-permute-start(bf16[192,128]{1,0:T(8,128)(2,1)S(1)} %get-tuple-element.32), channel_id=1, source_target_pairs={{0,8},{8,0},{16,24},{24,16},{1,9},{9,1},{17,25},{25,17},{2,10},{10... | collective-permute-start | bytes 147464 | tf_op jit(solution)/shard_map/ppermute | solution.py:44
  23.4 0.0 copy-done
  23.4 3.2 %inner.1 = (f32[12,64,2048]{2,1,0:T(8,128)S(1)}, f32[16,64,128]{2,1,0:T(8,128)S(1)}, f32[18,3,80,128]{3,2,1,0:T(8,128)S(1)}) custom-call(f32[2,8]{1,0:T(2,128)S(1)} %copy-done, f32[18,12,80,128]{3,2,1,0:T(8,128)S(1)} %get-tuple-element.36.state.state_in), custom_call_target="tpu_custom_call" | custom-call | flops 44236800 | bytes 17694720 | tf_op jit(solution)/shard_map/inner/pallas_call | solution.py:391
  26.6 0.0 collective-permute-done.4.edge_x1
  26.6 0.0 collective-permute-done.5.edge_x2
  26.6 0.0 collective-permute-done.6.edge_y1
  26.6 0.0 collective-permute-done.7.edge_y2
  26.6 3.4 %outer.1 = (f32[18,12,80,128]{3,2,1,0:T(8,128)S(1)}, f32[18,3,80,128]{3,2,1,0:T(8,128)S(1)}, f32[16,64,128]{2,1,0:T(8,128)S(1)}, f32[12,64,2048]{2,1,0:T(8,128)S...) custom-call(f32[2,8]{1,0:T(2,128)S(1)} %copy-done, ...), custom_call_target="tpu_custom_call", output_to_operand_aliasing={{0}: (9, {}), {1}: (10, {}), {2}: (11, {}), {3}: (12, {})} | custom-call | tf_op jit(solution)/shard_map/outer/pallas_call | solution.py:476
  30.0 1.9 %collective-permute-start.8 = (f32[6,128]{1,0:T(8,128)S(1)}, f32[6,128]{1,0:T(8,128)S(1)}, u32[]{:S(2)}, u32[]{:S(2)}) collective-permute-start(f32[6,128]{1,0:T(8,128)S(1)} %get-tuple-element.46), channel_id=1, source_target_pairs={{0,7},{1,2},{2,1},{3,4},{4,3},{5,6},{6,5},{7,0},{8,15},{9,10},{10,... | collective-permute-start | bytes 9224 | tf_op jit(solution)/shard_map/ppermute | solution.py:44
  31.9 1.3 %collective-permute-start.9 = (f32[6,128]{1,0:T(8,128)S(1)}, f32[6,128]{1,0:T(8,128)S(1)}, u32[]{:S(2)}, u32[]{:S(2)}) collective-permute-start(f32[6,128]{1,0:T(8,128)S(1)} %get-tuple-element.47), channel_id=1, source_target_pairs={{0,1},{1,0},{2,3},{3,2},{4,5},{5,4},{6,7},{7,6},{8,9},{9,8},{10,11... | collective-permute-start | bytes 9224 | tf_op jit(solution)/shard_map/ppermute | solution.py:44
  33.2 2.7 %late.1 = (f32[12,64,2048]{2,1,0:T(8,128)}, f32[12,64,2048]{2,1,0:T(8,128)S(1)}) custom-call(f32[18,12,80,128]{3,2,1,0:T(8,128)S(1)} %get-tuple-element.40.state, f32[18,3,80,128]{3,2,1,0:T(8,128)S(1)} %get-tuple-element.41.speed, f32[12,64,2048]{2,1,0:T(8,128)S(1)} %get-tuple-element.42.fresh_in), custom_call_target="tpu_custom_call", output_to_operand_aliasing={{1}: (2, {})} | custom-call | flops 11059200 | bytes 17694720 | tf_op jit(solution)/shard_map/late/pallas_call | solution.py:520
  35.9 0.5 %collective-permute-done.8 = f32[6,128]{1,0:T(8,128)S(1)} collective-permute-done((f32[6,128]{1,0:T(8,128)S(1)}, f32[6,128]{1,0:T(8,128)S(1)}, u32[]{:S(2)}, u32[]{:S(2)}) %collective-permute-start.8) | collective-permute-done | bytes 3104 | tf_op jit(solution)/shard_map/ppermute | solution.py:44
  36.4 0.0 collective-permute-done.9
  36.4 0.1 collective-permute-start.10
  36.5 1.1 %collective-permute-start.11 = (f32[6,128]{1,0:T(8,128)S(1)}, f32[6,128]{1,0:T(8,128)S(1)}, u32[]{:S(2)}, u32[]{:S(2)}) collective-permute-start(f32[6,128]{1,0:T(8,128)S(1)} %pad_maximum_fusion.4), channel_id=1, source_target_pairs={{0,8},{8,0},{16,24},{24,16},{1,9},{9,1},{17,25},{25,17},{2,10},{10... | collective-permute-start | bytes 9224 | tf_op jit(solution)/shard_map/ppermute | solution.py:44
  37.6 1.9 %collective-permute-done.10.first = f32[6,128]{1,0:T(8,128)S(1)} collective-permute-done((f32[6,128]{1,0:T(8,128)S(1)}, f32[6,128]{1,0:T(8,128)S(1)}, u32[]{:S(2)}, u32[]{:S(2)}) %collective-permute-start.10) | collective-permute-done | bytes 3104 | tf_op jit(solution)/shard_map/ppermute | solution.py:44
  39.5 0.0 collective-permute-done.11.second
  39.5 1.2 %pick.1 = bf16[18,128]{1,0:T(8,128)(2,1)} custom-call(s32[18]{0:T(128)S(1)} %get-tuple-element.44.place, f32[6,128]{1,0:T(8,128)S(1)} %pad_maximum_fusion.2.own, f32[6,128]{1,0:T(8,128)S(1)} %collective-permute-done.10.first, f32[6,128]{1,0:T(8,128)S(1)} %collective-permute-done.11.second), custom_call_target="tpu_custom_call" | custom-call | tf_op jit(solution)/shard_map/pick/pallas_call | solution.py:543
  (11 shorter events, 0.1 us)
Async XLA Ops:
  2.2 5.4 %collective-permute-start = (bf16[6,16,128]{2,1,0:T(8,128)(2,1)S(1)}, bf16[6,16,128]{2,1,0:T(8,128)(2,1)S(1)}, u32[]{:S(2)}, u32[]{:S(2)}) collective-permute-start(bf16[6,16,128]{2,1,0:T(8,128)(2,1)S(1)} %get-tuple-element.27), channel_id=1, source_target_pairs={{0,24},{8,16},{16,8},{24,0},{1,25},{9,17},{17,9},{25,1},{2,26},{10... | collective-permute-start | bytes 73736 | tf_op jit(solution)/shard_map/ppermute | solution.py:44
  4.7 2.9 %collective-permute-start.1 = (bf16[6,16,128]{2,1,0:T(8,128)(2,1)S(1)}, bf16[6,16,128]{2,1,0:T(8,128)(2,1)S(1)}, u32[]{:S(2)}, u32[]{:S(2)}) collective-permute-start(bf16[6,16,128]{2,1,0:T(8,128)(2,1)S(1)} %get-tuple-element.28), channel_id=1, source_target_pairs={{0,8},{8,0},{16,24},{24,16},{1,9},{9,1},{17,25},{25,17},{2,10},{10... | collective-permute-start | bytes 73736 | tf_op jit(solution)/shard_map/ppermute | solution.py:44
  7.6 8.5 %copy-start.1 = (s32[128]{0:T(128)S(1)}, s32[128]{0:T(128)}, u32[]{:S(2)}) copy-start(s32[128]{0:T(128)} %tile_slot.3) | copy-start | bytes 1540
  7.6 8.5 %copy-start.2 = (s32[128]{0:T(128)S(1)}, s32[128]{0:T(128)}, u32[]{:S(2)}) copy-start(s32[128]{0:T(128)} %tile_cell.3) | copy-start | bytes 1540
  7.7 8.3 %collective-permute-start.2 = (bf16[6,16,128]{2,1,0:T(8,128)(2,1)S(1)}, bf16[6,16,128]{2,1,0:T(8,128)(2,1)S(1)}, u32[]{:S(2)}, u32[]{:S(2)}) collective-permute-start(bf16[6,16,128]{2,1,0:T(8,128)(2,1)S(1)} %pad_maximum_fusion), channel_id=1, source_target_pairs={{0,7},{1,2},{2,1},{3,4},{4,3},{5,6},{6,5},{7,0},{8,15},{9,10},{10,... | collective-permute-start | bytes 73736 | tf_op jit(solution)/shard_map/ppermute | solution.py:44
  12.3 3.8 %collective-permute-start.3 = (bf16[6,16,128]{2,1,0:T(8,128)(2,1)S(1)}, bf16[6,16,128]{2,1,0:T(8,128)(2,1)S(1)}, u32[]{:S(2)}, u32[]{:S(2)}) collective-permute-start(bf16[6,16,128]{2,1,0:T(8,128)(2,1)S(1)} %pad_maximum_fusion.1), channel_id=1, source_target_pairs={{0,1},{1,0},{2,3},{3,2},{4,5},{5,4},{6,7},{7,6},{8,9},{9,8},{10,11... | collective-permute-start | bytes 73736 | tf_op jit(solution)/shard_map/ppermute | solution.py:44
  16.1 7.3 %copy-start = (f32[2,8]{1,0:T(2,128)S(1)}, f32[2,8]{1,0:T(2,128)}, u32[]{:S(2)}) copy-start(f32[2,8]{1,0:T(2,128)} %props.3) | copy-start | bytes 196
  18.2 8.4 %collective-permute-start.6 = (bf16[384,128]{1,0:T(8,128)(2,1)S(1)}, bf16[384,128]{1,0:T(8,128)(2,1)S(1)}, u32[]{:S(2)}, u32[]{:S(2)}) collective-permute-start(bf16[384,128]{1,0:T(8,128)(2,1)S(1)} %get-tuple-element.33), channel_id=1, source_target_pairs={{0,0},{1,2},{2,1},{3,4},{4,3},{5,6},{6,5},{7,7},{8,8},{9,10},{10,9... | collective-permute-start | bytes 294920 | tf_op jit(solution)/shard_map/ppermute | solution.py:44
  18.9 7.7 %collective-permute-start.7 = (bf16[384,128]{1,0:T(8,128)(2,1)S(1)}, bf16[384,128]{1,0:T(8,128)(2,1)S(1)}, u32[]{:S(2)}, u32[]{:S(2)}) collective-permute-start(bf16[384,128]{1,0:T(8,128)(2,1)S(1)} %get-tuple-element.34), channel_id=1, source_target_pairs={{0,1},{1,0},{2,3},{3,2},{4,5},{5,4},{6,7},{7,6},{8,9},{9,8},{10,11... | collective-permute-start | bytes 294920 | tf_op jit(solution)/shard_map/ppermute | solution.py:44
  22.2 4.4 %collective-permute-start.4 = (bf16[192,128]{1,0:T(8,128)(2,1)S(1)}, bf16[192,128]{1,0:T(8,128)(2,1)S(1)}, u32[]{:S(2)}, u32[]{:S(2)}) collective-permute-start(bf16[192,128]{1,0:T(8,128)(2,1)S(1)} %get-tuple-element.31), channel_id=1, source_target_pairs={{0,24},{8,16},{16,8},{24,0},{1,25},{9,17},{17,9},{25,1},{2,26},{10... | collective-permute-start | bytes 147464 | tf_op jit(solution)/shard_map/ppermute | solution.py:44
  22.2 4.4 %collective-permute-start.5 = (bf16[192,128]{1,0:T(8,128)(2,1)S(1)}, bf16[192,128]{1,0:T(8,128)(2,1)S(1)}, u32[]{:S(2)}, u32[]{:S(2)}) collective-permute-start(bf16[192,128]{1,0:T(8,128)(2,1)S(1)} %get-tuple-element.32), channel_id=1, source_target_pairs={{0,8},{8,0},{16,24},{24,16},{1,9},{9,1},{17,25},{25,17},{2,10},{10... | collective-permute-start | bytes 147464 | tf_op jit(solution)/shard_map/ppermute | solution.py:44
  30.0 6.4 %collective-permute-start.8 = (f32[6,128]{1,0:T(8,128)S(1)}, f32[6,128]{1,0:T(8,128)S(1)}, u32[]{:S(2)}, u32[]{:S(2)}) collective-permute-start(f32[6,128]{1,0:T(8,128)S(1)} %get-tuple-element.46), channel_id=1, source_target_pairs={{0,7},{1,2},{2,1},{3,4},{4,3},{5,6},{6,5},{7,0},{8,15},{9,10},{10,... | collective-permute-start | bytes 9224 | tf_op jit(solution)/shard_map/ppermute | solution.py:44
  31.9 4.5 %collective-permute-start.9 = (f32[6,128]{1,0:T(8,128)S(1)}, f32[6,128]{1,0:T(8,128)S(1)}, u32[]{:S(2)}, u32[]{:S(2)}) collective-permute-start(f32[6,128]{1,0:T(8,128)S(1)} %get-tuple-element.47), channel_id=1, source_target_pairs={{0,1},{1,0},{2,3},{3,2},{4,5},{5,4},{6,7},{7,6},{8,9},{9,8},{10,11... | collective-permute-start | bytes 9224 | tf_op jit(solution)/shard_map/ppermute | solution.py:44
  36.4 3.1 %collective-permute-start.10 = (f32[6,128]{1,0:T(8,128)S(1)}, f32[6,128]{1,0:T(8,128)S(1)}, u32[]{:S(2)}, u32[]{:S(2)}) collective-permute-start(f32[6,128]{1,0:T(8,128)S(1)} %pad_maximum_fusion.3), channel_id=1, source_target_pairs={{0,24},{8,16},{16,8},{24,0},{1,25},{9,17},{17,9},{25,1},{2,26},{10... | collective-permute-start | bytes 9224 | tf_op jit(solution)/shard_map/ppermute | solution.py:44
  36.5 3.0 %collective-permute-start.11 = (f32[6,128]{1,0:T(8,128)S(1)}, f32[6,128]{1,0:T(8,128)S(1)}, u32[]{:S(2)}, u32[]{:S(2)}) collective-permute-start(f32[6,128]{1,0:T(8,128)S(1)} %pad_maximum_fusion.4), channel_id=1, source_target_pairs={{0,8},{8,0},{16,24},{24,16},{1,9},{9,1},{17,25},{25,17},{2,10},{10... | collective-permute-start | bytes 9224 | tf_op jit(solution)/shard_map/ppermute | solution.py:44

commit v5 on v4

--- a/solution.py
+++ b/solution.py
@@ -36,12 +36,9 @@
     return (index + 1 if index % 2 else index - 1) % size
 
 
-def swap(value, axis, which, wrap=True):
+def swap(value, axis, which):
     size = lax.axis_size(axis)
-    pairs = [(i, partner(i, size, which)) for i in range(size)]
-    if not wrap:
-        pairs = [(i, j if abs(i - j) == 1 else i) for i, j in pairs]
-    return lax.ppermute(value, axis, pairs)
+    return lax.ppermute(value, axis, [(i, partner(i, size, which)) for i in range(size)])
 
 
 def has_far(index, size):
@@ -63,7 +60,7 @@
 
 
 def payload_kernel(
-    dest_hbm, props_hbm, volume_hbm, velocity_hbm, energy_hbm, mat_hbm, own, first, second, place,
+    dest_hbm, props_hbm, volume_hbm, velocity_hbm, energy_hbm, mat_hbm, weight_hbm, own, first, second, place, weight,
     dest, props, volume, velocity, energy, mat, seen, packed, sem, *, size_y
 ):
     moves = (
@@ -71,8 +68,11 @@
         (volume_hbm, volume), (velocity_hbm, velocity), (energy_hbm, energy),
     )
     copies = [pltpu.make_async_copy(src, dst, sem.at[k]) for k, (src, dst) in enumerate(moves)]
+    some = pl.ds(0, early_tiles(weight.shape[0]))
+    ahead = pltpu.make_async_copy(weight_hbm.at[some], weight.at[some], sem.at[len(moves)])
     for copy in copies:
         copy.start()
+    ahead.start()
     for copy in copies:
         copy.wait()
     pos_x, pos_y = lax.axis_index("gx"), lax.axis_index("gy")
@@ -100,17 +100,28 @@
     for k, out in enumerate((own, first, second)):
         for s in range(3 * CAP):
             out[s] = packed[k * 3 * CAP + s]
-
-
-def payload(dest, props, volume, velocity, energy, mat, size_y):
+    ahead.wait()
+
+
+def early_tiles(n_tiles):
+    return n_tiles * 3 // 8
+
+
+def payload(dest, props, volume, velocity, energy, mat, weight, size_y):
     n_blocks = volume.shape[0]
     parcel = pltpu.VMEM((3 * CAP, ROWS, BLK), BF16)
     return pl.pallas_call(
         functools.partial(payload_kernel, size_y=size_y),
         name="payload",
-        out_shape=(parcel, parcel, parcel, jax.ShapeDtypeStruct((n_blocks,), jnp.int32)),
-        in_specs=[ANY] * 6,
-        out_specs=(VMEM, VMEM, VMEM, SMEM),
+        out_shape=(
+            parcel,
+            parcel,
+            parcel,
+            jax.ShapeDtypeStruct((n_blocks,), jnp.int32),
+            pltpu.VMEM(weight.shape, weight.dtype),
+        ),
+        in_specs=[ANY] * 7,
+        out_specs=(VMEM, VMEM, VMEM, SMEM, VMEM),
         scratch_shapes=[
             pltpu.SMEM(dest.shape, jnp.int32),
             pltpu.SMEM(props.shape, F32),
@@ -120,10 +131,10 @@
             pltpu.VMEM(mat.shape, jnp.int32),
             pltpu.SMEM((9,), jnp.int32),
             pltpu.VMEM((9 * CAP, ROWS, BLK), BF16),
-            pltpu.SemaphoreType.DMA((6,)),
+            pltpu.SemaphoreType.DMA((7,)),
         ],
         compiler_params=pltpu.CompilerParams(vmem_limit_bytes=4 * MIB),
-    )(*(in_hbm(value) for value in (dest, props, volume, velocity, energy, mat)))
+    )(*(in_hbm(value) for value in (dest, props, volume, velocity, energy, mat, weight)))
 
 
 def stage_kernel(cell, weight, state, turned, sem):
@@ -166,23 +177,26 @@
     )(in_hbm(cell), weight)
 
 
-def fetch_kernel(source, target, sem):
-    copy = pltpu.make_async_copy(source, target, sem)
+def fetch_kernel(source, target_in, target, sem):
+    n_tiles = target.shape[0]
+    rest = pl.ds(early_tiles(n_tiles), n_tiles - early_tiles(n_tiles))
+    copy = pltpu.make_async_copy(source.at[rest], target.at[rest], sem)
     copy.start()
     copy.wait()
 
 
-def fetch(value):
+def fetch(value, target):
     return pl.pallas_call(
         fetch_kernel,
         name="fetch",
         out_shape=pltpu.VMEM(value.shape, value.dtype),
-        in_specs=[ANY],
+        in_specs=[ANY, VMEM],
         out_specs=VMEM,
+        input_output_aliases={1: 0},
         scratch_shapes=[pltpu.SemaphoreType.DMA],
         compiler_params=pltpu.CompilerParams(vmem_limit_bytes=2 * MIB),
         cost_estimate=pl.CostEstimate(flops=0, bytes_accessed=2 * value.size * 2, transcendentals=0),
-    )(in_hbm(value))
+    )(in_hbm(value), target)
 
 
 def local_slot(slot, pos_x, pos_y, size_y):
@@ -567,16 +581,17 @@
     size_x, size_y = lax.axis_size("gx"), lax.axis_size("gy")
     n_blocks = elem_dest.shape[0]
     shape = (n_blocks, BLK)
-    own, first, second, place = payload(
+    own, first, second, place, weight = payload(
         elem_dest,
         mat_props,
         elem_volume.reshape(shape),
         elem_velocity,
         elem_energy.reshape(shape),
         elem_mat.reshape(shape),
+        tile_weight,
         size_y,
     )
-    weight = fetch(tile_weight)
+    weight = fetch(tile_weight, weight)
 
     first = swap(first, "gx", 1)
     second = swap(second, "gx", 2)
@@ -595,7 +610,7 @@
     edges = (
         swap(edges[0], "gx", 1),
         swap(edges[1], "gx", 2),
-        swap(edges[2], "gy", 1, wrap=False),
+        swap(edges[2], "gy", 1),
         swap(edges[3], "gy", 2),
     )
     fresh, press, speed = inner(mat_props, state, cell_state.shape[1])

time: 40.9 us -> 41.1 us (level)
  waiting for transfers between devices: 2.58 us -> 3.16 us
  starting transfers between devices: 17.2 us -> 16.7 us
    ppermute x12, waiting for transfers between devices: 2.58 us -> 3.16 us  [swap(): lax.ppermute(value, axis, [(i, partner(i, size, which)) for i in range(si...]
    pallas_call x1, Pallas kernels: 1.57 us -> 2.14 us  [payload(): pl.pallas_call(functools.partial(payload_kernel, size_y=size_y), name='pa...]
    ppermute x12, starting transfers between devices: 17.2 us -> 16.7 us  [swap(): lax.ppermute(value, axis, [(i, partner(i, size, which)) for i in range(si...]
    pallas_call x1, Pallas kernels: 2.2 us -> 1.75 us  [fetch(): pl.pallas_call(fetch_kernel, name='fetch', out_shape=pltpu.VMEM(value.sha...]
  transfers between devices with their start and end apart: 12 -> 12, of which waited for: 3 -> 4; matrix products, arithmetic and copies ran while one was open for 0% -> 0% of each run, Pallas kernels for 27% -> 26%
where the time goes in v5:
time: 41.1 us; the launch traced here: 40.9 us
  Pallas kernels  19.5 us (47%)
  starting transfers between devices  16.7 us (41%)
  waiting for transfers between devices  3.16 us (8%)
  between operations  1.46 us (4%)
    ppermute x12, starting transfers between devices, swap(): lax.ppermute(value, axis, [(i, partner(i, size, which)) for i in range(si...  16.7 us
    pallas_call x1, Pallas kernels, outer(): pl.pallas_call(functools.partial(outer_kernel, size_x=size_x, size_y=size...  3.42 us
    ppermute x12, waiting for transfers between devices, swap(): lax.ppermute(value, axis, [(i, partner(i, size, which)) for i in range(si...  3.16 us
    pallas_call x1, Pallas kernels, inner(): pl.pallas_call(inner_kernel, name='inner', out_shape=(pltpu.VMEM((count,...  3.16 us
    pallas_call x1, Pallas kernels, stage(): pl.pallas_call(stage_kernel, name='stage', out_shape=(pltpu.VMEM((columns...  3.03 us
    pallas_call x1, Pallas kernels, late(): pl.pallas_call(late_kernel, name='late', out_shape=(jax.ShapeDtypeStruct(...  2.7 us
    pallas_call x1, Pallas kernels, payload(): pl.pallas_call(functools.partial(payload_kernel, size_y=size_y), name='pa...  2.14 us
    pallas_call x1, Pallas kernels, deposit(): pl.pallas_call(functools.partial(deposit_kernel, size_y=size_y), name='de...  2.13 us
  transfers between devices with their start and end apart: 12, of which 4 were waited for; matrix products, arithmetic and copies ran while one was open for 0% of the time, Pallas kernels for 26%

profile of v5, /device:TPU:0, one launch (start us, length us, event | category | flops | bytes accessed | tf_op | source)
XLA Modules:
  0.0 40.9 jit_solution(12061005565179352245)
XLA Ops:
  0.6 2.1 %payload.1 = (bf16[6,16,128]{2,1,0:T(8,128)(2,1)S(1)}, bf16[6,16,128]{2,1,0:T(8,128)(2,1)S(1)}, bf16[6,16,128]{2,1,0:T(8,128)(2,1)S(1)}, s32[18]{0:T(128)S(1)}, bf16[128,128,128]{2,1,0:T(8,128)(2,1)S(1)}) custom-call(s32[18]{0:T(128)} %dest_hbm.1, f32[2,8]{1,0:T(2,128)} %props.3, f32[18,128]{1,0:T(8,128)} %bitcast.4, f32[3,2304]{1,0:T(4,128)} %velocity_hbm.1, ...), custom_call_target="tpu_custom_call" | custom-call | tf_op jit(solution)/shard_map/payload/pallas_call | solution.py:113
  2.8 2.5 %collective-permute-start = (bf16[6,16,128]{2,1,0:T(8,128)(2,1)S(1)}, bf16[6,16,128]{2,1,0:T(8,128)(2,1)S(1)}, u32[]{:S(2)}, u32[]{:S(2)}) collective-permute-start(bf16[6,16,128]{2,1,0:T(8,128)(2,1)S(1)} %get-tuple-element.29), channel_id=1, source_target_pairs={{0,24},{8,16},{16,8},{24,0},{1,25},{9,17},{17,9},{25,1},{2,26},{10... | collective-permute-start | bytes 73736 | tf_op jit(solution)/shard_map/ppermute | solution.py:41
  5.2 0.7 %collective-permute-start.1 = (bf16[6,16,128]{2,1,0:T(8,128)(2,1)S(1)}, bf16[6,16,128]{2,1,0:T(8,128)(2,1)S(1)}, u32[]{:S(2)}, u32[]{:S(2)}) collective-permute-start(bf16[6,16,128]{2,1,0:T(8,128)(2,1)S(1)} %get-tuple-element.30), channel_id=1, source_target_pairs={{0,8},{8,0},{16,24},{24,16},{1,9},{9,1},{17,25},{25,17},{2,10},{10... | collective-permute-start | bytes 73736 | tf_op jit(solution)/shard_map/ppermute | solution.py:41
  5.9 1.7 %fetch.1.weight = bf16[128,128,128]{2,1,0:T(8,128)(2,1)S(1)} custom-call(bf16[128,128,128]{2,1,0:T(8,128)(2,1)} %source.1, bf16[128,128,128]{2,1,0:T(8,128)(2,1)S(1)} %get-tuple-element.26.target_in), custom_call_target="tpu_custom_call", output_to_operand_aliasing={{}: (1, {})} | custom-call | bytes 8388608 | tf_op jit(solution)/shard_map/fetch/pallas_call | solution.py:189
  7.7 0.0 copy-start.1
  7.7 0.0 copy-start.2
  7.7 0.0 collective-permute-done.first
  7.7 0.0 collective-permute-done.1.second
  7.8 4.6 %collective-permute-start.2 = (bf16[6,16,128]{2,1,0:T(8,128)(2,1)S(1)}, bf16[6,16,128]{2,1,0:T(8,128)(2,1)S(1)}, u32[]{:S(2)}, u32[]{:S(2)}) collective-permute-start(bf16[6,16,128]{2,1,0:T(8,128)(2,1)S(1)} %pad_maximum_fusion), channel_id=1, source_target_pairs={{0,7},{1,2},{2,1},{3,4},{4,3},{5,6},{6,5},{7,0},{8,15},{9,10},{10,... | collective-permute-start | bytes 73736 | tf_op jit(solution)/shard_map/ppermute | solution.py:41
  12.4 0.0 collective-permute-start.3
  13.0 3.0 %stage.1 = (f32[18,12,80,128]{3,2,1,0:T(8,128)S(1)}, bf16[128,128,128]{2,1,0:T(8,128)(2,1)S(1)}) custom-call(f32[12,64,2048]{2,1,0:T(8,128)} %cell.1, bf16[128,128,128]{2,1,0:T(8,128)(2,1)S(1)} %fetch.1.weight), custom_call_target="tpu_custom_call" | custom-call | bytes 12582912 | tf_op jit(solution)/shard_map/stage/pallas_call | solution.py:165
  16.1 0.0 collective-permute-done.2.south
  16.1 0.1 collective-permute-done.3.north
  16.2 0.0 copy-done.1
  16.2 0.0 copy-done.2
  16.2 0.0 copy-start
  16.2 2.1 %deposit.1 = (f32[18,12,80,128]{3,2,1,0:T(8,128)S(1)}, bf16[192,128]{1,0:T(8,128)(2,1)S(1)}, bf16[192,128]{1,0:T(8,128)(2,1)S(1)}, bf16[384,128]{1,0:T(8,128)(2,1)S(1)}, bf16[384,128]{1,0:T(8,128)(2,1)S(1)}) custom-call(s32[128]{0:T(128)S(1)} %copy-done.1, s32[128]{0:T(128)S(1)} %copy-done.2, ...), custom_call_target="tpu_custom_call", output_to_operand_aliasing={{0}: (9, {})} | custom-call | tf_op jit(solution)/shard_map/deposit/pallas_call | solution.py:271
  18.3 2.8 %collective-permute-start.6 = (bf16[384,128]{1,0:T(8,128)(2,1)S(1)}, bf16[384,128]{1,0:T(8,128)(2,1)S(1)}, u32[]{:S(2)}, u32[]{:S(2)}) collective-permute-start(bf16[384,128]{1,0:T(8,128)(2,1)S(1)} %get-tuple-element.35), channel_id=1, source_target_pairs={{0,7},{1,2},{2,1},{3,4},{4,3},{5,6},{6,5},{7,0},{8,15},{9,10},{10,... | collective-permute-start | bytes 294920 | tf_op jit(solution)/shard_map/ppermute | solution.py:41
  21.1 0.0 collective-permute-start.7
  21.1 0.0 collective-permute-start.4
  21.1 1.7 %collective-permute-start.5 = (bf16[192,128]{1,0:T(8,128)(2,1)S(1)}, bf16[192,128]{1,0:T(8,128)(2,1)S(1)}, u32[]{:S(2)}, u32[]{:S(2)}) collective-permute-start(bf16[192,128]{1,0:T(8,128)(2,1)S(1)} %get-tuple-element.34), channel_id=1, source_target_pairs={{0,8},{8,0},{16,24},{24,16},{1,9},{9,1},{17,25},{25,17},{2,10},{10... | collective-permute-start | bytes 147464 | tf_op jit(solution)/shard_map/ppermute | solution.py:41
  22.8 0.0 copy-done
  22.8 3.2 %inner.1 = (f32[12,64,2048]{2,1,0:T(8,128)S(1)}, f32[16,64,128]{2,1,0:T(8,128)S(1)}, f32[18,3,80,128]{3,2,1,0:T(8,128)S(1)}) custom-call(f32[2,8]{1,0:T(2,128)S(1)} %copy-done, f32[18,12,80,128]{3,2,1,0:T(8,128)S(1)} %get-tuple-element.38.state.state_in), custom_call_target="tpu_custom_call" | custom-call | flops 44236800 | bytes 17694720 | tf_op jit(solution)/shard_map/inner/pallas_call | solution.py:405
  26.0 0.0 collective-permute-done.4.edge_x1
  26.0 0.0 collective-permute-done.5.edge_x2
  26.0 0.0 collective-permute-done.6.edge_y1
  26.0 0.8 %collective-permute-done.7.edge_y2 = bf16[384,128]{1,0:T(8,128)(2,1)S(1)} collective-permute-done((bf16[384,128]{1,0:T(8,128)(2,1)S(1)}, bf16[384,128]{1,0:T(8,128)(2,1)S(1)}, u32[]{:S(2)}, u32[]{:S(2)}) %collective-permute-start.7) | collective-permute-done | bytes 98336 | tf_op jit(solution)/shard_map/ppermute | solution.py:41
  26.8 3.4 %outer.1 = (f32[18,12,80,128]{3,2,1,0:T(8,128)S(1)}, f32[18,3,80,128]{3,2,1,0:T(8,128)S(1)}, f32[16,64,128]{2,1,0:T(8,128)S(1)}, f32[12,64,2048]{2,1,0:T(8,128)S...) custom-call(f32[2,8]{1,0:T(2,128)S(1)} %copy-done, ...), custom_call_target="tpu_custom_call", output_to_operand_aliasing={{0}: (9, {}), {1}: (10, {}), {2}: (11, {}), {3}: (12, {})} | custom-call | tf_op jit(solution)/shard_map/outer/pallas_call | solution.py:490
  30.2 2.7 %collective-permute-start.8 = (f32[6,128]{1,0:T(8,128)S(1)}, f32[6,128]{1,0:T(8,128)S(1)}, u32[]{:S(2)}, u32[]{:S(2)}) collective-permute-start(f32[6,128]{1,0:T(8,128)S(1)} %get-tuple-element.48), channel_id=1, source_target_pairs={{0,7},{1,2},{2,1},{3,4},{4,3},{5,6},{6,5},{7,0},{8,15},{9,10},{10,... | collective-permute-start | bytes 9224 | tf_op jit(solution)/shard_map/ppermute | solution.py:41
  32.9 0.0 collective-permute-start.9
  32.9 2.7 %late.1 = (f32[12,64,2048]{2,1,0:T(8,128)}, f32[12,64,2048]{2,1,0:T(8,128)S(1)}) custom-call(f32[18,12,80,128]{3,2,1,0:T(8,128)S(1)} %get-tuple-element.42.state, f32[18,3,80,128]{3,2,1,0:T(8,128)S(1)} %get-tuple-element.43.speed, f32[12,64,2048]{2,1,0:T(8,128)S(1)} %get-tuple-element.44.fresh_in), custom_call_target="tpu_custom_call", output_to_operand_aliasing={{1}: (2, {})} | custom-call | flops 11059200 | bytes 17694720 | tf_op jit(solution)/shard_map/late/pallas_call | solution.py:534
  35.6 1.0 %collective-permute-done.8 = f32[6,128]{1,0:T(8,128)S(1)} collective-permute-done((f32[6,128]{1,0:T(8,128)S(1)}, f32[6,128]{1,0:T(8,128)S(1)}, u32[]{:S(2)}, u32[]{:S(2)}) %collective-permute-start.8) | collective-permute-done | bytes 3104 | tf_op jit(solution)/shard_map/ppermute | solution.py:41
  36.6 0.0 collective-permute-done.9
  36.6 0.1 collective-permute-start.10
  36.7 1.7 %collective-permute-start.11 = (f32[6,128]{1,0:T(8,128)S(1)}, f32[6,128]{1,0:T(8,128)S(1)}, u32[]{:S(2)}, u32[]{:S(2)}) collective-permute-start(f32[6,128]{1,0:T(8,128)S(1)} %pad_maximum_fusion.4), channel_id=1, source_target_pairs={{0,8},{8,0},{16,24},{24,16},{1,9},{9,1},{17,25},{25,17},{2,10},{10... | collective-permute-start | bytes 9224 | tf_op jit(solution)/shard_map/ppermute | solution.py:41
  38.4 1.3 %collective-permute-done.10.first = f32[6,128]{1,0:T(8,128)S(1)} collective-permute-done((f32[6,128]{1,0:T(8,128)S(1)}, f32[6,128]{1,0:T(8,128)S(1)}, u32[]{:S(2)}, u32[]{:S(2)}) %collective-permute-start.10) | collective-permute-done | bytes 3104 | tf_op jit(solution)/shard_map/ppermute | solution.py:41
  39.7 0.0 collective-permute-done.11.second
  39.7 1.2 %pick.1 = bf16[18,128]{1,0:T(8,128)(2,1)} custom-call(s32[18]{0:T(128)S(1)} %get-tuple-element.46.place, f32[6,128]{1,0:T(8,128)S(1)} %pad_maximum_fusion.2.own, f32[6,128]{1,0:T(8,128)S(1)} %collective-permute-done.10.first, f32[6,128]{1,0:T(8,128)S(1)} %collective-permute-done.11.second), custom_call_target="tpu_custom_call" | custom-call | tf_op jit(solution)/shard_map/pick/pallas_call | solution.py:557
  (11 shorter events, 0.1 us)
Async XLA Ops:
  2.8 4.9 %collective-permute-start = (bf16[6,16,128]{2,1,0:T(8,128)(2,1)S(1)}, bf16[6,16,128]{2,1,0:T(8,128)(2,1)S(1)}, u32[]{:S(2)}, u32[]{:S(2)}) collective-permute-start(bf16[6,16,128]{2,1,0:T(8,128)(2,1)S(1)} %get-tuple-element.29), channel_id=1, source_target_pairs={{0,24},{8,16},{16,8},{24,0},{1,25},{9,17},{17,9},{25,1},{2,26},{10... | collective-permute-start | bytes 73736 | tf_op jit(solution)/shard_map/ppermute | solution.py:41
  5.2 2.5 %collective-permute-start.1 = (bf16[6,16,128]{2,1,0:T(8,128)(2,1)S(1)}, bf16[6,16,128]{2,1,0:T(8,128)(2,1)S(1)}, u32[]{:S(2)}, u32[]{:S(2)}) collective-permute-start(bf16[6,16,128]{2,1,0:T(8,128)(2,1)S(1)} %get-tuple-element.30), channel_id=1, source_target_pairs={{0,8},{8,0},{16,24},{24,16},{1,9},{9,1},{17,25},{25,17},{2,10},{10... | collective-permute-start | bytes 73736 | tf_op jit(solution)/shard_map/ppermute | solution.py:41
  7.7 8.5 %copy-start.1 = (s32[128]{0:T(128)S(1)}, s32[128]{0:T(128)}, u32[]{:S(2)}) copy-start(s32[128]{0:T(128)} %tile_slot.3) | copy-start | bytes 1540
  7.7 8.5 %copy-start.2 = (s32[128]{0:T(128)S(1)}, s32[128]{0:T(128)}, u32[]{:S(2)}) copy-start(s32[128]{0:T(128)} %tile_cell.3) | copy-start | bytes 1540
  7.8 8.3 %collective-permute-start.2 = (bf16[6,16,128]{2,1,0:T(8,128)(2,1)S(1)}, bf16[6,16,128]{2,1,0:T(8,128)(2,1)S(1)}, u32[]{:S(2)}, u32[]{:S(2)}) collective-permute-start(bf16[6,16,128]{2,1,0:T(8,128)(2,1)S(1)} %pad_maximum_fusion), channel_id=1, source_target_pairs={{0,7},{1,2},{2,1},{3,4},{4,3},{5,6},{6,5},{7,0},{8,15},{9,10},{10,... | collective-permute-start | bytes 73736 | tf_op jit(solution)/shard_map/ppermute | solution.py:41
  12.4 3.8 %collective-permute-start.3 = (bf16[6,16,128]{2,1,0:T(8,128)(2,1)S(1)}, bf16[6,16,128]{2,1,0:T(8,128)(2,1)S(1)}, u32[]{:S(2)}, u32[]{:S(2)}) collective-permute-start(bf16[6,16,128]{2,1,0:T(8,128)(2,1)S(1)} %pad_maximum_fusion.1), channel_id=1, source_target_pairs={{0,1},{1,0},{2,3},{3,2},{4,5},{5,4},{6,7},{7,6},{8,9},{9,8},{10,11... | collective-permute-start | bytes 73736 | tf_op jit(solution)/shard_map/ppermute | solution.py:41
  16.2 6.6 %copy-start = (f32[2,8]{1,0:T(2,128)S(1)}, f32[2,8]{1,0:T(2,128)}, u32[]{:S(2)}) copy-start(f32[2,8]{1,0:T(2,128)} %props.3) | copy-start | bytes 196
  18.3 7.7 %collective-permute-start.6 = (bf16[384,128]{1,0:T(8,128)(2,1)S(1)}, bf16[384,128]{1,0:T(8,128)(2,1)S(1)}, u32[]{:S(2)}, u32[]{:S(2)}) collective-permute-start(bf16[384,128]{1,0:T(8,128)(2,1)S(1)} %get-tuple-element.35), channel_id=1, source_target_pairs={{0,7},{1,2},{2,1},{3,4},{4,3},{5,6},{6,5},{7,0},{8,15},{9,10},{10,... | collective-permute-start | bytes 294920 | tf_op jit(solution)/shard_map/ppermute | solution.py:41
  21.1 5.7 %collective-permute-start.7 = (bf16[384,128]{1,0:T(8,128)(2,1)S(1)}, bf16[384,128]{1,0:T(8,128)(2,1)S(1)}, u32[]{:S(2)}, u32[]{:S(2)}) collective-permute-start(bf16[384,128]{1,0:T(8,128)(2,1)S(1)} %get-tuple-element.36), channel_id=1, source_target_pairs={{0,1},{1,0},{2,3},{3,2},{4,5},{5,4},{6,7},{7,6},{8,9},{9,8},{10,11... | collective-permute-start | bytes 294920 | tf_op jit(solution)/shard_map/ppermute | solution.py:41
  21.1 4.8 %collective-permute-start.4 = (bf16[192,128]{1,0:T(8,128)(2,1)S(1)}, bf16[192,128]{1,0:T(8,128)(2,1)S(1)}, u32[]{:S(2)}, u32[]{:S(2)}) collective-permute-start(bf16[192,128]{1,0:T(8,128)(2,1)S(1)} %get-tuple-element.33), channel_id=1, source_target_pairs={{0,24},{8,16},{16,8},{24,0},{1,25},{9,17},{17,9},{25,1},{2,26},{10... | collective-permute-start | bytes 147464 | tf_op jit(solution)/shard_map/ppermute | solution.py:41
  21.1 4.9 %collective-permute-start.5 = (bf16[192,128]{1,0:T(8,128)(2,1)S(1)}, bf16[192,128]{1,0:T(8,128)(2,1)S(1)}, u32[]{:S(2)}, u32[]{:S(2)}) collective-permute-start(bf16[192,128]{1,0:T(8,128)(2,1)S(1)} %get-tuple-element.34), channel_id=1, source_target_pairs={{0,8},{8,0},{16,24},{24,16},{1,9},{9,1},{17,25},{25,17},{2,10},{10... | collective-permute-start | bytes 147464 | tf_op jit(solution)/shard_map/ppermute | solution.py:41
  30.2 6.4 %collective-permute-start.8 = (f32[6,128]{1,0:T(8,128)S(1)}, f32[6,128]{1,0:T(8,128)S(1)}, u32[]{:S(2)}, u32[]{:S(2)}) collective-permute-start(f32[6,128]{1,0:T(8,128)S(1)} %get-tuple-element.48), channel_id=1, source_target_pairs={{0,7},{1,2},{2,1},{3,4},{4,3},{5,6},{6,5},{7,0},{8,15},{9,10},{10,... | collective-permute-start | bytes 9224 | tf_op jit(solution)/shard_map/ppermute | solution.py:41
  32.9 3.7 %collective-permute-start.9 = (f32[6,128]{1,0:T(8,128)S(1)}, f32[6,128]{1,0:T(8,128)S(1)}, u32[]{:S(2)}, u32[]{:S(2)}) collective-permute-start(f32[6,128]{1,0:T(8,128)S(1)} %get-tuple-element.49), channel_id=1, source_target_pairs={{0,1},{1,0},{2,3},{3,2},{4,5},{5,4},{6,7},{7,6},{8,9},{9,8},{10,11... | collective-permute-start | bytes 9224 | tf_op jit(solution)/shard_map/ppermute | solution.py:41
  36.6 3.1 %collective-permute-start.10 = (f32[6,128]{1,0:T(8,128)S(1)}, f32[6,128]{1,0:T(8,128)S(1)}, u32[]{:S(2)}, u32[]{:S(2)}) collective-permute-start(f32[6,128]{1,0:T(8,128)S(1)} %pad_maximum_fusion.3), channel_id=1, source_target_pairs={{0,24},{8,16},{16,8},{24,0},{1,25},{9,17},{17,9},{25,1},{2,26},{10... | collective-permute-start | bytes 9224 | tf_op jit(solution)/shard_map/ppermute | solution.py:41
  36.7 3.0 %collective-permute-start.11 = (f32[6,128]{1,0:T(8,128)S(1)}, f32[6,128]{1,0:T(8,128)S(1)}, u32[]{:S(2)}, u32[]{:S(2)}) collective-permute-start(f32[6,128]{1,0:T(8,128)S(1)} %pad_maximum_fusion.4), channel_id=1, source_target_pairs={{0,8},{8,0},{16,24},{24,16},{1,9},{9,1},{17,25},{25,17},{2,10},{10... | collective-permute-start | bytes 9224 | tf_op jit(solution)/shard_map/ppermute | solution.py:41

commit v6 on v4

--- a/solution.py
+++ b/solution.py
@@ -63,12 +63,13 @@
 
 
 def payload_kernel(
-    dest_hbm, props_hbm, volume_hbm, velocity_hbm, energy_hbm, mat_hbm, own, first, second, place,
-    dest, props, volume, velocity, energy, mat, seen, packed, sem, *, size_y
+    dest_hbm, props_hbm, volume_hbm, velocity_hbm, energy_hbm, mat_hbm, slot_hbm, cell_hbm,
+    own, first, second, place, props, slot_out, cell_out, dest, volume, velocity, energy, mat, seen, packed, sem, *, size_y
 ):
     moves = (
         (dest_hbm, dest), (props_hbm, props), (mat_hbm, mat),
         (volume_hbm, volume), (velocity_hbm, velocity), (energy_hbm, energy),
+        (slot_hbm, slot_out), (cell_hbm, cell_out),
     )
     copies = [pltpu.make_async_copy(src, dst, sem.at[k]) for k, (src, dst) in enumerate(moves)]
     for copy in copies:
@@ -102,28 +103,35 @@
             out[s] = packed[k * 3 * CAP + s]
 
 
-def payload(dest, props, volume, velocity, energy, mat, size_y):
+def payload(dest, props, volume, velocity, energy, mat, tile_slot, tile_cell, size_y):
     n_blocks = volume.shape[0]
     parcel = pltpu.VMEM((3 * CAP, ROWS, BLK), BF16)
     return pl.pallas_call(
         functools.partial(payload_kernel, size_y=size_y),
         name="payload",
-        out_shape=(parcel, parcel, parcel, jax.ShapeDtypeStruct((n_blocks,), jnp.int32)),
-        in_specs=[ANY] * 6,
-        out_specs=(VMEM, VMEM, VMEM, SMEM),
+        out_shape=(
+            parcel,
+            parcel,
+            parcel,
+            pltpu.SMEM((n_blocks,), jnp.int32),
+            pltpu.SMEM(props.shape, F32),
+            pltpu.SMEM(tile_slot.shape, jnp.int32),
+            pltpu.SMEM(tile_cell.shape, jnp.int32),
+        ),
+        in_specs=[ANY] * 8,
+        out_specs=(VMEM, VMEM, VMEM, SMEM, SMEM, SMEM, SMEM),
         scratch_shapes=[
             pltpu.SMEM(dest.shape, jnp.int32),
-            pltpu.SMEM(props.shape, F32),
             pltpu.VMEM(volume.shape, F32),
             pltpu.VMEM(velocity.shape, F32),
             pltpu.VMEM(energy.shape, F32),
             pltpu.VMEM(mat.shape, jnp.int32),
             pltpu.SMEM((9,), jnp.int32),
             pltpu.VMEM((9 * CAP, ROWS, BLK), BF16),
-            pltpu.SemaphoreType.DMA((6,)),
+            pltpu.SemaphoreType.DMA((8,)),
         ],
         compiler_params=pltpu.CompilerParams(vmem_limit_bytes=4 * MIB),
-    )(*(in_hbm(value) for value in (dest, props, volume, velocity, energy, mat)))
+    )(*(in_hbm(value) for value in (dest, props, volume, velocity, energy, mat, tile_slot, tile_cell)))
 
 
 def stage_kernel(cell, weight, state, turned, sem):
@@ -567,13 +575,15 @@
     size_x, size_y = lax.axis_size("gx"), lax.axis_size("gy")
     n_blocks = elem_dest.shape[0]
     shape = (n_blocks, BLK)
-    own, first, second, place = payload(
+    own, first, second, place, mat_props, tile_slot, tile_cell = payload(
         elem_dest,
         mat_props,
         elem_volume.reshape(shape),
         elem_velocity,
         elem_energy.reshape(shape),
         elem_mat.reshape(shape),
+        tile_slot,
+        tile_cell,
         size_y,
     )
     weight = fetch(tile_weight)

time: 40.9 us -> 38.5 us (0.941)
  Pallas kernels: 19.4 us -> 17 us
  starting transfers between devices: 17.2 us -> 17.7 us
  waiting for transfers between devices: 2.58 us -> 2.1 us
    pallas_call x1, Pallas kernels: 1.16 us -> 0.62 us  [pick(): pl.pallas_call(pick_kernel, name='pick', out_shape=jax.ShapeDtypeStruct((...]
    pallas_call x1, Pallas kernels: 1.57 us -> 1.04 us  [payload(): pl.pallas_call(functools.partial(payload_kernel, size_y=size_y), name='pa...]
    pallas_call x1, Pallas kernels: 2.13 us -> 1.61 us  [deposit(): pl.pallas_call(functools.partial(deposit_kernel, size_y=size_y), name='de...]
    ppermute x12, starting transfers between devices: 17.2 us -> 17.7 us  [swap(): return lax.ppermute(value, axis, pairs)]
    ppermute x12, waiting for transfers between devices: 2.58 us -> 2.1 us  [swap(): return lax.ppermute(value, axis, pairs)]
    pallas_call x1, Pallas kernels: 3.43 us -> 2.99 us  [outer(): pl.pallas_call(functools.partial(outer_kernel, size_x=size_x, size_y=size...]
  transfers between devices with their start and end apart: 12 -> 12, of which waited for: 3 -> 3; matrix products, arithmetic and copies ran while one was open for 0% -> 0% of each run, Pallas kernels for 27% -> 28%
where the time goes in v6:
time: 38.5 us; the launch traced here: 38.3 us
  starting transfers between devices  17.7 us (46%)
  Pallas kernels  17 us (44%)
  waiting for transfers between devices  2.1 us (5%)
  between operations  1.46 us (4%)
    ppermute x12, starting transfers between devices, swap(): return lax.ppermute(value, axis, pairs)  17.7 us
    pallas_call x1, Pallas kernels, stage(): pl.pallas_call(stage_kernel, name='stage', out_shape=(pltpu.VMEM((columns...  3.03 us
    pallas_call x1, Pallas kernels, outer(): pl.pallas_call(functools.partial(outer_kernel, size_x=size_x, size_y=size...  2.99 us
    pallas_call x1, Pallas kernels, inner(): pl.pallas_call(inner_kernel, name='inner', out_shape=(pltpu.VMEM((count,...  2.77 us
    pallas_call x1, Pallas kernels, late(): pl.pallas_call(late_kernel, name='late', out_shape=(jax.ShapeDtypeStruct(...  2.7 us
    pallas_call x1, Pallas kernels, fetch(): pl.pallas_call(fetch_kernel, name='fetch', out_shape=pltpu.VMEM(value.sha...  2.2 us
    ppermute x12, waiting for transfers between devices, swap(): return lax.ppermute(value, axis, pairs)  2.1 us
    pallas_call x1, Pallas kernels, deposit(): pl.pallas_call(functools.partial(deposit_kernel, size_y=size_y), name='de...  1.61 us
  transfers between devices with their start and end apart: 12, of which 3 were waited for; matrix products, arithmetic and copies ran while one was open for 0% of the time, Pallas kernels for 28%

profile of v6, /device:TPU:0, one launch (start us, length us, event | category | flops | bytes accessed | tf_op | source)
XLA Modules:
  0.0 38.3 jit_solution(9887616487929374886)
XLA Ops:
  0.6 1.0 %payload.1 = (bf16[6,16,128]{2,1,0:T(8,128)(2,1)S(1)}, bf16[6,16,128]{2,1,0:T(8,128)(2,1)S(1)}, bf16[6,16,128]{2,1,0:T(8,128)(2,1)S(1)}, s32[18]{0:T(128)S(4)}, ...) custom-call(s32[18]{0:T(128)} %dest_hbm.1, f32[2,8]{1,0:T(2,128)} %props_hbm.1, f32[18,128]{1,0:T(8,128)} %bitcast.4, ...), custom_call_target="tpu_custom_call" | custom-call | tf_op jit(solution)/shard_map/payload/pallas_call | solution.py:109
  1.7 2.5 %collective-permute-start = (bf16[6,16,128]{2,1,0:T(8,128)(2,1)S(1)}, bf16[6,16,128]{2,1,0:T(8,128)(2,1)S(1)}, u32[]{:S(2)}, u32[]{:S(2)}) collective-permute-start(bf16[6,16,128]{2,1,0:T(8,128)(2,1)S(1)} %get-tuple-element.33), channel_id=1, source_target_pairs={{0,24},{8,16},{16,8},{24,0},{1,25},{9,17},{17,9},{25,1},{2,26},{10... | collective-permute-start | bytes 73736 | tf_op jit(solution)/shard_map/ppermute | solution.py:44
  4.2 0.7 %collective-permute-start.1 = (bf16[6,16,128]{2,1,0:T(8,128)(2,1)S(1)}, bf16[6,16,128]{2,1,0:T(8,128)(2,1)S(1)}, u32[]{:S(2)}, u32[]{:S(2)}) collective-permute-start(bf16[6,16,128]{2,1,0:T(8,128)(2,1)S(1)} %get-tuple-element.34), channel_id=1, source_target_pairs={{0,8},{8,0},{16,24},{24,16},{1,9},{9,1},{17,25},{25,17},{2,10},{10... | collective-permute-start | bytes 73736 | tf_op jit(solution)/shard_map/ppermute | solution.py:44
  4.8 2.2 %fetch.1.weight = bf16[128,128,128]{2,1,0:T(8,128)(2,1)S(1)} custom-call(bf16[128,128,128]{2,1,0:T(8,128)(2,1)} %source.1), custom_call_target="tpu_custom_call" | custom-call | bytes 8388608 | tf_op jit(solution)/shard_map/fetch/pallas_call | solution.py:184
  7.0 0.0 collective-permute-done.first
  7.1 0.0 collective-permute-done.1.second
  7.1 4.6 %collective-permute-start.2 = (bf16[6,16,128]{2,1,0:T(8,128)(2,1)S(1)}, bf16[6,16,128]{2,1,0:T(8,128)(2,1)S(1)}, u32[]{:S(2)}, u32[]{:S(2)}) collective-permute-start(bf16[6,16,128]{2,1,0:T(8,128)(2,1)S(1)} %pad_maximum_fusion), channel_id=1, source_target_pairs={{0,7},{1,2},{2,1},{3,4},{4,3},{5,6},{6,5},{7,0},{8,15},{9,10},{10,... | collective-permute-start | bytes 73736 | tf_op jit(solution)/shard_map/ppermute | solution.py:44
  11.7 0.0 collective-permute-start.3
  12.4 3.0 %stage.1 = (f32[18,12,80,128]{3,2,1,0:T(8,128)S(1)}, bf16[128,128,128]{2,1,0:T(8,128)(2,1)S(1)}) custom-call(f32[12,64,2048]{2,1,0:T(8,128)} %cell.1, bf16[128,128,128]{2,1,0:T(8,128)(2,1)S(1)} %fetch.1.weight), custom_call_target="tpu_custom_call" | custom-call | bytes 12582912 | tf_op jit(solution)/shard_map/stage/pallas_call | solution.py:162
  15.4 0.0 collective-permute-done.2.south
  15.4 0.1 collective-permute-done.3.north
  15.5 1.6 %deposit.1 = (f32[18,12,80,128]{3,2,1,0:T(8,128)S(1)}, bf16[192,128]{1,0:T(8,128)(2,1)S(1)}, bf16[192,128]{1,0:T(8,128)(2,1)S(1)}, bf16[384,128]{1,0:T(8,128)(2,1)S(1)}, bf16[384,128]{1,0:T(8,128)(2,1)S(1)}) custom-call(s32[128]{0:T(128)S(4)} %get-tuple-element.29.tile_slot, s32[128]{0:T(128)S(4)} %get-tuple-element.30.tile_cell, ...), custom_call_target="tpu_custom_call", output_to_operand_aliasing={{0}: (9, {})} | custom-call | tf_op jit(solution)/shard_map/deposit/pallas_call | solution.py:265
  17.2 0.7 %collective-permute-start.6 = (bf16[384,128]{1,0:T(8,128)(2,1)S(1)}, bf16[384,128]{1,0:T(8,128)(2,1)S(1)}, u32[]{:S(2)}, u32[]{:S(2)}) collective-permute-start(bf16[384,128]{1,0:T(8,128)(2,1)S(1)} %get-tuple-element.39), channel_id=1, source_target_pairs={{0,0},{1,2},{2,1},{3,4},{4,3},{5,6},{6,5},{7,7},{8,8},{9,10},{10,9... | collective-permute-start | bytes 294920 | tf_op jit(solution)/shard_map/ppermute | solution.py:44
  17.8 3.2 %collective-permute-start.7 = (bf16[384,128]{1,0:T(8,128)(2,1)S(1)}, bf16[384,128]{1,0:T(8,128)(2,1)S(1)}, u32[]{:S(2)}, u32[]{:S(2)}) collective-permute-start(bf16[384,128]{1,0:T(8,128)(2,1)S(1)} %get-tuple-element.40), channel_id=1, source_target_pairs={{0,1},{1,0},{2,3},{3,2},{4,5},{5,4},{6,7},{7,6},{8,9},{9,8},{10,11... | collective-permute-start | bytes 294920 | tf_op jit(solution)/shard_map/ppermute | solution.py:44
  21.1 0.0 collective-permute-start.4
  21.1 1.2 %collective-permute-start.5 = (bf16[192,128]{1,0:T(8,128)(2,1)S(1)}, bf16[192,128]{1,0:T(8,128)(2,1)S(1)}, u32[]{:S(2)}, u32[]{:S(2)}) collective-permute-start(bf16[192,128]{1,0:T(8,128)(2,1)S(1)} %get-tuple-element.38), channel_id=1, source_target_pairs={{0,8},{8,0},{16,24},{24,16},{1,9},{9,1},{17,25},{25,17},{2,10},{10... | collective-permute-start | bytes 147464 | tf_op jit(solution)/shard_map/ppermute | solution.py:44
  22.3 2.8 %inner.1 = (f32[12,64,2048]{2,1,0:T(8,128)S(1)}, f32[16,64,128]{2,1,0:T(8,128)S(1)}, f32[18,3,80,128]{3,2,1,0:T(8,128)S(1)}) custom-call(f32[2,8]{1,0:T(2,128)S(4)} %get-tuple-element.28.props, f32[18,12,80,128]{3,2,1,0:T(8,128)S(1)} %get-tuple-element.42.state.state_in), custom_call_target="tpu_custom_call" | custom-call | flops 44236800 | bytes 17694720 | tf_op jit(solution)/shard_map/inner/pallas_call | solution.py:399
  25.1 0.0 collective-permute-done.4.edge_x1
  25.1 0.0 collective-permute-done.5.edge_x2
  25.1 0.0 collective-permute-done.6.edge_y1
  25.1 0.0 collective-permute-done.7.edge_y2
  25.1 3.0 %outer.1 = (f32[18,12,80,128]{3,2,1,0:T(8,128)S(1)}, f32[18,3,80,128]{3,2,1,0:T(8,128)S(1)}, f32[16,64,128]{2,1,0:T(8,128)S(1)}, f32[12,64,2048]{2,1,0:T(8,128)S...) custom-call(f32[2,8]{1,0:T(2,128)S(4)} %get-tuple-element.28.props, ...), custom_call_target="tpu_custom_call", output_to_operand_aliasing={{0}: (9, {}), {1}: (10, {}), {2}: (11, {}), {3}: (12, {})} | custom-call | tf_op jit(solution)/shard_map/outer/pallas_call | solution.py:484
  28.1 1.9 %collective-permute-start.8 = (f32[6,128]{1,0:T(8,128)S(1)}, f32[6,128]{1,0:T(8,128)S(1)}, u32[]{:S(2)}, u32[]{:S(2)}) collective-permute-start(f32[6,128]{1,0:T(8,128)S(1)} %get-tuple-element.52), channel_id=1, source_target_pairs={{0,7},{1,2},{2,1},{3,4},{4,3},{5,6},{6,5},{7,0},{8,15},{9,10},{10,... | collective-permute-start | bytes 9224 | tf_op jit(solution)/shard_map/ppermute | solution.py:44
  30.0 1.7 %collective-permute-start.9 = (f32[6,128]{1,0:T(8,128)S(1)}, f32[6,128]{1,0:T(8,128)S(1)}, u32[]{:S(2)}, u32[]{:S(2)}) collective-permute-start(f32[6,128]{1,0:T(8,128)S(1)} %get-tuple-element.53), channel_id=1, source_target_pairs={{0,1},{1,0},{2,3},{3,2},{4,5},{5,4},{6,7},{7,6},{8,9},{9,8},{10,11... | collective-permute-start | bytes 9224 | tf_op jit(solution)/shard_map/ppermute | solution.py:44
  31.6 2.7 %late.1 = (f32[12,64,2048]{2,1,0:T(8,128)}, f32[12,64,2048]{2,1,0:T(8,128)S(1)}) custom-call(f32[18,12,80,128]{3,2,1,0:T(8,128)S(1)} %get-tuple-element.46.state, f32[18,3,80,128]{3,2,1,0:T(8,128)S(1)} %get-tuple-element.47.speed, f32[12,64,2048]{2,1,0:T(8,128)S(1)} %get-tuple-element.48.fresh_in), custom_call_target="tpu_custom_call", output_to_operand_aliasing={{1}: (2, {})} | custom-call | flops 11059200 | bytes 17694720 | tf_op jit(solution)/shard_map/late/pallas_call | solution.py:528
  34.4 0.1 collective-permute-done.8
  34.5 0.0 collective-permute-done.9
  34.5 0.1 collective-permute-start.10
  34.6 1.2 %collective-permute-start.11 = (f32[6,128]{1,0:T(8,128)S(1)}, f32[6,128]{1,0:T(8,128)S(1)}, u32[]{:S(2)}, u32[]{:S(2)}) collective-permute-start(f32[6,128]{1,0:T(8,128)S(1)} %pad_maximum_fusion.4), channel_id=1, source_target_pairs={{0,8},{8,0},{16,24},{24,16},{1,9},{9,1},{17,25},{25,17},{2,10},{10... | collective-permute-start | bytes 9224 | tf_op jit(solution)/shard_map/ppermute | solution.py:44
  35.8 1.8 %collective-permute-done.10.first = f32[6,128]{1,0:T(8,128)S(1)} collective-permute-done((f32[6,128]{1,0:T(8,128)S(1)}, f32[6,128]{1,0:T(8,128)S(1)}, u32[]{:S(2)}, u32[]{:S(2)}) %collective-permute-start.10) | collective-permute-done | bytes 3104 | tf_op jit(solution)/shard_map/ppermute | solution.py:44
  37.6 0.0 collective-permute-done.11.second
  37.6 0.6 %pick.1 = bf16[18,128]{1,0:T(8,128)(2,1)} custom-call(s32[18]{0:T(128)S(4)} %get-tuple-element.50.place, f32[6,128]{1,0:T(8,128)S(1)} %pad_maximum_fusion.2.own, f32[6,128]{1,0:T(8,128)S(1)} %collective-permute-done.10.first, f32[6,128]{1,0:T(8,128)S(1)} %collective-permute-done.11.second), custom_call_target="tpu_custom_call" | custom-call | tf_op jit(solution)/shard_map/pick/pallas_call | solution.py:551
  (11 shorter events, 0.1 us)
Async XLA Ops:
  1.7 5.4 %collective-permute-start = (bf16[6,16,128]{2,1,0:T(8,128)(2,1)S(1)}, bf16[6,16,128]{2,1,0:T(8,128)(2,1)S(1)}, u32[]{:S(2)}, u32[]{:S(2)}) collective-permute-start(bf16[6,16,128]{2,1,0:T(8,128)(2,1)S(1)} %get-tuple-element.33), channel_id=1, source_target_pairs={{0,24},{8,16},{16,8},{24,0},{1,25},{9,17},{17,9},{25,1},{2,26},{10... | collective-permute-start | bytes 73736 | tf_op jit(solution)/shard_map/ppermute | solution.py:44
  4.2 2.9 %collective-permute-start.1 = (bf16[6,16,128]{2,1,0:T(8,128)(2,1)S(1)}, bf16[6,16,128]{2,1,0:T(8,128)(2,1)S(1)}, u32[]{:S(2)}, u32[]{:S(2)}) collective-permute-start(bf16[6,16,128]{2,1,0:T(8,128)(2,1)S(1)} %get-tuple-element.34), channel_id=1, source_target_pairs={{0,8},{8,0},{16,24},{24,16},{1,9},{9,1},{17,25},{25,17},{2,10},{10... | collective-permute-start | bytes 73736 | tf_op jit(solution)/shard_map/ppermute | solution.py:44
  7.1 8.3 %collective-permute-start.2 = (bf16[6,16,128]{2,1,0:T(8,128)(2,1)S(1)}, bf16[6,16,128]{2,1,0:T(8,128)(2,1)S(1)}, u32[]{:S(2)}, u32[]{:S(2)}) collective-permute-start(bf16[6,16,128]{2,1,0:T(8,128)(2,1)S(1)} %pad_maximum_fusion), channel_id=1, source_target_pairs={{0,7},{1,2},{2,1},{3,4},{4,3},{5,6},{6,5},{7,0},{8,15},{9,10},{10,... | collective-permute-start | bytes 73736 | tf_op jit(solution)/shard_map/ppermute | solution.py:44
  11.7 3.8 %collective-permute-start.3 = (bf16[6,16,128]{2,1,0:T(8,128)(2,1)S(1)}, bf16[6,16,128]{2,1,0:T(8,128)(2,1)S(1)}, u32[]{:S(2)}, u32[]{:S(2)}) collective-permute-start(bf16[6,16,128]{2,1,0:T(8,128)(2,1)S(1)} %pad_maximum_fusion.1), channel_id=1, source_target_pairs={{0,1},{1,0},{2,3},{3,2},{4,5},{5,4},{6,7},{7,6},{8,9},{9,8},{10,11... | collective-permute-start | bytes 73736 | tf_op jit(solution)/shard_map/ppermute | solution.py:44
  17.2 8.0 %collective-permute-start.6 = (bf16[384,128]{1,0:T(8,128)(2,1)S(1)}, bf16[384,128]{1,0:T(8,128)(2,1)S(1)}, u32[]{:S(2)}, u32[]{:S(2)}) collective-permute-start(bf16[384,128]{1,0:T(8,128)(2,1)S(1)} %get-tuple-element.39), channel_id=1, source_target_pairs={{0,0},{1,2},{2,1},{3,4},{4,3},{5,6},{6,5},{7,7},{8,8},{9,10},{10,9... | collective-permute-start | bytes 294920 | tf_op jit(solution)/shard_map/ppermute | solution.py:44
  17.8 7.3 %collective-permute-start.7 = (bf16[384,128]{1,0:T(8,128)(2,1)S(1)}, bf16[384,128]{1,0:T(8,128)(2,1)S(1)}, u32[]{:S(2)}, u32[]{:S(2)}) collective-permute-start(bf16[384,128]{1,0:T(8,128)(2,1)S(1)} %get-tuple-element.40), channel_id=1, source_target_pairs={{0,1},{1,0},{2,3},{3,2},{4,5},{5,4},{6,7},{7,6},{8,9},{9,8},{10,11... | collective-permute-start | bytes 294920 | tf_op jit(solution)/shard_map/ppermute | solution.py:44
  21.1 4.0 %collective-permute-start.4 = (bf16[192,128]{1,0:T(8,128)(2,1)S(1)}, bf16[192,128]{1,0:T(8,128)(2,1)S(1)}, u32[]{:S(2)}, u32[]{:S(2)}) collective-permute-start(bf16[192,128]{1,0:T(8,128)(2,1)S(1)} %get-tuple-element.37), channel_id=1, source_target_pairs={{0,24},{8,16},{16,8},{24,0},{1,25},{9,17},{17,9},{25,1},{2,26},{10... | collective-permute-start | bytes 147464 | tf_op jit(solution)/shard_map/ppermute | solution.py:44
  21.1 4.0 %collective-permute-start.5 = (bf16[192,128]{1,0:T(8,128)(2,1)S(1)}, bf16[192,128]{1,0:T(8,128)(2,1)S(1)}, u32[]{:S(2)}, u32[]{:S(2)}) collective-permute-start(bf16[192,128]{1,0:T(8,128)(2,1)S(1)} %get-tuple-element.38), channel_id=1, source_target_pairs={{0,8},{8,0},{16,24},{24,16},{1,9},{9,1},{17,25},{25,17},{2,10},{10... | collective-permute-start | bytes 147464 | tf_op jit(solution)/shard_map/ppermute | solution.py:44
  28.1 6.4 %collective-permute-start.8 = (f32[6,128]{1,0:T(8,128)S(1)}, f32[6,128]{1,0:T(8,128)S(1)}, u32[]{:S(2)}, u32[]{:S(2)}) collective-permute-start(f32[6,128]{1,0:T(8,128)S(1)} %get-tuple-element.52), channel_id=1, source_target_pairs={{0,7},{1,2},{2,1},{3,4},{4,3},{5,6},{6,5},{7,0},{8,15},{9,10},{10,... | collective-permute-start | bytes 9224 | tf_op jit(solution)/shard_map/ppermute | solution.py:44
  30.0 4.5 %collective-permute-start.9 = (f32[6,128]{1,0:T(8,128)S(1)}, f32[6,128]{1,0:T(8,128)S(1)}, u32[]{:S(2)}, u32[]{:S(2)}) collective-permute-start(f32[6,128]{1,0:T(8,128)S(1)} %get-tuple-element.53), channel_id=1, source_target_pairs={{0,1},{1,0},{2,3},{3,2},{4,5},{5,4},{6,7},{7,6},{8,9},{9,8},{10,11... | collective-permute-start | bytes 9224 | tf_op jit(solution)/shard_map/ppermute | solution.py:44
  34.5 3.1 %collective-permute-start.10 = (f32[6,128]{1,0:T(8,128)S(1)}, f32[6,128]{1,0:T(8,128)S(1)}, u32[]{:S(2)}, u32[]{:S(2)}) collective-permute-start(f32[6,128]{1,0:T(8,128)S(1)} %pad_maximum_fusion.3), channel_id=1, source_target_pairs={{0,24},{8,16},{16,8},{24,0},{1,25},{9,17},{17,9},{25,1},{2,26},{10... | collective-permute-start | bytes 9224 | tf_op jit(solution)/shard_map/ppermute | solution.py:44
  34.6 3.0 %collective-permute-start.11 = (f32[6,128]{1,0:T(8,128)S(1)}, f32[6,128]{1,0:T(8,128)S(1)}, u32[]{:S(2)}, u32[]{:S(2)}) collective-permute-start(f32[6,128]{1,0:T(8,128)S(1)} %pad_maximum_fusion.4), channel_id=1, source_target_pairs={{0,8},{8,0},{16,24},{24,16},{1,9},{9,1},{17,25},{25,17},{2,10},{10... | collective-permute-start | bytes 9224 | tf_op jit(solution)/shard_map/ppermute | solution.py:44

commit v7 on v6

--- a/solution.py
+++ b/solution.py
@@ -13,9 +13,12 @@
 CAP = 2
 HALF = BLK // 2
 PAD = 8
+AFTER = 16
+ROOM = PAD + AFTER
 ROWS = 16
-UNROLL = 128
 PAIR = 2
+TOGETHER = 4
+PARTS = 4
 TURN = 16
 GROUP = 8
 DELAY = 4
@@ -134,9 +137,12 @@
     )(*(in_hbm(value) for value in (dest, props, volume, velocity, energy, mat, tile_slot, tile_cell)))
 
 
-def stage_kernel(cell, weight, state, turned, sem):
-    columns = state.shape[0] - 2
-    width = state.shape[2] - 2 * PAD
+def stage_kernel(
+    tile_slot, tile_cell, tile_count, cell, weight, state, turned, slots, spots, points, sem, *, size_y
+):
+    pos_x, pos_y = lax.axis_index("gx"), lax.axis_index("gy")
+    columns, count, tall = state.shape[0] - 2, state.shape[1], state.shape[2]
+    width = tall - ROOM
     copies = [
         pltpu.make_async_copy(
             cell.at[:, :, pl.ds(j * BLK, BLK)], state.at[j + 1, :, pl.ds(PAD, width)], sem.at[j]
@@ -152,26 +158,42 @@
         return carry
 
     lax.fori_loop(0, weight.shape[0] // TURN, transpose, 0)
+    counted = tile_count[0]
+
+    def index(step, carry):
+        for k in range(TURN):
+            t = step * TURN + k
+            x, j = split_device(tile_cell[t], columns)
+            slots[t] = jnp.where(t < counted, local_slot(tile_slot[t], pos_x, pos_y, size_y), 9 * CAP)
+            spots[t] = (j + 1) * (count * tall) + x + PAD
+            points[t] = j * width + x
+        return carry
+
+    lax.fori_loop(0, weight.shape[0] // TURN, index, 0)
     for copy in copies:
         copy.wait()
 
 
-def stage(cell, weight):
+def stage(tile_slot, tile_cell, tile_count, cell, weight, size_y):
     count, width, lanes = cell.shape
     columns = lanes // BLK
+    indices = pltpu.SMEM(tile_slot.shape, jnp.int32)
     return pl.pallas_call(
-        stage_kernel,
+        functools.partial(stage_kernel, size_y=size_y),
         name="stage",
         out_shape=(
-            pltpu.VMEM((columns + 2, count, width + 2 * PAD, BLK), F32),
+            pltpu.VMEM((columns + 2, count, width + ROOM, BLK), F32),
             pltpu.VMEM(weight.shape, weight.dtype),
+            indices,
+            indices,
+            indices,
         ),
-        in_specs=[ANY, VMEM],
-        out_specs=(VMEM, VMEM),
+        in_specs=[SMEM, SMEM, SMEM, ANY, VMEM],
+        out_specs=(VMEM, VMEM, SMEM, SMEM, SMEM),
         scratch_shapes=[pltpu.SemaphoreType.DMA((columns,))],
         compiler_params=pltpu.CompilerParams(vmem_limit_bytes=2 * MIB),
         cost_estimate=pl.CostEstimate(flops=0, bytes_accessed=2 * cell.size * 4, transcendentals=0),
-    )(in_hbm(cell), weight)
+    )(tile_slot, tile_cell, tile_count, in_hbm(cell), weight)
 
 
 def fetch_kernel(source, target, sem):
@@ -206,38 +228,46 @@
     return pltpu.roll(value, HALF, value.ndim - 1)
 
 
+def beside(weight, t):
+    return jnp.concatenate([weight[t], weight[t + 1]], axis=1)
+
+
+def add_at(buffer, places, index, values):
+    held = [buffer[index(place)] for place in places]
+    for k, place in enumerate(places):
+        value = values[k]
+        for earlier in range(k):
+            value = value + jnp.where(places[earlier] == place, values[earlier], 0.0)
+        buffer[index(place)] = held[k] + value
+
+
 def deposit_kernel(
-    tile_slot, tile_cell, tile_count, own, first, second, south, north, weight, state_in,
-    state, edge_x1, edge_x2, edge_y1, edge_y2, rows, *, size_y
+    slots, spots, own, first, second, south, north, weight, state_in,
+    state, edge_x1, edge_x2, edge_y1, edge_y2, rows
 ):
     pos_x, pos_y = lax.axis_index("gx"), lax.axis_index("gy")
     n_tiles = weight.shape[0]
     columns, count, tall = state.shape[0] - 2, state.shape[1], state.shape[2]
-    flat = state.reshape(columns + 2, count * tall, BLK)
+    line = state.reshape((columns + 2) * count * tall, BLK)
+    rows[9 * CAP] = jnp.zeros(rows.shape[1:], BF16)
     for k, part in enumerate((own, first, second)):
         for r in range(CAP):
             rows[k * CAP + r] = part[r]
     for k, part in enumerate((south, north)):
         for r in range(3 * CAP):
             rows[(k + 1) * 3 * CAP + r] = part[r]
-    counted = tile_count[0]
-
-    def add_tiles(step, carry):
-        for k in range(UNROLL):
-            t = step * UNROLL + k
-            slot = local_slot(tile_slot[t], pos_x, pos_y, size_y)
-            contrib = jnp.dot(rows[slot], weight[t], preferred_element_type=F32)[:count]
-            contrib = jnp.where(t < counted, contrib, 0.0)
-            x, j = split_device(tile_cell[t], columns)
-            at = pl.ds(x + PAD, count, stride=tall)
-            flat[j + 1, at, :] = flat[j + 1, at, :] + contrib
-        return carry
-
-    lax.fori_loop(0, n_tiles // UNROLL, add_tiles, 0)
+    for first_tile in range(0, n_tiles, TOGETHER):
+        tiles = range(first_tile, first_tile + TOGETHER)
+        contribs = []
+        for t in tiles[::2]:
+            both = jnp.concatenate([rows[slots[t]], rows[slots[t + 1]]], axis=0)
+            found = jnp.dot(both, beside(weight, t), preferred_element_type=F32)
+            contribs += [found[:count, :BLK], found[ROWS : ROWS + count, BLK:]]
+        add_at(line, [spots[t] for t in tiles], lambda place: (pl.ds(place, count, stride=tall), slice(None)), contribs)
 
     even_x, even_y = (pos_x & 1) == 0, (pos_y & 1) == 0
-    top, bottom = tall - PAD - 1, PAD
-    line = state.reshape((columns + 2) * count * tall, BLK)
+    width = tall - ROOM
+    top, bottom = PAD + width - 1, PAD
     for edge, row in (
         (edge_x1, jnp.where(even_x, bottom, top)),
         (edge_x2, jnp.where(even_x, top, bottom)),
@@ -246,7 +276,6 @@
             at = pl.ds(count * tall + q * tall + row, columns, stride=count * tall)
             edge[q * columns : (q + 1) * columns, :] = line[at, :].astype(BF16)
     low = low_lanes()
-    width = tall - 2 * PAD
     for edge, upper in ((edge_y1, jnp.logical_not(even_y)), (edge_y2, even_y)):
         column = jnp.where(upper, columns, 1)
         for q in range(count // 2):
@@ -258,20 +287,20 @@
                 edge[q * width + i * ROWS : q * width + (i + 1) * ROWS, :] = both.astype(BF16)
 
 
-def deposit(tile_slot, tile_cell, tile_count, parts, weight, state, size_y):
+def deposit(slots, spots, parts, weight, state):
     columns, count, tall = state.shape[0] - 2, state.shape[1], state.shape[2]
     edge_x = pltpu.VMEM((count * columns, BLK), BF16)
-    edge_y = pltpu.VMEM((count // 2 * (tall - 2 * PAD), BLK), BF16)
+    edge_y = pltpu.VMEM((count // 2 * (tall - ROOM), BLK), BF16)
     return pl.pallas_call(
-        functools.partial(deposit_kernel, size_y=size_y),
+        deposit_kernel,
         name="deposit",
         out_shape=(pltpu.VMEM(state.shape, F32), edge_x, edge_x, edge_y, edge_y),
-        in_specs=[SMEM] * 3 + [VMEM] * 7,
+        in_specs=[SMEM] * 2 + [VMEM] * 7,
         out_specs=(VMEM,) * 5,
-        input_output_aliases={9: 0},
-        scratch_shapes=[pltpu.VMEM((9 * CAP, ROWS, BLK), BF16)],
+        input_output_aliases={8: 0},
+        scratch_shapes=[pltpu.VMEM((9 * CAP + 1, ROWS, BLK), BF16)],
         compiler_params=pltpu.CompilerParams(vmem_limit_bytes=4 * MIB),
-    )(tile_slot, tile_cell, tile_count, *parts, weight, state)
+    )(slots, spots, *parts, weight, state)
 
 
 def total(terms):
@@ -378,7 +407,7 @@
     columns, tall = state.shape[0] - 2, state.shape[2]
 
     def speeds(step, carry):
-        rows = range(PAD, tall - PAD, 8)
+        rows = range(PAD, tall - AFTER, 8)
         places = [(1 + step * GROUP + k, row) for k in range(GROUP) for row in rows]
         store_speeds(props, state, speed, places, (0, 1))
         return carry
@@ -386,7 +415,7 @@
     lax.fori_loop(0, columns // GROUP, speeds, 0)
 
     def remap(step, carry):
-        rows = range(PAD + 8, tall - PAD - 8, 8)
+        rows = range(PAD + 8, tall - AFTER - 8, 8)
         places = [(2 + step * PAIR + k, row) for k in range(PAIR) for row in rows]
         remap_tiles(props, state, speed, press, fresh, places, scalars(state.shape[1]))
         return carry
@@ -412,16 +441,19 @@
 
 
 def outer_kernel(
-    props, tile_slot, tile_cell, tile_count, edge_x1, edge_x2, edge_y1, edge_y2, weight, state_in, speed_in, press_in,
-    fresh_in, state, speed, press, fresh, own, first, second, sums, *, size_x, size_y
+    props, slots, points, edge_x1, edge_x2, edge_y1, edge_y2, weight, state_in, speed_in, press_in,
+    fresh_in, remapped, state, speed, press, fresh, own, first, second, sums, sem, *, size_x, size_y
 ):
     pos_x, pos_y = lax.axis_index("gx"), lax.axis_index("gy")
     n_tiles = weight.shape[0]
     columns, count, tall = state.shape[0] - 2, state.shape[1], state.shape[2]
-    width = tall - 2 * PAD
+    width = tall - ROOM
+    copies = area_copies(fresh, remapped, sem, scalar_planes(count), [inner_area(fresh)])
+    for copy in copies:
+        copy.start()
     even_x, even_y = (pos_x & 1) == 0, (pos_y & 1) == 0
     line = state.reshape((columns + 2) * count * tall, BLK)
-    above, below = tall - PAD, PAD - 1
+    above, below = PAD + width, PAD - 1
     for edge, row, there in (
         (edge_x1, jnp.where(even_x, below, above), has_far(pos_x, size_x)),
         (edge_x2, jnp.where(even_x, above, below), True),
@@ -443,48 +475,48 @@
                 state[column, q, here, :] = jnp.where(low, both, turned)
                 state[column, q + count // 2, here, :] = jnp.where(low, turned, both)
 
-    places = [(j, row) for j in range(1, columns + 1) for row in (0, tall - PAD)]
+    places = [(j, row) for j in range(1, columns + 1) for row in (0, tall - AFTER)]
     store_speeds(props, state, speed, places, (0,))
-    places = [(j, row) for j in (0, columns + 1) for row in range(PAD, tall - PAD, 8)]
+    places = [(j, row) for j in (0, columns + 1) for row in range(PAD, tall - AFTER, 8)]
     store_speeds(props, state, speed, places, (1,))
 
     def sides(step, carry):
-        places = [(1 + step * 2 * PAIR + k, row) for k in range(2 * PAIR) for row in (PAD, tall - PAD - 8)]
+        places = [(1 + step * 2 * PAIR + k, row) for k in range(2 * PAIR) for row in (PAD, tall - AFTER - 8)]
         remap_tiles(props, state, speed, press, fresh, places, scalars(state.shape[1]))
         return carry
 
     lax.fori_loop(0, columns // (2 * PAIR), sides, 0)
-    places = [(j, row) for j in (1, columns) for row in range(PAD + 8, tall - PAD - 8, 8)]
+    places = [(j, row) for j in (1, columns) for row in range(PAD + 8, tall - AFTER - 8, 8)]
     remap_tiles(props, state, speed, press, fresh, places, scalars(state.shape[1]))
 
     sums[...] = jnp.zeros(sums.shape, F32)
-    counted = tile_count[0]
-    head = lax.broadcasted_iota(jnp.int32, (ROWS, BLK), 0) == 0
-
-    def sample(step, carry):
-        for k in range(UNROLL):
-            t = step * UNROLL + k
-            slot = local_slot(tile_slot[t], pos_x, pos_y, size_y)
-            x, j = split_device(tile_cell[t], columns)
-            probe = jnp.where(head, press[j, pl.ds(x, 1), :], 1.0).astype(BF16)
-            both = jnp.dot(probe, weight[t], preferred_element_type=F32)[:8]
-            sums[slot] = sums[slot] + jnp.where(t < counted, both, 0.0)
-        return carry
-
-    lax.fori_loop(0, n_tiles // UNROLL, sample, 0)
+    line_of = lax.broadcasted_iota(jnp.int32, (ROWS, BLK), 0)
+    field = press.reshape(columns * width, BLK)
+    for first_tile in range(0, n_tiles, TOGETHER):
+        tiles = range(first_tile, first_tile + TOGETHER)
+        found = []
+        for t in tiles[::2]:
+            one, two = (field[pl.ds(points[k], 1), :] for k in (t, t + 1))
+            probe = jnp.where(line_of == 0, one, jnp.where(line_of == 8, two, 1.0)).astype(BF16)
+            both = jnp.dot(probe, beside(weight, t), preferred_element_type=F32)
+            found += [both[:8, :BLK], both[8:, BLK:]]
+        add_at(sums, [slots[t] for t in tiles], lambda place: place, found)
     table = sums.reshape(sums.shape[0] * 8, BLK)
     for k, out in enumerate((own, first, second)):
         top = table[pl.ds(k * 3 * CAP * 8, 3 * CAP, stride=8), :]
         under = table[pl.ds(k * 3 * CAP * 8 + 1, 3 * CAP, stride=8), :]
         out[...] = top / jnp.maximum(under, 1.0)
-
-
-def outer(props, tile_slot, tile_cell, tile_count, edges, weight, state, speed, press, fresh, size_x, size_y):
+    for copy in copies:
+        copy.wait()
+
+
+def outer(props, slots, points, edges, weight, state, speed, press, fresh, size_x, size_y):
     answer = pltpu.VMEM((3 * CAP, BLK), F32)
     outs = pl.pallas_call(
         functools.partial(outer_kernel, size_x=size_x, size_y=size_y),
         name="outer",
         out_shape=(
+            jax.ShapeDtypeStruct(fresh.shape, F32),
             pltpu.VMEM(state.shape, F32),
             pltpu.VMEM(speed.shape, F32),
             pltpu.VMEM(press.shape, F32),
@@ -493,49 +525,64 @@
             answer,
             answer,
         ),
-        in_specs=[SMEM] * 4 + [VMEM] * 9,
-        out_specs=(VMEM,) * 7,
-        input_output_aliases={9: 0, 10: 1, 11: 2, 12: 3},
-        scratch_shapes=[pltpu.VMEM((9 * CAP, 8, BLK), F32)],
+        in_specs=[SMEM] * 3 + [VMEM] * 9,
+        out_specs=(ANY,) + (VMEM,) * 7,
+        input_output_aliases={8: 1, 9: 2, 10: 3, 11: 4},
+        scratch_shapes=[pltpu.VMEM((9 * CAP + 1, 8, BLK), F32), pltpu.SemaphoreType.DMA((2,))],
         compiler_params=pltpu.CompilerParams(vmem_limit_bytes=4 * MIB),
-    )(props, tile_slot, tile_cell, tile_count, *edges, weight, state, speed, press, fresh)
-    return outs[0], outs[1], outs[3], outs[4], outs[5], outs[6]
-
-
-def late_kernel(state, speed, fresh_in, remapped, fresh, sem):
+    )(props, slots, points, *edges, weight, state, speed, press, fresh)
+    return outs[0], outs[1], outs[2], outs[4], outs[5], outs[6], outs[7]
+
+
+def late_kernel(state, speed, fresh_in, remapped_in, remapped, fresh, sem, sem_moving):
     columns, count, tall = state.shape[0] - 2, state.shape[1], state.shape[2]
-    moving = range(MAT, count - 1)
-    copies = [
-        pltpu.make_async_copy(fresh.at[rows], remapped.at[rows], sem.at[k])
-        for k, rows in enumerate((pl.ds(0, MAT), pl.ds(count - 1, 1), pl.ds(MAT, count - 1 - MAT)))
+    width, lanes = fresh.shape[1], fresh.shape[2]
+    rows = pl.ds(8, width - 16)
+    areas = [
+        (pl.ds(0, 8), pl.ds(0, lanes)),
+        (pl.ds(width - 8, 8), pl.ds(0, lanes)),
+        (rows, pl.ds(0, BLK)),
+        (rows, pl.ds(lanes - BLK, BLK)),
     ]
-    copies[0].start()
-    copies[1].start()
-
-    def remap(step, carry):
-        rows = range(PAD, tall - PAD, 8)
-        places = [(1 + step * PAIR + k, row) for k in range(PAIR) for row in rows]
-        remap_tiles(None, state, speed, None, fresh, places, moving)
-        return carry
-
-    lax.fori_loop(0, columns // PAIR, remap, 0)
-    copies[2].start()
+    copies = area_copies(fresh, remapped, sem, scalar_planes(count), areas)
+    for copy in copies:
+        copy.start()
+    for part in range(PARTS):
+        held = range(1 + part * columns // PARTS, 1 + (part + 1) * columns // PARTS)
+        places = [(j, row) for j in held for row in range(PAD, tall - AFTER, 8)]
+        remap_tiles(None, state, speed, None, fresh, places, range(MAT, count - 1))
+        area = (pl.ds(0, width), pl.ds((held[0] - 1) * BLK, len(held) * BLK))
+        copies += area_copies(fresh, remapped, sem_moving.at[part], [pl.ds(MAT, count - 1 - MAT)], [area])
+        copies[-1].start()
     for copy in copies:
         copy.wait()
 
 
-def late(state, speed, fresh):
+def scalar_planes(count):
+    return [pl.ds(0, MAT), pl.ds(count - 1, 1)]
+
+
+def inner_area(fresh):
+    return pl.ds(8, fresh.shape[1] - 16), pl.ds(BLK, fresh.shape[2] - 2 * BLK)
+
+
+def area_copies(fresh, remapped, sem, planes, areas):
+    boxes = [(plane, *area) for area in areas for plane in planes]
+    return [pltpu.make_async_copy(fresh.at[box], remapped.at[box], sem.at[k]) for k, box in enumerate(boxes)]
+
+
+def late(state, speed, fresh, remapped):
     return pl.pallas_call(
         late_kernel,
         name="late",
         out_shape=(jax.ShapeDtypeStruct(fresh.shape, F32), pltpu.VMEM(fresh.shape, F32)),
-        in_specs=[VMEM] * 3,
+        in_specs=[VMEM] * 3 + [ANY],
         out_specs=(ANY, VMEM),
-        input_output_aliases={2: 1},
-        scratch_shapes=[pltpu.SemaphoreType.DMA((3,))],
+        input_output_aliases={2: 1, 3: 0},
+        scratch_shapes=[pltpu.SemaphoreType.DMA((8,)), pltpu.SemaphoreType.DMA((PARTS, 1))],
         compiler_params=pltpu.CompilerParams(vmem_limit_bytes=4 * MIB),
         cost_estimate=pl.CostEstimate(flops=5 * state.size, bytes_accessed=2 * state.size * 4, transcendentals=0),
-    )(state, speed, fresh)[0]
+    )(state, speed, fresh, remapped)[0]
 
 
 def pick_kernel(place, own, first, second, out, table, lines):
@@ -591,7 +638,9 @@
     first = swap(first, "gx", 1)
     second = swap(second, "gx", 2)
     weight, own = lax.optimization_barrier((weight, own))
-    state, turned = stage(cell_state, weight)
+    state, turned, slots, spots, points = stage(
+        tile_slot, tile_cell, tile_count, cell_state, weight, size_y
+    )
 
     def along_y(which):
         rows = slice(which * CAP, (which + 1) * CAP)
@@ -600,7 +649,7 @@
     south = swap(along_y(1), "gy", 1)
     north = swap(along_y(2), "gy", 2)
     state, *edges = deposit(
-        tile_slot, tile_cell, tile_count, (own, first, second, south, north), weight, state, size_y
+        slots, spots, (own, first, second, south, north), weight, state
     )
     edges = (
         swap(edges[0], "gx", 1),
@@ -609,10 +658,10 @@
         swap(edges[3], "gy", 2),
     )
     fresh, press, speed = inner(mat_props, state, cell_state.shape[1])
-    state, speed, fresh, own, first, second = outer(
-        mat_props, tile_slot, tile_cell, tile_count, edges, turned, state, speed, press, fresh, size_x, size_y
-    )
-    remapped = late(state, speed, fresh)
+    remapped, state, speed, fresh, own, first, second = outer(
+        mat_props, slots, points, edges, turned, state, speed, press, fresh, size_x, size_y
+    )
+    remapped = late(state, speed, fresh, remapped)
     first = swap(first, "gy", 1)
     second = swap(second, "gy", 2)
 

time: 38.5 us -> 37.6 us (0.977)
  Pallas kernels: 17 us -> 15.5 us
  waiting for transfers between devices: 2.1 us -> 2.54 us
    pallas_call x1, Pallas kernels: 2.7 us -> 2.13 us  [late(): pl.pallas_call(late_kernel, name='late', out_shape=(jax.ShapeDtypeStruct(...]
    pallas_call x1, Pallas kernels: 2.99 us -> 2.42 us  [outer(): pl.pallas_call(functools.partial(outer_kernel, size_x=size_x, size_y=size...]
    ppermute x12, waiting for transfers between devices: 2.1 us -> 2.54 us  [swap(): return lax.ppermute(value, axis, pairs)]
  transfers between devices with their start and end apart: 12 -> 12, of which waited for: 3 -> 2; matrix products, arithmetic and copies ran while one was open for 0% -> 0% of each run, Pallas kernels for 28% -> 28%
where the time goes in v7:
time: 37.6 us; the launch traced here: 37.4 us
  starting transfers between devices  17.8 us (47%)
  Pallas kernels  15.5 us (41%)
  waiting for transfers between devices  2.54 us (7%)
  between operations  1.47 us (4%)
    ppermute x12, starting transfers between devices, swap(): return lax.ppermute(value, axis, pairs)  17.8 us
    pallas_call x1, Pallas kernels, stage(): pl.pallas_call(functools.partial(stage_kernel, size_y=size_y), name='stag...  3.31 us
    pallas_call x1, Pallas kernels, inner(): pl.pallas_call(inner_kernel, name='inner', out_shape=(pltpu.VMEM((count,...  2.7 us
    ppermute x12, waiting for transfers between devices, swap(): return lax.ppermute(value, axis, pairs)  2.54 us
    pallas_call x1, Pallas kernels, outer(): pl.pallas_call(functools.partial(outer_kernel, size_x=size_x, size_y=size...  2.42 us
    pallas_call x1, Pallas kernels, fetch(): pl.pallas_call(fetch_kernel, name='fetch', out_shape=pltpu.VMEM(value.sha...  2.2 us
    pallas_call x1, Pallas kernels, late(): pl.pallas_call(late_kernel, name='late', out_shape=(jax.ShapeDtypeStruct(...  2.13 us
    pallas_call x1, Pallas kernels, deposit(): pl.pallas_call(deposit_kernel, name='deposit', out_shape=(pltpu.VMEM(stat...  1.11 us
  transfers between devices with their start and end apart: 12, of which 2 were waited for; matrix products, arithmetic and copies ran while one was open for 0% of the time, Pallas kernels for 28%

profile of v7, /device:TPU:0, one launch (start us, length us, event | category | flops | bytes accessed | tf_op | source)
XLA Modules:
  0.0 37.4 jit_solution(14828556953363382598)
XLA Ops:
  0.6 1.0 %payload.1 = (bf16[6,16,128]{2,1,0:T(8,128)(2,1)S(1)}, bf16[6,16,128]{2,1,0:T(8,128)(2,1)S(1)}, bf16[6,16,128]{2,1,0:T(8,128)(2,1)S(1)}, s32[18]{0:T(128)S(4)}, ...) custom-call(s32[18]{0:T(128)} %dest_hbm.1, f32[2,8]{1,0:T(2,128)} %props_hbm.1, f32[18,128]{1,0:T(8,128)} %bitcast.4, ...), custom_call_target="tpu_custom_call" | custom-call | tf_op jit(solution)/shard_map/payload/pallas_call | solution.py:112
  1.7 2.5 %collective-permute-start = (bf16[6,16,128]{2,1,0:T(8,128)(2,1)S(1)}, bf16[6,16,128]{2,1,0:T(8,128)(2,1)S(1)}, u32[]{:S(2)}, u32[]{:S(2)}) collective-permute-start(bf16[6,16,128]{2,1,0:T(8,128)(2,1)S(1)} %get-tuple-element.41), channel_id=1, source_target_pairs={{0,24},{8,16},{16,8},{24,0},{1,25},{9,17},{17,9},{25,1},{2,26},{10... | collective-permute-start | bytes 73736 | tf_op jit(solution)/shard_map/ppermute | solution.py:47
  4.2 0.7 %collective-permute-start.1 = (bf16[6,16,128]{2,1,0:T(8,128)(2,1)S(1)}, bf16[6,16,128]{2,1,0:T(8,128)(2,1)S(1)}, u32[]{:S(2)}, u32[]{:S(2)}) collective-permute-start(bf16[6,16,128]{2,1,0:T(8,128)(2,1)S(1)} %get-tuple-element.42), channel_id=1, source_target_pairs={{0,8},{8,0},{16,24},{24,16},{1,9},{9,1},{17,25},{25,17},{2,10},{10... | collective-permute-start | bytes 73736 | tf_op jit(solution)/shard_map/ppermute | solution.py:47
  4.8 2.2 %fetch.1.weight = bf16[128,128,128]{2,1,0:T(8,128)(2,1)S(1)} custom-call(bf16[128,128,128]{2,1,0:T(8,128)(2,1)} %source.1), custom_call_target="tpu_custom_call" | custom-call | bytes 8388608 | tf_op jit(solution)/shard_map/fetch/pallas_call | solution.py:206
  7.0 0.0 collective-permute-done.first
  7.1 0.0 collective-permute-done.1.second
  7.1 4.6 %collective-permute-start.2 = (bf16[6,16,128]{2,1,0:T(8,128)(2,1)S(1)}, bf16[6,16,128]{2,1,0:T(8,128)(2,1)S(1)}, u32[]{:S(2)}, u32[]{:S(2)}) collective-permute-start(bf16[6,16,128]{2,1,0:T(8,128)(2,1)S(1)} %pad_maximum_fusion), channel_id=1, source_target_pairs={{0,7},{1,2},{2,1},{3,4},{4,3},{5,6},{6,5},{7,0},{8,15},{9,10},{10,... | collective-permute-start | bytes 73736 | tf_op jit(solution)/shard_map/ppermute | solution.py:47
  11.7 0.0 collective-permute-start.3
  12.4 3.3 %stage.1 = (f32[18,12,88,128]{3,2,1,0:T(8,128)S(1)}, bf16[128,128,128]{2,1,0:T(8,128)(2,1)S(1)}, s32[128]{0:T(128)S(4)}, s32[128]{0:T(128)S(4)}, s32[128]{0:T(128)S(4)}) custom-call(s32[128]{0:T(128)S(4)} %get-tuple-element.33.tile_slot, s32[128]{0:T(128)S(4)} %get-tuple-element.34.tile_cell, s32[1]{0:T(128)S(6)} %copy.27.tile_count, f32[12,64,2048]{2,1,0:T(8,128)} %cell.1, ...), custom_call_target="tpu_custom_call" | custom-call | bytes 12582912 | tf_op jit(solution)/shard_map/stage/pallas_call | solution.py:181
  15.7 0.0 collective-permute-done.2.south
  15.7 0.0 collective-permute-done.3.north
  15.7 1.1 %deposit.1 = (f32[18,12,88,128]{3,2,1,0:T(8,128)S(1)}, bf16[192,128]{1,0:T(8,128)(2,1)S(1)}, bf16[192,128]{1,0:T(8,128)(2,1)S(1)}, bf16[384,128]{1,0:T(8,128)(2,1)S(1)}, bf16[384,128]{1,0:T(8,128)(2,1)S(1)}) custom-call(s32[128]{0:T(128)S(4)} %get-tuple-element.37.slots, s32[128]{0:T(128)S(4)} %get-tuple-element.39.spots, ...), custom_call_target="tpu_custom_call", output_to_operand_aliasing={{0}: (8, {})} | custom-call | tf_op jit(solution)/shard_map/deposit/pallas_call | solution.py:294
  16.8 0.7 %collective-permute-start.6 = (bf16[384,128]{1,0:T(8,128)(2,1)S(1)}, bf16[384,128]{1,0:T(8,128)(2,1)S(1)}, u32[]{:S(2)}, u32[]{:S(2)}) collective-permute-start(bf16[384,128]{1,0:T(8,128)(2,1)S(1)} %get-tuple-element.46), channel_id=1, source_target_pairs={{0,0},{1,2},{2,1},{3,4},{4,3},{5,6},{6,5},{7,7},{8,8},{9,10},{10,9... | collective-permute-start | bytes 294920 | tf_op jit(solution)/shard_map/ppermute | solution.py:47
  17.5 3.3 %collective-permute-start.7 = (bf16[384,128]{1,0:T(8,128)(2,1)S(1)}, bf16[384,128]{1,0:T(8,128)(2,1)S(1)}, u32[]{:S(2)}, u32[]{:S(2)}) collective-permute-start(bf16[384,128]{1,0:T(8,128)(2,1)S(1)} %get-tuple-element.47), channel_id=1, source_target_pairs={{0,1},{1,0},{2,3},{3,2},{4,5},{5,4},{6,7},{7,6},{8,9},{9,8},{10,11... | collective-permute-start | bytes 294920 | tf_op jit(solution)/shard_map/ppermute | solution.py:47
  20.8 0.0 collective-permute-start.4
  20.9 1.2 %collective-permute-start.5 = (bf16[192,128]{1,0:T(8,128)(2,1)S(1)}, bf16[192,128]{1,0:T(8,128)(2,1)S(1)}, u32[]{:S(2)}, u32[]{:S(2)}) collective-permute-start(bf16[192,128]{1,0:T(8,128)(2,1)S(1)} %get-tuple-element.45), channel_id=1, source_target_pairs={{0,8},{8,0},{16,24},{24,16},{1,9},{9,1},{17,25},{25,17},{2,10},{10... | collective-permute-start | bytes 147464 | tf_op jit(solution)/shard_map/ppermute | solution.py:47
  22.1 2.7 %inner.1 = (f32[12,64,2048]{2,1,0:T(8,128)S(1)}, f32[16,64,128]{2,1,0:T(8,128)S(1)}, f32[18,3,88,128]{3,2,1,0:T(8,128)S(1)}) custom-call(f32[2,8]{1,0:T(2,128)S(4)} %get-tuple-element.32.props, f32[18,12,88,128]{3,2,1,0:T(8,128)S(1)} %get-tuple-element.49.state.state_in), custom_call_target="tpu_custom_call" | custom-call | flops 48660480 | bytes 19464192 | tf_op jit(solution)/shard_map/inner/pallas_call | solution.py:428
  24.8 0.0 collective-permute-done.4.edge_x1
  24.8 0.0 collective-permute-done.5.edge_x2
  24.8 0.0 collective-permute-done.6.edge_y1
  24.8 0.0 collective-permute-done.7.edge_y2
  24.8 2.4 %outer.1 = (f32[12,64,2048]{2,1,0:T(8,128)}, f32[18,12,88,128]{3,2,1,0:T(8,128)S(1)}, f32[18,3,88,128]{3,2,1,0:T(8,128)S(1)}, f32[16,64,128]{2,1,0:T(8,128)S(1)}...) custom-call(f32[2,8]{1,0:T(2,128)S(4)} %get-tuple-element.32.props, ...), custom_call_target="tpu_custom_call", output_to_operand_aliasing={{1}: (8, {}), {2}: (9, {}), {3}: (10, {}), {4}: (11, {})} | custom-call | tf_op jit(solution)/shard_map/outer/pallas_call | solution.py:515
  27.3 1.9 %collective-permute-start.8 = (f32[6,128]{1,0:T(8,128)S(1)}, f32[6,128]{1,0:T(8,128)S(1)}, u32[]{:S(2)}, u32[]{:S(2)}) collective-permute-start(f32[6,128]{1,0:T(8,128)S(1)} %get-tuple-element.60), channel_id=1, source_target_pairs={{0,7},{1,2},{2,1},{3,4},{4,3},{5,6},{6,5},{7,0},{8,15},{9,10},{10,... | collective-permute-start | bytes 9224 | tf_op jit(solution)/shard_map/ppermute | solution.py:47
  29.1 1.7 %collective-permute-start.9 = (f32[6,128]{1,0:T(8,128)S(1)}, f32[6,128]{1,0:T(8,128)S(1)}, u32[]{:S(2)}, u32[]{:S(2)}) collective-permute-start(f32[6,128]{1,0:T(8,128)S(1)} %get-tuple-element.61), channel_id=1, source_target_pairs={{0,1},{1,0},{2,3},{3,2},{4,5},{5,4},{6,7},{7,6},{8,9},{9,8},{10,11... | collective-permute-start | bytes 9224 | tf_op jit(solution)/shard_map/ppermute | solution.py:47
  30.8 2.1 %late.1 = (f32[12,64,2048]{2,1,0:T(8,128)}, f32[12,64,2048]{2,1,0:T(8,128)S(1)}) custom-call(f32[18,12,88,128]{3,2,1,0:T(8,128)S(1)} %get-tuple-element.53.state, f32[18,3,88,128]{3,2,1,0:T(8,128)S(1)} %get-tuple-element.54.speed, f32[12,64,2048]{2,1,0:T(8,128)S(1)} %get-tuple-element.55.fresh_in, ...), custom_call_target="tpu_custom_call", output_to_operand_aliasing={{1}: (2, {}), {0}: (3, {})} | custom-call | flops 12165120 | bytes 19464192 | tf_op jit(solution)/shard_map/late/pallas_call | solution.py:575
  33.0 0.7 %collective-permute-done.8 = f32[6,128]{1,0:T(8,128)S(1)} collective-permute-done((f32[6,128]{1,0:T(8,128)S(1)}, f32[6,128]{1,0:T(8,128)S(1)}, u32[]{:S(2)}, u32[]{:S(2)}) %collective-permute-start.8) | collective-permute-done | bytes 3104 | tf_op jit(solution)/shard_map/ppermute | solution.py:47
  33.6 0.0 collective-permute-done.9
  33.7 0.1 collective-permute-start.10
  33.7 1.1 %collective-permute-start.11 = (f32[6,128]{1,0:T(8,128)S(1)}, f32[6,128]{1,0:T(8,128)S(1)}, u32[]{:S(2)}, u32[]{:S(2)}) collective-permute-start(f32[6,128]{1,0:T(8,128)S(1)} %pad_maximum_fusion.4), channel_id=1, source_target_pairs={{0,8},{8,0},{16,24},{24,16},{1,9},{9,1},{17,25},{25,17},{2,10},{10... | collective-permute-start | bytes 9224 | tf_op jit(solution)/shard_map/ppermute | solution.py:47
  34.9 1.8 %collective-permute-done.10.first = f32[6,128]{1,0:T(8,128)S(1)} collective-permute-done((f32[6,128]{1,0:T(8,128)S(1)}, f32[6,128]{1,0:T(8,128)S(1)}, u32[]{:S(2)}, u32[]{:S(2)}) %collective-permute-start.10) | collective-permute-done | bytes 3104 | tf_op jit(solution)/shard_map/ppermute | solution.py:47
  36.8 0.0 collective-permute-done.11.second
  36.8 0.6 %pick.1 = bf16[18,128]{1,0:T(8,128)(2,1)} custom-call(s32[18]{0:T(128)S(4)} %get-tuple-element.58.place, f32[6,128]{1,0:T(8,128)S(1)} %pad_maximum_fusion.2.own, f32[6,128]{1,0:T(8,128)S(1)} %collective-permute-done.10.first, f32[6,128]{1,0:T(8,128)S(1)} %collective-permute-done.11.second), custom_call_target="tpu_custom_call" | custom-call | tf_op jit(solution)/shard_map/pick/pallas_call | solution.py:598
  (11 shorter events, 0.1 us)
Async XLA Ops:
  1.7 5.4 %collective-permute-start = (bf16[6,16,128]{2,1,0:T(8,128)(2,1)S(1)}, bf16[6,16,128]{2,1,0:T(8,128)(2,1)S(1)}, u32[]{:S(2)}, u32[]{:S(2)}) collective-permute-start(bf16[6,16,128]{2,1,0:T(8,128)(2,1)S(1)} %get-tuple-element.41), channel_id=1, source_target_pairs={{0,24},{8,16},{16,8},{24,0},{1,25},{9,17},{17,9},{25,1},{2,26},{10... | collective-permute-start | bytes 73736 | tf_op jit(solution)/shard_map/ppermute | solution.py:47
  4.2 2.9 %collective-permute-start.1 = (bf16[6,16,128]{2,1,0:T(8,128)(2,1)S(1)}, bf16[6,16,128]{2,1,0:T(8,128)(2,1)S(1)}, u32[]{:S(2)}, u32[]{:S(2)}) collective-permute-start(bf16[6,16,128]{2,1,0:T(8,128)(2,1)S(1)} %get-tuple-element.42), channel_id=1, source_target_pairs={{0,8},{8,0},{16,24},{24,16},{1,9},{9,1},{17,25},{25,17},{2,10},{10... | collective-permute-start | bytes 73736 | tf_op jit(solution)/shard_map/ppermute | solution.py:47
  7.1 8.6 %collective-permute-start.2 = (bf16[6,16,128]{2,1,0:T(8,128)(2,1)S(1)}, bf16[6,16,128]{2,1,0:T(8,128)(2,1)S(1)}, u32[]{:S(2)}, u32[]{:S(2)}) collective-permute-start(bf16[6,16,128]{2,1,0:T(8,128)(2,1)S(1)} %pad_maximum_fusion), channel_id=1, source_target_pairs={{0,7},{1,2},{2,1},{3,4},{4,3},{5,6},{6,5},{7,0},{8,15},{9,10},{10,... | collective-permute-start | bytes 73736 | tf_op jit(solution)/shard_map/ppermute | solution.py:47
  11.7 4.0 %collective-permute-start.3 = (bf16[6,16,128]{2,1,0:T(8,128)(2,1)S(1)}, bf16[6,16,128]{2,1,0:T(8,128)(2,1)S(1)}, u32[]{:S(2)}, u32[]{:S(2)}) collective-permute-start(bf16[6,16,128]{2,1,0:T(8,128)(2,1)S(1)} %pad_maximum_fusion.1), channel_id=1, source_target_pairs={{0,1},{1,0},{2,3},{3,2},{4,5},{5,4},{6,7},{7,6},{8,9},{9,8},{10,11... | collective-permute-start | bytes 73736 | tf_op jit(solution)/shard_map/ppermute | solution.py:47
  16.8 8.0 %collective-permute-start.6 = (bf16[384,128]{1,0:T(8,128)(2,1)S(1)}, bf16[384,128]{1,0:T(8,128)(2,1)S(1)}, u32[]{:S(2)}, u32[]{:S(2)}) collective-permute-start(bf16[384,128]{1,0:T(8,128)(2,1)S(1)} %get-tuple-element.46), channel_id=1, source_target_pairs={{0,0},{1,2},{2,1},{3,4},{4,3},{5,6},{6,5},{7,7},{8,8},{9,10},{10,9... | collective-permute-start | bytes 294920 | tf_op jit(solution)/shard_map/ppermute | solution.py:47
  17.5 7.3 %collective-permute-start.7 = (bf16[384,128]{1,0:T(8,128)(2,1)S(1)}, bf16[384,128]{1,0:T(8,128)(2,1)S(1)}, u32[]{:S(2)}, u32[]{:S(2)}) collective-permute-start(bf16[384,128]{1,0:T(8,128)(2,1)S(1)} %get-tuple-element.47), channel_id=1, source_target_pairs={{0,1},{1,0},{2,3},{3,2},{4,5},{5,4},{6,7},{7,6},{8,9},{9,8},{10,11... | collective-permute-start | bytes 294920 | tf_op jit(solution)/shard_map/ppermute | solution.py:47
  20.8 4.0 %collective-permute-start.4 = (bf16[192,128]{1,0:T(8,128)(2,1)S(1)}, bf16[192,128]{1,0:T(8,128)(2,1)S(1)}, u32[]{:S(2)}, u32[]{:S(2)}) collective-permute-start(bf16[192,128]{1,0:T(8,128)(2,1)S(1)} %get-tuple-element.44), channel_id=1, source_target_pairs={{0,24},{8,16},{16,8},{24,0},{1,25},{9,17},{17,9},{25,1},{2,26},{10... | collective-permute-start | bytes 147464 | tf_op jit(solution)/shard_map/ppermute | solution.py:47
  20.9 4.0 %collective-permute-start.5 = (bf16[192,128]{1,0:T(8,128)(2,1)S(1)}, bf16[192,128]{1,0:T(8,128)(2,1)S(1)}, u32[]{:S(2)}, u32[]{:S(2)}) collective-permute-start(bf16[192,128]{1,0:T(8,128)(2,1)S(1)} %get-tuple-element.45), channel_id=1, source_target_pairs={{0,8},{8,0},{16,24},{24,16},{1,9},{9,1},{17,25},{25,17},{2,10},{10... | collective-permute-start | bytes 147464 | tf_op jit(solution)/shard_map/ppermute | solution.py:47
  27.3 6.4 %collective-permute-start.8 = (f32[6,128]{1,0:T(8,128)S(1)}, f32[6,128]{1,0:T(8,128)S(1)}, u32[]{:S(2)}, u32[]{:S(2)}) collective-permute-start(f32[6,128]{1,0:T(8,128)S(1)} %get-tuple-element.60), channel_id=1, source_target_pairs={{0,7},{1,2},{2,1},{3,4},{4,3},{5,6},{6,5},{7,0},{8,15},{9,10},{10,... | collective-permute-start | bytes 9224 | tf_op jit(solution)/shard_map/ppermute | solution.py:47
  29.1 4.5 %collective-permute-start.9 = (f32[6,128]{1,0:T(8,128)S(1)}, f32[6,128]{1,0:T(8,128)S(1)}, u32[]{:S(2)}, u32[]{:S(2)}) collective-permute-start(f32[6,128]{1,0:T(8,128)S(1)} %get-tuple-element.61), channel_id=1, source_target_pairs={{0,1},{1,0},{2,3},{3,2},{4,5},{5,4},{6,7},{7,6},{8,9},{9,8},{10,11... | collective-permute-start | bytes 9224 | tf_op jit(solution)/shard_map/ppermute | solution.py:47
  33.7 3.1 %collective-permute-start.10 = (f32[6,128]{1,0:T(8,128)S(1)}, f32[6,128]{1,0:T(8,128)S(1)}, u32[]{:S(2)}, u32[]{:S(2)}) collective-permute-start(f32[6,128]{1,0:T(8,128)S(1)} %pad_maximum_fusion.3), channel_id=1, source_target_pairs={{0,24},{8,16},{16,8},{24,0},{1,25},{9,17},{17,9},{25,1},{2,26},{10... | collective-permute-start | bytes 9224 | tf_op jit(solution)/shard_map/ppermute | solution.py:47
  33.7 3.0 %collective-permute-start.11 = (f32[6,128]{1,0:T(8,128)S(1)}, f32[6,128]{1,0:T(8,128)S(1)}, u32[]{:S(2)}, u32[]{:S(2)}) collective-permute-start(f32[6,128]{1,0:T(8,128)S(1)} %pad_maximum_fusion.4), channel_id=1, source_target_pairs={{0,8},{8,0},{16,24},{24,16},{1,9},{9,1},{17,25},{25,17},{2,10},{10... | collective-permute-start | bytes 9224 | tf_op jit(solution)/shard_map/ppermute | solution.py:47

commit v8 on v7

--- a/solution.py
+++ b/solution.py
@@ -152,24 +152,19 @@
     for copy in copies:
         copy.start()
 
-    def transpose(step, carry):
-        for k in range(TURN):
-            turned[step * TURN + k] = weight[step * TURN + k].T
-        return carry
-
-    lax.fori_loop(0, weight.shape[0] // TURN, transpose, 0)
     counted = tile_count[0]
 
-    def index(step, carry):
+    def turn_and_index(step, carry):
         for k in range(TURN):
             t = step * TURN + k
+            turned[t] = weight[t].T
             x, j = split_device(tile_cell[t], columns)
             slots[t] = jnp.where(t < counted, local_slot(tile_slot[t], pos_x, pos_y, size_y), 9 * CAP)
             spots[t] = (j + 1) * (count * tall) + x + PAD
             points[t] = j * width + x
         return carry
 
-    lax.fori_loop(0, weight.shape[0] // TURN, index, 0)
+    lax.fori_loop(0, weight.shape[0] // TURN, turn_and_index, 0)
     for copy in copies:
         copy.wait()
 
@@ -441,7 +436,7 @@
 
 
 def outer_kernel(
-    props, slots, points, edge_x1, edge_x2, edge_y1, edge_y2, weight, state_in, speed_in, press_in,
+    props, slots, points, edge_x1, edge_x2, edge_y2, edge_y1, weight, state_in, speed_in, press_in,
     fresh_in, remapped, state, speed, press, fresh, own, first, second, sums, sem, *, size_x, size_y
 ):
     pos_x, pos_y = lax.axis_index("gx"), lax.axis_index("gy")
@@ -654,8 +649,8 @@
     edges = (
         swap(edges[0], "gx", 1),
         swap(edges[1], "gx", 2),
+        swap(edges[3], "gy", 2),
         swap(edges[2], "gy", 1, wrap=False),
-        swap(edges[3], "gy", 2),
     )
     fresh, press, speed = inner(mat_props, state, cell_state.shape[1])
     remapped, state, speed, fresh, own, first, second = outer(

time: 37.6 us -> 36.3 us (0.965)
  starting transfers between devices: 17.8 us -> 17.2 us
  waiting for transfers between devices: 2.54 us -> 2.07 us
    ppermute x12, starting transfers between devices: 17.8 us -> 17.2 us  [swap(): return lax.ppermute(value, axis, pairs)]
    ppermute x12, waiting for transfers between devices: 2.54 us -> 2.07 us  [swap(): return lax.ppermute(value, axis, pairs)]
where the time goes in v8:
time: 36.3 us; the launch traced here: 36 us
  starting transfers between devices  17.2 us (47%)
  Pallas kernels  15.2 us (42%)
  waiting for transfers between devices  2.07 us (6%)
  between operations  1.5 us (4%)
    ppermute x12, starting transfers between devices, swap(): return lax.ppermute(value, axis, pairs)  17.2 us
    pallas_call x1, Pallas kernels, stage(): pl.pallas_call(functools.partial(stage_kernel, size_y=size_y), name='stag...  3.04 us
    pallas_call x1, Pallas kernels, inner(): pl.pallas_call(inner_kernel, name='inner', out_shape=(pltpu.VMEM((count,...  2.7 us
    pallas_call x1, Pallas kernels, outer(): pl.pallas_call(functools.partial(outer_kernel, size_x=size_x, size_y=size...  2.4 us
    pallas_call x1, Pallas kernels, fetch(): pl.pallas_call(fetch_kernel, name='fetch', out_shape=pltpu.VMEM(value.sha...  2.2 us
    pallas_call x1, Pallas kernels, late(): pl.pallas_call(late_kernel, name='late', out_shape=(jax.ShapeDtypeStruct(...  2.13 us
    ppermute x12, waiting for transfers between devices, swap(): return lax.ppermute(value, axis, pairs)  2.07 us
    pallas_call x1, Pallas kernels, deposit(): pl.pallas_call(deposit_kernel, name='deposit', out_shape=(pltpu.VMEM(stat...  1.1 us
  transfers between devices with their start and end apart: 12, of which 2 were waited for; matrix products, arithmetic and copies ran while one was open for 0% of the time, Pallas kernels for 28%

profile of v8, /device:TPU:0, one launch (start us, length us, event | category | flops | bytes accessed | tf_op | source)
XLA Modules:
  0.0 36.0 jit_solution(11678635171582001642)
XLA Ops:
  0.6 1.0 %payload.1 = (bf16[6,16,128]{2,1,0:T(8,128)(2,1)S(1)}, bf16[6,16,128]{2,1,0:T(8,128)(2,1)S(1)}, bf16[6,16,128]{2,1,0:T(8,128)(2,1)S(1)}, s32[18]{0:T(128)S(4)}, ...) custom-call(s32[18]{0:T(128)} %dest_hbm.1, f32[2,8]{1,0:T(2,128)} %props_hbm.1, f32[18,128]{1,0:T(8,128)} %bitcast.4, ...), custom_call_target="tpu_custom_call" | custom-call | tf_op jit(solution)/shard_map/payload/pallas_call | solution.py:112
  1.7 2.5 %collective-permute-start = (bf16[6,16,128]{2,1,0:T(8,128)(2,1)S(1)}, bf16[6,16,128]{2,1,0:T(8,128)(2,1)S(1)}, u32[]{:S(2)}, u32[]{:S(2)}) collective-permute-start(bf16[6,16,128]{2,1,0:T(8,128)(2,1)S(1)} %get-tuple-element.41), channel_id=1, source_target_pairs={{0,24},{8,16},{16,8},{24,0},{1,25},{9,17},{17,9},{25,1},{2,26},{10... | collective-permute-start | bytes 73736 | tf_op jit(solution)/shard_map/ppermute | solution.py:47
  4.2 0.7 %collective-permute-start.1 = (bf16[6,16,128]{2,1,0:T(8,128)(2,1)S(1)}, bf16[6,16,128]{2,1,0:T(8,128)(2,1)S(1)}, u32[]{:S(2)}, u32[]{:S(2)}) collective-permute-start(bf16[6,16,128]{2,1,0:T(8,128)(2,1)S(1)} %get-tuple-element.42), channel_id=1, source_target_pairs={{0,8},{8,0},{16,24},{24,16},{1,9},{9,1},{17,25},{25,17},{2,10},{10... | collective-permute-start | bytes 73736 | tf_op jit(solution)/shard_map/ppermute | solution.py:47
  4.8 2.2 %fetch.1.weight = bf16[128,128,128]{2,1,0:T(8,128)(2,1)S(1)} custom-call(bf16[128,128,128]{2,1,0:T(8,128)(2,1)} %source.1), custom_call_target="tpu_custom_call" | custom-call | bytes 8388608 | tf_op jit(solution)/shard_map/fetch/pallas_call | solution.py:201
  7.0 0.0 collective-permute-done.first
  7.1 0.0 collective-permute-done.1.second
  7.1 4.6 %collective-permute-start.2 = (bf16[6,16,128]{2,1,0:T(8,128)(2,1)S(1)}, bf16[6,16,128]{2,1,0:T(8,128)(2,1)S(1)}, u32[]{:S(2)}, u32[]{:S(2)}) collective-permute-start(bf16[6,16,128]{2,1,0:T(8,128)(2,1)S(1)} %pad_maximum_fusion), channel_id=1, source_target_pairs={{0,7},{1,2},{2,1},{3,4},{4,3},{5,6},{6,5},{7,0},{8,15},{9,10},{10,... | collective-permute-start | bytes 73736 | tf_op jit(solution)/shard_map/ppermute | solution.py:47
  11.7 0.0 collective-permute-start.3
  12.4 3.0 %stage.1 = (f32[18,12,88,128]{3,2,1,0:T(8,128)S(1)}, bf16[128,128,128]{2,1,0:T(8,128)(2,1)S(1)}, s32[128]{0:T(128)S(4)}, s32[128]{0:T(128)S(4)}, s32[128]{0:T(128)S(4)}) custom-call(s32[128]{0:T(128)S(4)} %get-tuple-element.33.tile_slot, s32[128]{0:T(128)S(4)} %get-tuple-element.34.tile_cell, s32[1]{0:T(128)S(6)} %copy.27.tile_count, f32[12,64,2048]{2,1,0:T(8,128)} %cell.1, ...), custom_call_target="tpu_custom_call" | custom-call | bytes 12582912 | tf_op jit(solution)/shard_map/stage/pallas_call | solution.py:176
  15.4 0.0 collective-permute-done.2.south
  15.4 0.1 collective-permute-done.3.north
  15.5 1.1 %deposit.1 = (f32[18,12,88,128]{3,2,1,0:T(8,128)S(1)}, bf16[192,128]{1,0:T(8,128)(2,1)S(1)}, bf16[192,128]{1,0:T(8,128)(2,1)S(1)}, bf16[384,128]{1,0:T(8,128)(2,1)S(1)}, bf16[384,128]{1,0:T(8,128)(2,1)S(1)}) custom-call(s32[128]{0:T(128)S(4)} %get-tuple-element.37.slots, s32[128]{0:T(128)S(4)} %get-tuple-element.39.spots, ...), custom_call_target="tpu_custom_call", output_to_operand_aliasing={{0}: (8, {})} | custom-call | tf_op jit(solution)/shard_map/deposit/pallas_call | solution.py:289
  16.6 2.0 %collective-permute-start.6 = (bf16[384,128]{1,0:T(8,128)(2,1)S(1)}, bf16[384,128]{1,0:T(8,128)(2,1)S(1)}, u32[]{:S(2)}, u32[]{:S(2)}) collective-permute-start(bf16[384,128]{1,0:T(8,128)(2,1)S(1)} %get-tuple-element.46), channel_id=1, source_target_pairs={{0,1},{1,0},{2,3},{3,2},{4,5},{5,4},{6,7},{7,6},{8,9},{9,8},{10,11... | collective-permute-start | bytes 294920 | tf_op jit(solution)/shard_map/ppermute | solution.py:47
  18.6 0.7 %collective-permute-start.7 = (bf16[384,128]{1,0:T(8,128)(2,1)S(1)}, bf16[384,128]{1,0:T(8,128)(2,1)S(1)}, u32[]{:S(2)}, u32[]{:S(2)}) collective-permute-start(bf16[384,128]{1,0:T(8,128)(2,1)S(1)} %get-tuple-element.47), channel_id=1, source_target_pairs={{0,0},{1,2},{2,1},{3,4},{4,3},{5,6},{6,5},{7,7},{8,8},{9,10},{10,9... | collective-permute-start | bytes 294920 | tf_op jit(solution)/shard_map/ppermute | solution.py:47
  19.3 0.1 collective-permute-start.4
  19.4 1.2 %collective-permute-start.5 = (bf16[192,128]{1,0:T(8,128)(2,1)S(1)}, bf16[192,128]{1,0:T(8,128)(2,1)S(1)}, u32[]{:S(2)}, u32[]{:S(2)}) collective-permute-start(bf16[192,128]{1,0:T(8,128)(2,1)S(1)} %get-tuple-element.45), channel_id=1, source_target_pairs={{0,8},{8,0},{16,24},{24,16},{1,9},{9,1},{17,25},{25,17},{2,10},{10... | collective-permute-start | bytes 147464 | tf_op jit(solution)/shard_map/ppermute | solution.py:47
  20.6 2.7 %inner.1 = (f32[12,64,2048]{2,1,0:T(8,128)S(1)}, f32[16,64,128]{2,1,0:T(8,128)S(1)}, f32[18,3,88,128]{3,2,1,0:T(8,128)S(1)}) custom-call(f32[2,8]{1,0:T(2,128)S(4)} %get-tuple-element.32.props, f32[18,12,88,128]{3,2,1,0:T(8,128)S(1)} %get-tuple-element.49.state.state_in), custom_call_target="tpu_custom_call" | custom-call | flops 48660480 | bytes 19464192 | tf_op jit(solution)/shard_map/inner/pallas_call | solution.py:423
  23.3 0.0 collective-permute-done.4.edge_x1
  23.3 0.0 collective-permute-done.5.edge_x2
  23.3 0.0 collective-permute-done.6.edge_y2
  23.3 0.0 collective-permute-done.7.edge_y1
  23.4 2.4 %outer.1 = (f32[12,64,2048]{2,1,0:T(8,128)}, f32[18,12,88,128]{3,2,1,0:T(8,128)S(1)}, f32[18,3,88,128]{3,2,1,0:T(8,128)S(1)}, f32[16,64,128]{2,1,0:T(8,128)S(1)}...) custom-call(f32[2,8]{1,0:T(2,128)S(4)} %get-tuple-element.32.props, ...), custom_call_target="tpu_custom_call", output_to_operand_aliasing={{1}: (8, {}), {2}: (9, {}), {3}: (10, {}), {4}: (11, {})} | custom-call | tf_op jit(solution)/shard_map/outer/pallas_call | solution.py:510
  25.8 0.9 %collective-permute-start.8 = (f32[6,128]{1,0:T(8,128)S(1)}, f32[6,128]{1,0:T(8,128)S(1)}, u32[]{:S(2)}, u32[]{:S(2)}) collective-permute-start(f32[6,128]{1,0:T(8,128)S(1)} %get-tuple-element.60), channel_id=1, source_target_pairs={{0,7},{1,2},{2,1},{3,4},{4,3},{5,6},{6,5},{7,0},{8,15},{9,10},{10,... | collective-permute-start | bytes 9224 | tf_op jit(solution)/shard_map/ppermute | solution.py:47
  26.7 3.5 %collective-permute-start.9 = (f32[6,128]{1,0:T(8,128)S(1)}, f32[6,128]{1,0:T(8,128)S(1)}, u32[]{:S(2)}, u32[]{:S(2)}) collective-permute-start(f32[6,128]{1,0:T(8,128)S(1)} %get-tuple-element.61), channel_id=1, source_target_pairs={{0,1},{1,0},{2,3},{3,2},{4,5},{5,4},{6,7},{7,6},{8,9},{9,8},{10,11... | collective-permute-start | bytes 9224 | tf_op jit(solution)/shard_map/ppermute | solution.py:47
  30.1 2.1 %late.1 = (f32[12,64,2048]{2,1,0:T(8,128)}, f32[12,64,2048]{2,1,0:T(8,128)S(1)}) custom-call(f32[18,12,88,128]{3,2,1,0:T(8,128)S(1)} %get-tuple-element.53.state, f32[18,3,88,128]{3,2,1,0:T(8,128)S(1)} %get-tuple-element.54.speed, f32[12,64,2048]{2,1,0:T(8,128)S(1)} %get-tuple-element.55.fresh_in, ...), custom_call_target="tpu_custom_call", output_to_operand_aliasing={{1}: (2, {}), {0}: (3, {})} | custom-call | flops 12165120 | bytes 19464192 | tf_op jit(solution)/shard_map/late/pallas_call | solution.py:570
  32.2 0.0 collective-permute-done.8
  32.3 0.0 collective-permute-done.9
  32.3 0.1 collective-permute-start.10
  32.4 1.1 %collective-permute-start.11 = (f32[6,128]{1,0:T(8,128)S(1)}, f32[6,128]{1,0:T(8,128)S(1)}, u32[]{:S(2)}, u32[]{:S(2)}) collective-permute-start(f32[6,128]{1,0:T(8,128)S(1)} %pad_maximum_fusion.4), channel_id=1, source_target_pairs={{0,8},{8,0},{16,24},{24,16},{1,9},{9,1},{17,25},{25,17},{2,10},{10... | collective-permute-start | bytes 9224 | tf_op jit(solution)/shard_map/ppermute | solution.py:47
  33.5 1.9 %collective-permute-done.10.first = f32[6,128]{1,0:T(8,128)S(1)} collective-permute-done((f32[6,128]{1,0:T(8,128)S(1)}, f32[6,128]{1,0:T(8,128)S(1)}, u32[]{:S(2)}, u32[]{:S(2)}) %collective-permute-start.10) | collective-permute-done | bytes 3104 | tf_op jit(solution)/shard_map/ppermute | solution.py:47
  35.4 0.0 collective-permute-done.11.second
  35.4 0.6 %pick.1 = bf16[18,128]{1,0:T(8,128)(2,1)} custom-call(s32[18]{0:T(128)S(4)} %get-tuple-element.58.place, f32[6,128]{1,0:T(8,128)S(1)} %pad_maximum_fusion.2.own, f32[6,128]{1,0:T(8,128)S(1)} %collective-permute-done.10.first, f32[6,128]{1,0:T(8,128)S(1)} %collective-permute-done.11.second), custom_call_target="tpu_custom_call" | custom-call | tf_op jit(solution)/shard_map/pick/pallas_call | solution.py:593
  (11 shorter events, 0.1 us)
Async XLA Ops:
  1.7 5.4 %collective-permute-start = (bf16[6,16,128]{2,1,0:T(8,128)(2,1)S(1)}, bf16[6,16,128]{2,1,0:T(8,128)(2,1)S(1)}, u32[]{:S(2)}, u32[]{:S(2)}) collective-permute-start(bf16[6,16,128]{2,1,0:T(8,128)(2,1)S(1)} %get-tuple-element.41), channel_id=1, source_target_pairs={{0,24},{8,16},{16,8},{24,0},{1,25},{9,17},{17,9},{25,1},{2,26},{10... | collective-permute-start | bytes 73736 | tf_op jit(solution)/shard_map/ppermute | solution.py:47
  4.2 2.9 %collective-permute-start.1 = (bf16[6,16,128]{2,1,0:T(8,128)(2,1)S(1)}, bf16[6,16,128]{2,1,0:T(8,128)(2,1)S(1)}, u32[]{:S(2)}, u32[]{:S(2)}) collective-permute-start(bf16[6,16,128]{2,1,0:T(8,128)(2,1)S(1)} %get-tuple-element.42), channel_id=1, source_target_pairs={{0,8},{8,0},{16,24},{24,16},{1,9},{9,1},{17,25},{25,17},{2,10},{10... | collective-permute-start | bytes 73736 | tf_op jit(solution)/shard_map/ppermute | solution.py:47
  7.1 8.3 %collective-permute-start.2 = (bf16[6,16,128]{2,1,0:T(8,128)(2,1)S(1)}, bf16[6,16,128]{2,1,0:T(8,128)(2,1)S(1)}, u32[]{:S(2)}, u32[]{:S(2)}) collective-permute-start(bf16[6,16,128]{2,1,0:T(8,128)(2,1)S(1)} %pad_maximum_fusion), channel_id=1, source_target_pairs={{0,7},{1,2},{2,1},{3,4},{4,3},{5,6},{6,5},{7,0},{8,15},{9,10},{10,... | collective-permute-start | bytes 73736 | tf_op jit(solution)/shard_map/ppermute | solution.py:47
  11.7 3.8 %collective-permute-start.3 = (bf16[6,16,128]{2,1,0:T(8,128)(2,1)S(1)}, bf16[6,16,128]{2,1,0:T(8,128)(2,1)S(1)}, u32[]{:S(2)}, u32[]{:S(2)}) collective-permute-start(bf16[6,16,128]{2,1,0:T(8,128)(2,1)S(1)} %pad_maximum_fusion.1), channel_id=1, source_target_pairs={{0,1},{1,0},{2,3},{3,2},{4,5},{5,4},{6,7},{7,6},{8,9},{9,8},{10,11... | collective-permute-start | bytes 73736 | tf_op jit(solution)/shard_map/ppermute | solution.py:47
  16.6 6.7 %collective-permute-start.6 = (bf16[384,128]{1,0:T(8,128)(2,1)S(1)}, bf16[384,128]{1,0:T(8,128)(2,1)S(1)}, u32[]{:S(2)}, u32[]{:S(2)}) collective-permute-start(bf16[384,128]{1,0:T(8,128)(2,1)S(1)} %get-tuple-element.46), channel_id=1, source_target_pairs={{0,1},{1,0},{2,3},{3,2},{4,5},{5,4},{6,7},{7,6},{8,9},{9,8},{10,11... | collective-permute-start | bytes 294920 | tf_op jit(solution)/shard_map/ppermute | solution.py:47
  18.6 4.7 %collective-permute-start.7 = (bf16[384,128]{1,0:T(8,128)(2,1)S(1)}, bf16[384,128]{1,0:T(8,128)(2,1)S(1)}, u32[]{:S(2)}, u32[]{:S(2)}) collective-permute-start(bf16[384,128]{1,0:T(8,128)(2,1)S(1)} %get-tuple-element.47), channel_id=1, source_target_pairs={{0,0},{1,2},{2,1},{3,4},{4,3},{5,6},{6,5},{7,7},{8,8},{9,10},{10,9... | collective-permute-start | bytes 294920 | tf_op jit(solution)/shard_map/ppermute | solution.py:47
  19.3 4.0 %collective-permute-start.4 = (bf16[192,128]{1,0:T(8,128)(2,1)S(1)}, bf16[192,128]{1,0:T(8,128)(2,1)S(1)}, u32[]{:S(2)}, u32[]{:S(2)}) collective-permute-start(bf16[192,128]{1,0:T(8,128)(2,1)S(1)} %get-tuple-element.44), channel_id=1, source_target_pairs={{0,24},{8,16},{16,8},{24,0},{1,25},{9,17},{17,9},{25,1},{2,26},{10... | collective-permute-start | bytes 147464 | tf_op jit(solution)/shard_map/ppermute | solution.py:47
  19.4 4.0 %collective-permute-start.5 = (bf16[192,128]{1,0:T(8,128)(2,1)S(1)}, bf16[192,128]{1,0:T(8,128)(2,1)S(1)}, u32[]{:S(2)}, u32[]{:S(2)}) collective-permute-start(bf16[192,128]{1,0:T(8,128)(2,1)S(1)} %get-tuple-element.45), channel_id=1, source_target_pairs={{0,8},{8,0},{16,24},{24,16},{1,9},{9,1},{17,25},{25,17},{2,10},{10... | collective-permute-start | bytes 147464 | tf_op jit(solution)/shard_map/ppermute | solution.py:47
  25.8 6.5 %collective-permute-start.8 = (f32[6,128]{1,0:T(8,128)S(1)}, f32[6,128]{1,0:T(8,128)S(1)}, u32[]{:S(2)}, u32[]{:S(2)}) collective-permute-start(f32[6,128]{1,0:T(8,128)S(1)} %get-tuple-element.60), channel_id=1, source_target_pairs={{0,7},{1,2},{2,1},{3,4},{4,3},{5,6},{6,5},{7,0},{8,15},{9,10},{10,... | collective-permute-start | bytes 9224 | tf_op jit(solution)/shard_map/ppermute | solution.py:47
  26.7 5.6 %collective-permute-start.9 = (f32[6,128]{1,0:T(8,128)S(1)}, f32[6,128]{1,0:T(8,128)S(1)}, u32[]{:S(2)}, u32[]{:S(2)}) collective-permute-start(f32[6,128]{1,0:T(8,128)S(1)} %get-tuple-element.61), channel_id=1, source_target_pairs={{0,1},{1,0},{2,3},{3,2},{4,5},{5,4},{6,7},{7,6},{8,9},{9,8},{10,11... | collective-permute-start | bytes 9224 | tf_op jit(solution)/shard_map/ppermute | solution.py:47
  32.3 3.1 %collective-permute-start.10 = (f32[6,128]{1,0:T(8,128)S(1)}, f32[6,128]{1,0:T(8,128)S(1)}, u32[]{:S(2)}, u32[]{:S(2)}) collective-permute-start(f32[6,128]{1,0:T(8,128)S(1)} %pad_maximum_fusion.3), channel_id=1, source_target_pairs={{0,24},{8,16},{16,8},{24,0},{1,25},{9,17},{17,9},{25,1},{2,26},{10... | collective-permute-start | bytes 9224 | tf_op jit(solution)/shard_map/ppermute | solution.py:47
  32.4 3.0 %collective-permute-start.11 = (f32[6,128]{1,0:T(8,128)S(1)}, f32[6,128]{1,0:T(8,128)S(1)}, u32[]{:S(2)}, u32[]{:S(2)}) collective-permute-start(f32[6,128]{1,0:T(8,128)S(1)} %pad_maximum_fusion.4), channel_id=1, source_target_pairs={{0,8},{8,0},{16,24},{24,16},{1,9},{9,1},{17,25},{25,17},{2,10},{10... | collective-permute-start | bytes 9224 | tf_op jit(solution)/shard_map/ppermute | solution.py:47

commit v9 on v8

--- a/solution.py
+++ b/solution.py
@@ -237,7 +237,7 @@
 
 
 def deposit_kernel(
-    slots, spots, own, first, second, south, north, weight, state_in,
+    slots, spots, own, first, second, north, south, weight, state_in,
     state, edge_x1, edge_x2, edge_y1, edge_y2, rows
 ):
     pos_x, pos_y = lax.axis_index("gx"), lax.axis_index("gy")
@@ -644,7 +644,7 @@
     south = swap(along_y(1), "gy", 1)
     north = swap(along_y(2), "gy", 2)
     state, *edges = deposit(
-        slots, spots, (own, first, second, south, north), weight, state
+        slots, spots, (own, first, second, north, south), weight, state
     )
     edges = (
         swap(edges[0], "gx", 1),

time: 36.3 us -> 36.7 us (1.011)
  starting transfers between devices: 17.2 us -> 17.7 us
    ppermute x12, starting transfers between devices: 17.2 us -> 17.7 us  [swap(): return lax.ppermute(value, axis, pairs)]
  transfers between devices with their start and end apart: 12 -> 12, of which waited for: 2 -> 1; matrix products, arithmetic and copies ran while one was open for 0% -> 0% of each run, Pallas kernels for 28% -> 28%
where the time goes in v9:
time: 36.7 us; the launch traced here: 36.5 us
  starting transfers between devices  17.7 us (48%)
  Pallas kernels  15.3 us (42%)
  waiting for transfers between devices  1.97 us (5%)
  between operations  1.51 us (4%)
    ppermute x12, starting transfers between devices, swap(): return lax.ppermute(value, axis, pairs)  17.7 us
    pallas_call x1, Pallas kernels, stage(): pl.pallas_call(functools.partial(stage_kernel, size_y=size_y), name='stag...  3.04 us
    pallas_call x1, Pallas kernels, inner(): pl.pallas_call(inner_kernel, name='inner', out_shape=(pltpu.VMEM((count,...  2.7 us
    pallas_call x1, Pallas kernels, outer(): pl.pallas_call(functools.partial(outer_kernel, size_x=size_x, size_y=size...  2.43 us
    pallas_call x1, Pallas kernels, fetch(): pl.pallas_call(fetch_kernel, name='fetch', out_shape=pltpu.VMEM(value.sha...  2.2 us
    pallas_call x1, Pallas kernels, late(): pl.pallas_call(late_kernel, name='late', out_shape=(jax.ShapeDtypeStruct(...  2.13 us
    ppermute x12, waiting for transfers between devices, swap(): return lax.ppermute(value, axis, pairs)  1.97 us
    pallas_call x1, Pallas kernels, deposit(): pl.pallas_call(deposit_kernel, name='deposit', out_shape=(pltpu.VMEM(stat...  1.11 us
  transfers between devices with their start and end apart: 12, of which 1 were waited for; matrix products, arithmetic and copies ran while one was open for 0% of the time, Pallas kernels for 28%

profile of v9, /device:TPU:0, one launch (start us, length us, event | category | flops | bytes accessed | tf_op | source)
XLA Modules:
  0.0 36.5 jit_solution(5287850388942709144)
XLA Ops:
  0.6 1.0 %payload.1 = (bf16[6,16,128]{2,1,0:T(8,128)(2,1)S(1)}, bf16[6,16,128]{2,1,0:T(8,128)(2,1)S(1)}, bf16[6,16,128]{2,1,0:T(8,128)(2,1)S(1)}, s32[18]{0:T(128)S(4)}, ...) custom-call(s32[18]{0:T(128)} %dest_hbm.1, f32[2,8]{1,0:T(2,128)} %props_hbm.1, f32[18,128]{1,0:T(8,128)} %bitcast.4, ...), custom_call_target="tpu_custom_call" | custom-call | tf_op jit(solution)/shard_map/payload/pallas_call | solution.py:112
  1.7 2.5 %collective-permute-start = (bf16[6,16,128]{2,1,0:T(8,128)(2,1)S(1)}, bf16[6,16,128]{2,1,0:T(8,128)(2,1)S(1)}, u32[]{:S(2)}, u32[]{:S(2)}) collective-permute-start(bf16[6,16,128]{2,1,0:T(8,128)(2,1)S(1)} %get-tuple-element.41), channel_id=1, source_target_pairs={{0,24},{8,16},{16,8},{24,0},{1,25},{9,17},{17,9},{25,1},{2,26},{10... | collective-permute-start | bytes 73736 | tf_op jit(solution)/shard_map/ppermute | solution.py:47
  4.2 0.7 %collective-permute-start.1 = (bf16[6,16,128]{2,1,0:T(8,128)(2,1)S(1)}, bf16[6,16,128]{2,1,0:T(8,128)(2,1)S(1)}, u32[]{:S(2)}, u32[]{:S(2)}) collective-permute-start(bf16[6,16,128]{2,1,0:T(8,128)(2,1)S(1)} %get-tuple-element.42), channel_id=1, source_target_pairs={{0,8},{8,0},{16,24},{24,16},{1,9},{9,1},{17,25},{25,17},{2,10},{10... | collective-permute-start | bytes 73736 | tf_op jit(solution)/shard_map/ppermute | solution.py:47
  4.8 2.2 %fetch.1.weight = bf16[128,128,128]{2,1,0:T(8,128)(2,1)S(1)} custom-call(bf16[128,128,128]{2,1,0:T(8,128)(2,1)} %source.1), custom_call_target="tpu_custom_call" | custom-call | bytes 8388608 | tf_op jit(solution)/shard_map/fetch/pallas_call | solution.py:201
  7.0 0.0 collective-permute-done.first
  7.1 0.0 collective-permute-done.1.second
  7.1 1.6 %collective-permute-start.2 = (bf16[6,16,128]{2,1,0:T(8,128)(2,1)S(1)}, bf16[6,16,128]{2,1,0:T(8,128)(2,1)S(1)}, u32[]{:S(2)}, u32[]{:S(2)}) collective-permute-start(bf16[6,16,128]{2,1,0:T(8,128)(2,1)S(1)} %pad_maximum_fusion), channel_id=1, source_target_pairs={{0,1},{1,0},{2,3},{3,2},{4,5},{5,4},{6,7},{7,6},{8,9},{9,8},{10,11... | collective-permute-start | bytes 73736 | tf_op jit(solution)/shard_map/ppermute | solution.py:47
  8.7 3.6 %collective-permute-start.3 = (bf16[6,16,128]{2,1,0:T(8,128)(2,1)S(1)}, bf16[6,16,128]{2,1,0:T(8,128)(2,1)S(1)}, u32[]{:S(2)}, u32[]{:S(2)}) collective-permute-start(bf16[6,16,128]{2,1,0:T(8,128)(2,1)S(1)} %pad_maximum_fusion.1), channel_id=1, source_target_pairs={{0,7},{1,2},{2,1},{3,4},{4,3},{5,6},{6,5},{7,0},{8,15},{9,10},{10,... | collective-permute-start | bytes 73736 | tf_op jit(solution)/shard_map/ppermute | solution.py:47
  12.9 3.0 %stage.1 = (f32[18,12,88,128]{3,2,1,0:T(8,128)S(1)}, bf16[128,128,128]{2,1,0:T(8,128)(2,1)S(1)}, s32[128]{0:T(128)S(4)}, s32[128]{0:T(128)S(4)}, s32[128]{0:T(128)S(4)}) custom-call(s32[128]{0:T(128)S(4)} %get-tuple-element.33.tile_slot, s32[128]{0:T(128)S(4)} %get-tuple-element.34.tile_cell, s32[1]{0:T(128)S(6)} %copy.27.tile_count, f32[12,64,2048]{2,1,0:T(8,128)} %cell.1, ...), custom_call_target="tpu_custom_call" | custom-call | bytes 12582912 | tf_op jit(solution)/shard_map/stage/pallas_call | solution.py:176
  15.9 0.0 collective-permute-done.2.north
  15.9 0.0 collective-permute-done.3.south
  16.0 1.1 %deposit.1 = (f32[18,12,88,128]{3,2,1,0:T(8,128)S(1)}, bf16[192,128]{1,0:T(8,128)(2,1)S(1)}, bf16[192,128]{1,0:T(8,128)(2,1)S(1)}, bf16[384,128]{1,0:T(8,128)(2,1)S(1)}, bf16[384,128]{1,0:T(8,128)(2,1)S(1)}) custom-call(s32[128]{0:T(128)S(4)} %get-tuple-element.37.slots, s32[128]{0:T(128)S(4)} %get-tuple-element.39.spots, ...), custom_call_target="tpu_custom_call", output_to_operand_aliasing={{0}: (8, {})} | custom-call | tf_op jit(solution)/shard_map/deposit/pallas_call | solution.py:289
  17.1 0.1 collective-permute-start.6
  17.2 0.7 %collective-permute-start.7 = (bf16[384,128]{1,0:T(8,128)(2,1)S(1)}, bf16[384,128]{1,0:T(8,128)(2,1)S(1)}, u32[]{:S(2)}, u32[]{:S(2)}) collective-permute-start(bf16[384,128]{1,0:T(8,128)(2,1)S(1)} %get-tuple-element.47), channel_id=1, source_target_pairs={{0,0},{1,2},{2,1},{3,4},{4,3},{5,6},{6,5},{7,7},{8,8},{9,10},{10,9... | collective-permute-start | bytes 294920 | tf_op jit(solution)/shard_map/ppermute | solution.py:47
  17.8 0.4 collective-permute-start.4
  18.2 0.9 %collective-permute-start.5 = (bf16[192,128]{1,0:T(8,128)(2,1)S(1)}, bf16[192,128]{1,0:T(8,128)(2,1)S(1)}, u32[]{:S(2)}, u32[]{:S(2)}) collective-permute-start(bf16[192,128]{1,0:T(8,128)(2,1)S(1)} %get-tuple-element.45), channel_id=1, source_target_pairs={{0,8},{8,0},{16,24},{24,16},{1,9},{9,1},{17,25},{25,17},{2,10},{10... | collective-permute-start | bytes 147464 | tf_op jit(solution)/shard_map/ppermute | solution.py:47
  19.1 2.7 %inner.1 = (f32[12,64,2048]{2,1,0:T(8,128)S(1)}, f32[16,64,128]{2,1,0:T(8,128)S(1)}, f32[18,3,88,128]{3,2,1,0:T(8,128)S(1)}) custom-call(f32[2,8]{1,0:T(2,128)S(4)} %get-tuple-element.32.props, f32[18,12,88,128]{3,2,1,0:T(8,128)S(1)} %get-tuple-element.49.state.state_in), custom_call_target="tpu_custom_call" | custom-call | flops 48660480 | bytes 19464192 | tf_op jit(solution)/shard_map/inner/pallas_call | solution.py:423
  21.8 0.0 collective-permute-done.4.edge_x1
  21.8 0.0 collective-permute-done.5.edge_x2
  21.9 0.0 collective-permute-done.6.edge_y2
  21.9 0.0 collective-permute-done.7.edge_y1
  21.9 2.4 %outer.1 = (f32[12,64,2048]{2,1,0:T(8,128)}, f32[18,12,88,128]{3,2,1,0:T(8,128)S(1)}, f32[18,3,88,128]{3,2,1,0:T(8,128)S(1)}, f32[16,64,128]{2,1,0:T(8,128)S(1)}...) custom-call(f32[2,8]{1,0:T(2,128)S(4)} %get-tuple-element.32.props, ...), custom_call_target="tpu_custom_call", output_to_operand_aliasing={{1}: (8, {}), {2}: (9, {}), {3}: (10, {}), {4}: (11, {})} | custom-call | tf_op jit(solution)/shard_map/outer/pallas_call | solution.py:510
  24.3 2.9 %collective-permute-start.8 = (f32[6,128]{1,0:T(8,128)S(1)}, f32[6,128]{1,0:T(8,128)S(1)}, u32[]{:S(2)}, u32[]{:S(2)}) collective-permute-start(f32[6,128]{1,0:T(8,128)S(1)} %get-tuple-element.60), channel_id=1, source_target_pairs={{0,7},{1,2},{2,1},{3,4},{4,3},{5,6},{6,5},{7,0},{8,15},{9,10},{10,... | collective-permute-start | bytes 9224 | tf_op jit(solution)/shard_map/ppermute | solution.py:47
  27.2 3.4 %collective-permute-start.9 = (f32[6,128]{1,0:T(8,128)S(1)}, f32[6,128]{1,0:T(8,128)S(1)}, u32[]{:S(2)}, u32[]{:S(2)}) collective-permute-start(f32[6,128]{1,0:T(8,128)S(1)} %get-tuple-element.61), channel_id=1, source_target_pairs={{0,1},{1,0},{2,3},{3,2},{4,5},{5,4},{6,7},{7,6},{8,9},{9,8},{10,11... | collective-permute-start | bytes 9224 | tf_op jit(solution)/shard_map/ppermute | solution.py:47
  30.5 2.1 %late.1 = (f32[12,64,2048]{2,1,0:T(8,128)}, f32[12,64,2048]{2,1,0:T(8,128)S(1)}) custom-call(f32[18,12,88,128]{3,2,1,0:T(8,128)S(1)} %get-tuple-element.53.state, f32[18,3,88,128]{3,2,1,0:T(8,128)S(1)} %get-tuple-element.54.speed, f32[12,64,2048]{2,1,0:T(8,128)S(1)} %get-tuple-element.55.fresh_in, ...), custom_call_target="tpu_custom_call", output_to_operand_aliasing={{1}: (2, {}), {0}: (3, {})} | custom-call | flops 12165120 | bytes 19464192 | tf_op jit(solution)/shard_map/late/pallas_call | solution.py:570
  32.7 0.0 collective-permute-done.8
  32.7 0.0 collective-permute-done.9
  32.7 0.1 collective-permute-start.10
  32.8 1.1 %collective-permute-start.11 = (f32[6,128]{1,0:T(8,128)S(1)}, f32[6,128]{1,0:T(8,128)S(1)}, u32[]{:S(2)}, u32[]{:S(2)}) collective-permute-start(f32[6,128]{1,0:T(8,128)S(1)} %pad_maximum_fusion.4), channel_id=1, source_target_pairs={{0,8},{8,0},{16,24},{24,16},{1,9},{9,1},{17,25},{25,17},{2,10},{10... | collective-permute-start | bytes 9224 | tf_op jit(solution)/shard_map/ppermute | solution.py:47
  33.9 1.9 %collective-permute-done.10.first = f32[6,128]{1,0:T(8,128)S(1)} collective-permute-done((f32[6,128]{1,0:T(8,128)S(1)}, f32[6,128]{1,0:T(8,128)S(1)}, u32[]{:S(2)}, u32[]{:S(2)}) %collective-permute-start.10) | collective-permute-done | bytes 3104 | tf_op jit(solution)/shard_map/ppermute | solution.py:47
  35.8 0.0 collective-permute-done.11.second
  35.8 0.6 %pick.1 = bf16[18,128]{1,0:T(8,128)(2,1)} custom-call(s32[18]{0:T(128)S(4)} %get-tuple-element.58.place, f32[6,128]{1,0:T(8,128)S(1)} %pad_maximum_fusion.2.own, f32[6,128]{1,0:T(8,128)S(1)} %collective-permute-done.10.first, f32[6,128]{1,0:T(8,128)S(1)} %collective-permute-done.11.second), custom_call_target="tpu_custom_call" | custom-call | tf_op jit(solution)/shard_map/pick/pallas_call | solution.py:593
  (11 shorter events, 0.1 us)
Async XLA Ops:
  1.7 5.4 %collective-permute-start = (bf16[6,16,128]{2,1,0:T(8,128)(2,1)S(1)}, bf16[6,16,128]{2,1,0:T(8,128)(2,1)S(1)}, u32[]{:S(2)}, u32[]{:S(2)}) collective-permute-start(bf16[6,16,128]{2,1,0:T(8,128)(2,1)S(1)} %get-tuple-element.41), channel_id=1, source_target_pairs={{0,24},{8,16},{16,8},{24,0},{1,25},{9,17},{17,9},{25,1},{2,26},{10... | collective-permute-start | bytes 73736 | tf_op jit(solution)/shard_map/ppermute | solution.py:47
  4.2 2.9 %collective-permute-start.1 = (bf16[6,16,128]{2,1,0:T(8,128)(2,1)S(1)}, bf16[6,16,128]{2,1,0:T(8,128)(2,1)S(1)}, u32[]{:S(2)}, u32[]{:S(2)}) collective-permute-start(bf16[6,16,128]{2,1,0:T(8,128)(2,1)S(1)} %get-tuple-element.42), channel_id=1, source_target_pairs={{0,8},{8,0},{16,24},{24,16},{1,9},{9,1},{17,25},{25,17},{2,10},{10... | collective-permute-start | bytes 73736 | tf_op jit(solution)/shard_map/ppermute | solution.py:47
  7.1 8.8 %collective-permute-start.2 = (bf16[6,16,128]{2,1,0:T(8,128)(2,1)S(1)}, bf16[6,16,128]{2,1,0:T(8,128)(2,1)S(1)}, u32[]{:S(2)}, u32[]{:S(2)}) collective-permute-start(bf16[6,16,128]{2,1,0:T(8,128)(2,1)S(1)} %pad_maximum_fusion), channel_id=1, source_target_pairs={{0,1},{1,0},{2,3},{3,2},{4,5},{5,4},{6,7},{7,6},{8,9},{9,8},{10,11... | collective-permute-start | bytes 73736 | tf_op jit(solution)/shard_map/ppermute | solution.py:47
  8.7 7.3 %collective-permute-start.3 = (bf16[6,16,128]{2,1,0:T(8,128)(2,1)S(1)}, bf16[6,16,128]{2,1,0:T(8,128)(2,1)S(1)}, u32[]{:S(2)}, u32[]{:S(2)}) collective-permute-start(bf16[6,16,128]{2,1,0:T(8,128)(2,1)S(1)} %pad_maximum_fusion.1), channel_id=1, source_target_pairs={{0,7},{1,2},{2,1},{3,4},{4,3},{5,6},{6,5},{7,0},{8,15},{9,10},{10,... | collective-permute-start | bytes 73736 | tf_op jit(solution)/shard_map/ppermute | solution.py:47
  17.1 4.8 %collective-permute-start.6 = (bf16[384,128]{1,0:T(8,128)(2,1)S(1)}, bf16[384,128]{1,0:T(8,128)(2,1)S(1)}, u32[]{:S(2)}, u32[]{:S(2)}) collective-permute-start(bf16[384,128]{1,0:T(8,128)(2,1)S(1)} %get-tuple-element.46), channel_id=1, source_target_pairs={{0,1},{1,0},{2,3},{3,2},{4,5},{5,4},{6,7},{7,6},{8,9},{9,8},{10,11... | collective-permute-start | bytes 294920 | tf_op jit(solution)/shard_map/ppermute | solution.py:47
  17.2 4.7 %collective-permute-start.7 = (bf16[384,128]{1,0:T(8,128)(2,1)S(1)}, bf16[384,128]{1,0:T(8,128)(2,1)S(1)}, u32[]{:S(2)}, u32[]{:S(2)}) collective-permute-start(bf16[384,128]{1,0:T(8,128)(2,1)S(1)} %get-tuple-element.47), channel_id=1, source_target_pairs={{0,0},{1,2},{2,1},{3,4},{4,3},{5,6},{6,5},{7,7},{8,8},{9,10},{10,9... | collective-permute-start | bytes 294920 | tf_op jit(solution)/shard_map/ppermute | solution.py:47
  17.8 4.0 %collective-permute-start.4 = (bf16[192,128]{1,0:T(8,128)(2,1)S(1)}, bf16[192,128]{1,0:T(8,128)(2,1)S(1)}, u32[]{:S(2)}, u32[]{:S(2)}) collective-permute-start(bf16[192,128]{1,0:T(8,128)(2,1)S(1)} %get-tuple-element.44), channel_id=1, source_target_pairs={{0,24},{8,16},{16,8},{24,0},{1,25},{9,17},{17,9},{25,1},{2,26},{10... | collective-permute-start | bytes 147464 | tf_op jit(solution)/shard_map/ppermute | solution.py:47
  18.2 3.7 %collective-permute-start.5 = (bf16[192,128]{1,0:T(8,128)(2,1)S(1)}, bf16[192,128]{1,0:T(8,128)(2,1)S(1)}, u32[]{:S(2)}, u32[]{:S(2)}) collective-permute-start(bf16[192,128]{1,0:T(8,128)(2,1)S(1)} %get-tuple-element.45), channel_id=1, source_target_pairs={{0,8},{8,0},{16,24},{24,16},{1,9},{9,1},{17,25},{25,17},{2,10},{10... | collective-permute-start | bytes 147464 | tf_op jit(solution)/shard_map/ppermute | solution.py:47
  24.3 8.4 %collective-permute-start.8 = (f32[6,128]{1,0:T(8,128)S(1)}, f32[6,128]{1,0:T(8,128)S(1)}, u32[]{:S(2)}, u32[]{:S(2)}) collective-permute-start(f32[6,128]{1,0:T(8,128)S(1)} %get-tuple-element.60), channel_id=1, source_target_pairs={{0,7},{1,2},{2,1},{3,4},{4,3},{5,6},{6,5},{7,0},{8,15},{9,10},{10,... | collective-permute-start | bytes 9224 | tf_op jit(solution)/shard_map/ppermute | solution.py:47
  27.2 5.5 %collective-permute-start.9 = (f32[6,128]{1,0:T(8,128)S(1)}, f32[6,128]{1,0:T(8,128)S(1)}, u32[]{:S(2)}, u32[]{:S(2)}) collective-permute-start(f32[6,128]{1,0:T(8,128)S(1)} %get-tuple-element.61), channel_id=1, source_target_pairs={{0,1},{1,0},{2,3},{3,2},{4,5},{5,4},{6,7},{7,6},{8,9},{9,8},{10,11... | collective-permute-start | bytes 9224 | tf_op jit(solution)/shard_map/ppermute | solution.py:47
  32.7 3.1 %collective-permute-start.10 = (f32[6,128]{1,0:T(8,128)S(1)}, f32[6,128]{1,0:T(8,128)S(1)}, u32[]{:S(2)}, u32[]{:S(2)}) collective-permute-start(f32[6,128]{1,0:T(8,128)S(1)} %pad_maximum_fusion.3), channel_id=1, source_target_pairs={{0,24},{8,16},{16,8},{24,0},{1,25},{9,17},{17,9},{25,1},{2,26},{10... | collective-permute-start | bytes 9224 | tf_op jit(solution)/shard_map/ppermute | solution.py:47
  32.8 3.0 %collective-permute-start.11 = (f32[6,128]{1,0:T(8,128)S(1)}, f32[6,128]{1,0:T(8,128)S(1)}, u32[]{:S(2)}, u32[]{:S(2)}) collective-permute-start(f32[6,128]{1,0:T(8,128)S(1)} %pad_maximum_fusion.4), channel_id=1, source_target_pairs={{0,8},{8,0},{16,24},{24,16},{1,9},{9,1},{17,25},{25,17},{2,10},{10... | collective-permute-start | bytes 9224 | tf_op jit(solution)/shard_map/ppermute | solution.py:47

commit v10 on v8

--- a/solution.py
+++ b/solution.py
@@ -16,11 +16,11 @@
 AFTER = 16
 ROOM = PAD + AFTER
 ROWS = 16
-PAIR = 2
+PAIR = 7
 TOGETHER = 4
 PARTS = 4
 TURN = 16
-GROUP = 8
+GROUP = 16
 DELAY = 4
 MIB = 2**20
 
@@ -251,8 +251,8 @@
     for k, part in enumerate((south, north)):
         for r in range(3 * CAP):
             rows[(k + 1) * 3 * CAP + r] = part[r]
-    for first_tile in range(0, n_tiles, TOGETHER):
-        tiles = range(first_tile, first_tile + TOGETHER)
+    for first_tile in range(0, n_tiles, 2):
+        tiles = range(first_tile, first_tile + 2)
         contribs = []
         for t in tiles[::2]:
             both = jnp.concatenate([rows[slots[t]], rows[slots[t + 1]]], axis=0)
@@ -398,24 +398,31 @@
     return pl.ds(pl.multiple_of((j - 1) * BLK, BLK), BLK)
 
 
+def share(columns, most):
+    return max(k for k in range(1, most + 1) if columns % k == 0)
+
+
 def inner_kernel(props, state, fresh, press, speed):
     columns, tall = state.shape[0] - 2, state.shape[2]
 
+    group = share(columns, GROUP)
+
     def speeds(step, carry):
         rows = range(PAD, tall - AFTER, 8)
-        places = [(1 + step * GROUP + k, row) for k in range(GROUP) for row in rows]
+        places = [(1 + step * group + k, row) for k in range(group) for row in rows]
         store_speeds(props, state, speed, places, (0, 1))
         return carry
 
-    lax.fori_loop(0, columns // GROUP, speeds, 0)
+    lax.fori_loop(0, columns // group, speeds, 0)
+    pair = share(columns - 2, PAIR)
 
     def remap(step, carry):
         rows = range(PAD + 8, tall - AFTER - 8, 8)
-        places = [(2 + step * PAIR + k, row) for k in range(PAIR) for row in rows]
+        places = [(2 + step * pair + k, row) for k in range(pair) for row in rows]
         remap_tiles(props, state, speed, press, fresh, places, scalars(state.shape[1]))
         return carry
 
-    lax.fori_loop(0, (columns - 2) // PAIR, remap, 0)
+    lax.fori_loop(0, (columns - 2) // pair, remap, 0)
 
 
 def inner(props, state, width):
@@ -475,12 +482,14 @@
     places = [(j, row) for j in (0, columns + 1) for row in range(PAD, tall - AFTER, 8)]
     store_speeds(props, state, speed, places, (1,))
 
+    group = share(columns, GROUP)
+
     def sides(step, carry):
-        places = [(1 + step * 2 * PAIR + k, row) for k in range(2 * PAIR) for row in (PAD, tall - AFTER - 8)]
+        places = [(1 + step * group + k, row) for k in range(group) for row in (PAD, tall - AFTER - 8)]
         remap_tiles(props, state, speed, press, fresh, places, scalars(state.shape[1]))
         return carry
 
-    lax.fori_loop(0, columns // (2 * PAIR), sides, 0)
+    lax.fori_loop(0, columns // group, sides, 0)
     places = [(j, row) for j in (1, columns) for row in range(PAD + 8, tall - AFTER - 8, 8)]
     remap_tiles(props, state, speed, press, fresh, places, scalars(state.shape[1]))
 
@@ -582,7 +591,9 @@
 
 def pick_kernel(place, own, first, second, out, table, lines):
     for k, part in enumerate((own, first, second)):
-        table[k * 3 * CAP : (k + 1) * 3 * CAP, :] = part[...]
+        for spot, code in enumerate((0, 2, 1)):
+            row = (k * 3 + code) * CAP
+            table[row : row + CAP, :] = part[spot * CAP : (spot + 1) * CAP, :]
     for b in range(out.shape[0]):
         lines[b : b + 1, :] = table[pl.ds(place[b], 1), :]
     out[...] = lines[...].astype(BF16)
@@ -662,7 +673,7 @@
 
     def along_x(which):
         rows = slice(which * CAP, (which + 1) * CAP)
-        return jnp.concatenate([own[rows], first[rows], second[rows]], axis=0)
+        return jnp.concatenate([own[rows], second[rows], first[rows]], axis=0)
 
     back = pick(place, along_x(0), swap(along_x(1), "gx", 1), swap(along_x(2), "gx", 2))
     return remapped, back.reshape(n_blocks * BLK)

time: 36.3 us -> 38.8 us (1.069)
  starting transfers between devices: 17.2 us -> 18.7 us
  waiting for transfers between devices: 2.07 us -> 3.28 us
    ppermute x12, starting transfers between devices: 17.2 us -> 18.7 us  [swap(): return lax.ppermute(value, axis, pairs)]
    ppermute x12, waiting for transfers between devices: 2.07 us -> 3.28 us  [swap(): return lax.ppermute(value, axis, pairs)]
  transfers between devices with their start and end apart: 12 -> 12, of which waited for: 2 -> 3; matrix products, arithmetic and copies ran while one was open for 0% -> 0% of each run, Pallas kernels for 28% -> 26%
where the time goes in v10:
time: 38.8 us; the launch traced here: 38.6 us
  starting transfers between devices  18.7 us (48%)
  Pallas kernels  15.1 us (39%)
  waiting for transfers between devices  3.28 us (8%)
  between operations  1.47 us (4%)
    ppermute x12, starting transfers between devices, swap(): return lax.ppermute(value, axis, pairs)  18.7 us
    ppermute x12, waiting for transfers between devices, swap(): return lax.ppermute(value, axis, pairs)  3.28 us
    pallas_call x1, Pallas kernels, stage(): pl.pallas_call(functools.partial(stage_kernel, size_y=size_y), name='stag...  3.04 us
    pallas_call x1, Pallas kernels, inner(): pl.pallas_call(inner_kernel, name='inner', out_shape=(pltpu.VMEM((count,...  2.6 us
    pallas_call x1, Pallas kernels, outer(): pl.pallas_call(functools.partial(outer_kernel, size_x=size_x, size_y=size...  2.39 us
    pallas_call x1, Pallas kernels, fetch(): pl.pallas_call(fetch_kernel, name='fetch', out_shape=pltpu.VMEM(value.sha...  2.2 us
    pallas_call x1, Pallas kernels, late(): pl.pallas_call(late_kernel, name='late', out_shape=(jax.ShapeDtypeStruct(...  2.13 us
    pallas_call x1, Pallas kernels, deposit(): pl.pallas_call(deposit_kernel, name='deposit', out_shape=(pltpu.VMEM(stat...  1.04 us
  transfers between devices with their start and end apart: 12, of which 3 were waited for; matrix products, arithmetic and copies ran while one was open for 0% of the time, Pallas kernels for 26%

profile of v10, /device:TPU:0, one launch (start us, length us, event | category | flops | bytes accessed | tf_op | source)
XLA Modules:
  0.0 38.6 jit_solution(3316235556023822218)
XLA Ops:
  0.6 1.0 %payload.1 = (bf16[6,16,128]{2,1,0:T(8,128)(2,1)S(1)}, bf16[6,16,128]{2,1,0:T(8,128)(2,1)S(1)}, bf16[6,16,128]{2,1,0:T(8,128)(2,1)S(1)}, s32[18]{0:T(128)S(4)}, ...) custom-call(s32[18]{0:T(128)} %dest_hbm.1, f32[2,8]{1,0:T(2,128)} %props_hbm.1, f32[18,128]{1,0:T(8,128)} %bitcast.4, ...), custom_call_target="tpu_custom_call" | custom-call | tf_op jit(solution)/shard_map/payload/pallas_call | solution.py:112
  1.7 2.5 %collective-permute-start = (bf16[6,16,128]{2,1,0:T(8,128)(2,1)S(1)}, bf16[6,16,128]{2,1,0:T(8,128)(2,1)S(1)}, u32[]{:S(2)}, u32[]{:S(2)}) collective-permute-start(bf16[6,16,128]{2,1,0:T(8,128)(2,1)S(1)} %get-tuple-element.41), channel_id=1, source_target_pairs={{0,24},{8,16},{16,8},{24,0},{1,25},{9,17},{17,9},{25,1},{2,26},{10... | collective-permute-start | bytes 73736 | tf_op jit(solution)/shard_map/ppermute | solution.py:47
  4.2 0.7 %collective-permute-start.1 = (bf16[6,16,128]{2,1,0:T(8,128)(2,1)S(1)}, bf16[6,16,128]{2,1,0:T(8,128)(2,1)S(1)}, u32[]{:S(2)}, u32[]{:S(2)}) collective-permute-start(bf16[6,16,128]{2,1,0:T(8,128)(2,1)S(1)} %get-tuple-element.42), channel_id=1, source_target_pairs={{0,8},{8,0},{16,24},{24,16},{1,9},{9,1},{17,25},{25,17},{2,10},{10... | collective-permute-start | bytes 73736 | tf_op jit(solution)/shard_map/ppermute | solution.py:47
  4.8 2.2 %fetch.1.weight = bf16[128,128,128]{2,1,0:T(8,128)(2,1)S(1)} custom-call(bf16[128,128,128]{2,1,0:T(8,128)(2,1)} %source.1), custom_call_target="tpu_custom_call" | custom-call | bytes 8388608 | tf_op jit(solution)/shard_map/fetch/pallas_call | solution.py:201
  7.0 0.0 collective-permute-done.first
  7.1 0.0 collective-permute-done.1.second
  7.1 4.6 %collective-permute-start.2 = (bf16[6,16,128]{2,1,0:T(8,128)(2,1)S(1)}, bf16[6,16,128]{2,1,0:T(8,128)(2,1)S(1)}, u32[]{:S(2)}, u32[]{:S(2)}) collective-permute-start(bf16[6,16,128]{2,1,0:T(8,128)(2,1)S(1)} %pad_maximum_fusion), channel_id=1, source_target_pairs={{0,7},{1,2},{2,1},{3,4},{4,3},{5,6},{6,5},{7,0},{8,15},{9,10},{10,... | collective-permute-start | bytes 73736 | tf_op jit(solution)/shard_map/ppermute | solution.py:47
  11.7 0.0 collective-permute-start.3
  12.4 3.0 %stage.1 = (f32[18,12,88,128]{3,2,1,0:T(8,128)S(1)}, bf16[128,128,128]{2,1,0:T(8,128)(2,1)S(1)}, s32[128]{0:T(128)S(4)}, s32[128]{0:T(128)S(4)}, s32[128]{0:T(128)S(4)}) custom-call(s32[128]{0:T(128)S(4)} %get-tuple-element.33.tile_slot, s32[128]{0:T(128)S(4)} %get-tuple-element.34.tile_cell, s32[1]{0:T(128)S(6)} %copy.27.tile_count, f32[12,64,2048]{2,1,0:T(8,128)} %cell.1, ...), custom_call_target="tpu_custom_call" | custom-call | bytes 12582912 | tf_op jit(solution)/shard_map/stage/pallas_call | solution.py:176
  15.4 0.0 collective-permute-done.2.south
  15.4 0.1 collective-permute-done.3.north
  15.5 1.0 %deposit.1 = (f32[18,12,88,128]{3,2,1,0:T(8,128)S(1)}, bf16[192,128]{1,0:T(8,128)(2,1)S(1)}, bf16[192,128]{1,0:T(8,128)(2,1)S(1)}, bf16[384,128]{1,0:T(8,128)(2,1)S(1)}, bf16[384,128]{1,0:T(8,128)(2,1)S(1)}) custom-call(s32[128]{0:T(128)S(4)} %get-tuple-element.37.slots, s32[128]{0:T(128)S(4)} %get-tuple-element.39.spots, ...), custom_call_target="tpu_custom_call", output_to_operand_aliasing={{0}: (8, {})} | custom-call | tf_op jit(solution)/shard_map/deposit/pallas_call | solution.py:289
  16.6 2.0 %collective-permute-start.6 = (bf16[384,128]{1,0:T(8,128)(2,1)S(1)}, bf16[384,128]{1,0:T(8,128)(2,1)S(1)}, u32[]{:S(2)}, u32[]{:S(2)}) collective-permute-start(bf16[384,128]{1,0:T(8,128)(2,1)S(1)} %get-tuple-element.46), channel_id=1, source_target_pairs={{0,1},{1,0},{2,3},{3,2},{4,5},{5,4},{6,7},{7,6},{8,9},{9,8},{10,11... | collective-permute-start | bytes 294920 | tf_op jit(solution)/shard_map/ppermute | solution.py:47
  18.6 0.7 %collective-permute-start.7 = (bf16[384,128]{1,0:T(8,128)(2,1)S(1)}, bf16[384,128]{1,0:T(8,128)(2,1)S(1)}, u32[]{:S(2)}, u32[]{:S(2)}) collective-permute-start(bf16[384,128]{1,0:T(8,128)(2,1)S(1)} %get-tuple-element.47), channel_id=1, source_target_pairs={{0,0},{1,2},{2,1},{3,4},{4,3},{5,6},{6,5},{7,7},{8,8},{9,10},{10,9... | collective-permute-start | bytes 294920 | tf_op jit(solution)/shard_map/ppermute | solution.py:47
  19.2 0.1 collective-permute-start.4
  19.3 1.2 %collective-permute-start.5 = (bf16[192,128]{1,0:T(8,128)(2,1)S(1)}, bf16[192,128]{1,0:T(8,128)(2,1)S(1)}, u32[]{:S(2)}, u32[]{:S(2)}) collective-permute-start(bf16[192,128]{1,0:T(8,128)(2,1)S(1)} %get-tuple-element.45), channel_id=1, source_target_pairs={{0,8},{8,0},{16,24},{24,16},{1,9},{9,1},{17,25},{25,17},{2,10},{10... | collective-permute-start | bytes 147464 | tf_op jit(solution)/shard_map/ppermute | solution.py:47
  20.5 2.6 %inner.1 = (f32[12,64,2048]{2,1,0:T(8,128)S(1)}, f32[16,64,128]{2,1,0:T(8,128)S(1)}, f32[18,3,88,128]{3,2,1,0:T(8,128)S(1)}) custom-call(f32[2,8]{1,0:T(2,128)S(4)} %get-tuple-element.32.props, f32[18,12,88,128]{3,2,1,0:T(8,128)S(1)} %get-tuple-element.49.state.state_in), custom_call_target="tpu_custom_call" | custom-call | flops 48660480 | bytes 19464192 | tf_op jit(solution)/shard_map/inner/pallas_call | solution.py:430
  23.2 0.0 collective-permute-done.4.edge_x1
  23.2 0.0 collective-permute-done.5.edge_x2
  23.2 0.0 collective-permute-done.6.edge_y2
  23.2 0.0 collective-permute-done.7.edge_y1
  23.2 2.4 %outer.1 = (f32[12,64,2048]{2,1,0:T(8,128)}, f32[18,12,88,128]{3,2,1,0:T(8,128)S(1)}, f32[18,3,88,128]{3,2,1,0:T(8,128)S(1)}, f32[16,64,128]{2,1,0:T(8,128)S(1)}...) custom-call(f32[2,8]{1,0:T(2,128)S(4)} %get-tuple-element.32.props, ...), custom_call_target="tpu_custom_call", output_to_operand_aliasing={{1}: (8, {}), {2}: (9, {}), {3}: (10, {}), {4}: (11, {})} | custom-call | tf_op jit(solution)/shard_map/outer/pallas_call | solution.py:519
  25.6 2.9 %collective-permute-start.8 = (f32[6,128]{1,0:T(8,128)S(1)}, f32[6,128]{1,0:T(8,128)S(1)}, u32[]{:S(2)}, u32[]{:S(2)}) collective-permute-start(f32[6,128]{1,0:T(8,128)S(1)} %get-tuple-element.60), channel_id=1, source_target_pairs={{0,1},{1,0},{2,3},{3,2},{4,5},{5,4},{6,7},{7,6},{8,9},{9,8},{10,11... | collective-permute-start | bytes 9224 | tf_op jit(solution)/shard_map/ppermute | solution.py:47
  28.5 2.7 %collective-permute-start.9 = (f32[6,128]{1,0:T(8,128)S(1)}, f32[6,128]{1,0:T(8,128)S(1)}, u32[]{:S(2)}, u32[]{:S(2)}) collective-permute-start(f32[6,128]{1,0:T(8,128)S(1)} %get-tuple-element.61), channel_id=1, source_target_pairs={{0,7},{1,2},{2,1},{3,4},{4,3},{5,6},{6,5},{7,0},{8,15},{9,10},{10,... | collective-permute-start | bytes 9224 | tf_op jit(solution)/shard_map/ppermute | solution.py:47
  31.2 2.1 %late.1 = (f32[12,64,2048]{2,1,0:T(8,128)}, f32[12,64,2048]{2,1,0:T(8,128)S(1)}) custom-call(f32[18,12,88,128]{3,2,1,0:T(8,128)S(1)} %get-tuple-element.53.state, f32[18,3,88,128]{3,2,1,0:T(8,128)S(1)} %get-tuple-element.54.speed, f32[12,64,2048]{2,1,0:T(8,128)S(1)} %get-tuple-element.55.fresh_in, ...), custom_call_target="tpu_custom_call", output_to_operand_aliasing={{1}: (2, {}), {0}: (3, {})} | custom-call | flops 12165120 | bytes 19464192 | tf_op jit(solution)/shard_map/late/pallas_call | solution.py:579
  33.3 0.0 collective-permute-done.8
  33.4 1.4 %collective-permute-done.9 = f32[6,128]{1,0:T(8,128)S(1)} collective-permute-done((f32[6,128]{1,0:T(8,128)S(1)}, f32[6,128]{1,0:T(8,128)S(1)}, u32[]{:S(2)}, u32[]{:S(2)}) %collective-permute-start.9) | collective-permute-done | bytes 3104 | tf_op jit(solution)/shard_map/ppermute | solution.py:47
  34.8 0.1 collective-permute-start.10
  34.9 1.3 %collective-permute-start.11 = (f32[6,128]{1,0:T(8,128)S(1)}, f32[6,128]{1,0:T(8,128)S(1)}, u32[]{:S(2)}, u32[]{:S(2)}) collective-permute-start(f32[6,128]{1,0:T(8,128)S(1)} %pad_maximum_fusion.4), channel_id=1, source_target_pairs={{0,8},{8,0},{16,24},{24,16},{1,9},{9,1},{17,25},{25,17},{2,10},{10... | collective-permute-start | bytes 9224 | tf_op jit(solution)/shard_map/ppermute | solution.py:47
  36.2 1.7 %collective-permute-done.10.first = f32[6,128]{1,0:T(8,128)S(1)} collective-permute-done((f32[6,128]{1,0:T(8,128)S(1)}, f32[6,128]{1,0:T(8,128)S(1)}, u32[]{:S(2)}, u32[]{:S(2)}) %collective-permute-start.10) | collective-permute-done | bytes 3104 | tf_op jit(solution)/shard_map/ppermute | solution.py:47
  37.9 0.0 collective-permute-done.11.second
  37.9 0.6 %pick.1 = bf16[18,128]{1,0:T(8,128)(2,1)} custom-call(s32[18]{0:T(128)S(4)} %get-tuple-element.58.place, f32[6,128]{1,0:T(8,128)S(1)} %pad_maximum_fusion.2.own, f32[6,128]{1,0:T(8,128)S(1)} %collective-permute-done.10.first, f32[6,128]{1,0:T(8,128)S(1)} %collective-permute-done.11.second), custom_call_target="tpu_custom_call" | custom-call | tf_op jit(solution)/shard_map/pick/pallas_call | solution.py:604
  (11 shorter events, 0.1 us)
Async XLA Ops:
  1.7 5.4 %collective-permute-start = (bf16[6,16,128]{2,1,0:T(8,128)(2,1)S(1)}, bf16[6,16,128]{2,1,0:T(8,128)(2,1)S(1)}, u32[]{:S(2)}, u32[]{:S(2)}) collective-permute-start(bf16[6,16,128]{2,1,0:T(8,128)(2,1)S(1)} %get-tuple-element.41), channel_id=1, source_target_pairs={{0,24},{8,16},{16,8},{24,0},{1,25},{9,17},{17,9},{25,1},{2,26},{10... | collective-permute-start | bytes 73736 | tf_op jit(solution)/shard_map/ppermute | solution.py:47
  4.2 2.9 %collective-permute-start.1 = (bf16[6,16,128]{2,1,0:T(8,128)(2,1)S(1)}, bf16[6,16,128]{2,1,0:T(8,128)(2,1)S(1)}, u32[]{:S(2)}, u32[]{:S(2)}) collective-permute-start(bf16[6,16,128]{2,1,0:T(8,128)(2,1)S(1)} %get-tuple-element.42), channel_id=1, source_target_pairs={{0,8},{8,0},{16,24},{24,16},{1,9},{9,1},{17,25},{25,17},{2,10},{10... | collective-permute-start | bytes 73736 | tf_op jit(solution)/shard_map/ppermute | solution.py:47
  7.1 8.3 %collective-permute-start.2 = (bf16[6,16,128]{2,1,0:T(8,128)(2,1)S(1)}, bf16[6,16,128]{2,1,0:T(8,128)(2,1)S(1)}, u32[]{:S(2)}, u32[]{:S(2)}) collective-permute-start(bf16[6,16,128]{2,1,0:T(8,128)(2,1)S(1)} %pad_maximum_fusion), channel_id=1, source_target_pairs={{0,7},{1,2},{2,1},{3,4},{4,3},{5,6},{6,5},{7,0},{8,15},{9,10},{10,... | collective-permute-start | bytes 73736 | tf_op jit(solution)/shard_map/ppermute | solution.py:47
  11.7 3.8 %collective-permute-start.3 = (bf16[6,16,128]{2,1,0:T(8,128)(2,1)S(1)}, bf16[6,16,128]{2,1,0:T(8,128)(2,1)S(1)}, u32[]{:S(2)}, u32[]{:S(2)}) collective-permute-start(bf16[6,16,128]{2,1,0:T(8,128)(2,1)S(1)} %pad_maximum_fusion.1), channel_id=1, source_target_pairs={{0,1},{1,0},{2,3},{3,2},{4,5},{5,4},{6,7},{7,6},{8,9},{9,8},{10,11... | collective-permute-start | bytes 73736 | tf_op jit(solution)/shard_map/ppermute | solution.py:47
  16.6 6.6 %collective-permute-start.6 = (bf16[384,128]{1,0:T(8,128)(2,1)S(1)}, bf16[384,128]{1,0:T(8,128)(2,1)S(1)}, u32[]{:S(2)}, u32[]{:S(2)}) collective-permute-start(bf16[384,128]{1,0:T(8,128)(2,1)S(1)} %get-tuple-element.46), channel_id=1, source_target_pairs={{0,1},{1,0},{2,3},{3,2},{4,5},{5,4},{6,7},{7,6},{8,9},{9,8},{10,11... | collective-permute-start | bytes 294920 | tf_op jit(solution)/shard_map/ppermute | solution.py:47
  18.6 4.6 %collective-permute-start.7 = (bf16[384,128]{1,0:T(8,128)(2,1)S(1)}, bf16[384,128]{1,0:T(8,128)(2,1)S(1)}, u32[]{:S(2)}, u32[]{:S(2)}) collective-permute-start(bf16[384,128]{1,0:T(8,128)(2,1)S(1)} %get-tuple-element.47), channel_id=1, source_target_pairs={{0,0},{1,2},{2,1},{3,4},{4,3},{5,6},{6,5},{7,7},{8,8},{9,10},{10,9... | collective-permute-start | bytes 294920 | tf_op jit(solution)/shard_map/ppermute | solution.py:47
  19.2 3.9 %collective-permute-start.4 = (bf16[192,128]{1,0:T(8,128)(2,1)S(1)}, bf16[192,128]{1,0:T(8,128)(2,1)S(1)}, u32[]{:S(2)}, u32[]{:S(2)}) collective-permute-start(bf16[192,128]{1,0:T(8,128)(2,1)S(1)} %get-tuple-element.44), channel_id=1, source_target_pairs={{0,24},{8,16},{16,8},{24,0},{1,25},{9,17},{17,9},{25,1},{2,26},{10... | collective-permute-start | bytes 147464 | tf_op jit(solution)/shard_map/ppermute | solution.py:47
  19.3 3.9 %collective-permute-start.5 = (bf16[192,128]{1,0:T(8,128)(2,1)S(1)}, bf16[192,128]{1,0:T(8,128)(2,1)S(1)}, u32[]{:S(2)}, u32[]{:S(2)}) collective-permute-start(bf16[192,128]{1,0:T(8,128)(2,1)S(1)} %get-tuple-element.45), channel_id=1, source_target_pairs={{0,8},{8,0},{16,24},{24,16},{1,9},{9,1},{17,25},{25,17},{2,10},{10... | collective-permute-start | bytes 147464 | tf_op jit(solution)/shard_map/ppermute | solution.py:47
  25.6 7.8 %collective-permute-start.8 = (f32[6,128]{1,0:T(8,128)S(1)}, f32[6,128]{1,0:T(8,128)S(1)}, u32[]{:S(2)}, u32[]{:S(2)}) collective-permute-start(f32[6,128]{1,0:T(8,128)S(1)} %get-tuple-element.60), channel_id=1, source_target_pairs={{0,1},{1,0},{2,3},{3,2},{4,5},{5,4},{6,7},{7,6},{8,9},{9,8},{10,11... | collective-permute-start | bytes 9224 | tf_op jit(solution)/shard_map/ppermute | solution.py:47
  28.5 6.3 %collective-permute-start.9 = (f32[6,128]{1,0:T(8,128)S(1)}, f32[6,128]{1,0:T(8,128)S(1)}, u32[]{:S(2)}, u32[]{:S(2)}) collective-permute-start(f32[6,128]{1,0:T(8,128)S(1)} %get-tuple-element.61), channel_id=1, source_target_pairs={{0,7},{1,2},{2,1},{3,4},{4,3},{5,6},{6,5},{7,0},{8,15},{9,10},{10,... | collective-permute-start | bytes 9224 | tf_op jit(solution)/shard_map/ppermute | solution.py:47
  34.8 3.1 %collective-permute-start.10 = (f32[6,128]{1,0:T(8,128)S(1)}, f32[6,128]{1,0:T(8,128)S(1)}, u32[]{:S(2)}, u32[]{:S(2)}) collective-permute-start(f32[6,128]{1,0:T(8,128)S(1)} %pad_maximum_fusion.3), channel_id=1, source_target_pairs={{0,24},{8,16},{16,8},{24,0},{1,25},{9,17},{17,9},{25,1},{2,26},{10... | collective-permute-start | bytes 9224 | tf_op jit(solution)/shard_map/ppermute | solution.py:47
  34.9 3.0 %collective-permute-start.11 = (f32[6,128]{1,0:T(8,128)S(1)}, f32[6,128]{1,0:T(8,128)S(1)}, u32[]{:S(2)}, u32[]{:S(2)}) collective-permute-start(f32[6,128]{1,0:T(8,128)S(1)} %pad_maximum_fusion.4), channel_id=1, source_target_pairs={{0,8},{8,0},{16,24},{24,16},{1,9},{9,1},{17,25},{25,17},{2,10},{10... | collective-permute-start | bytes 9224 | tf_op jit(solution)/shard_map/ppermute | solution.py:47

commit v11 on v10

--- a/solution.py
+++ b/solution.py
@@ -591,9 +591,7 @@
 
 def pick_kernel(place, own, first, second, out, table, lines):
     for k, part in enumerate((own, first, second)):
-        for spot, code in enumerate((0, 2, 1)):
-            row = (k * 3 + code) * CAP
-            table[row : row + CAP, :] = part[spot * CAP : (spot + 1) * CAP, :]
+        table[k * 3 * CAP : (k + 1) * 3 * CAP, :] = part[...]
     for b in range(out.shape[0]):
         lines[b : b + 1, :] = table[pl.ds(place[b], 1), :]
     out[...] = lines[...].astype(BF16)
@@ -673,7 +671,7 @@
 
     def along_x(which):
         rows = slice(which * CAP, (which + 1) * CAP)
-        return jnp.concatenate([own[rows], second[rows], first[rows]], axis=0)
+        return jnp.concatenate([own[rows], first[rows], second[rows]], axis=0)
 
     back = pick(place, along_x(0), swap(along_x(1), "gx", 1), swap(along_x(2), "gx", 2))
     return remapped, back.reshape(n_blocks * BLK)

time: 38.8 us -> 36.1 us (0.930)
  starting transfers between devices: 18.7 us -> 17.1 us
  waiting for transfers between devices: 3.28 us -> 2.1 us
    ppermute x12, starting transfers between devices: 18.7 us -> 17.1 us  [swap(): return lax.ppermute(value, axis, pairs)]
    ppermute x12, waiting for transfers between devices: 3.28 us -> 2.1 us  [swap(): return lax.ppermute(value, axis, pairs)]
  transfers between devices with their start and end apart: 12 -> 12, of which waited for: 3 -> 2; matrix products, arithmetic and copies ran while one was open for 0% -> 0% of each run, Pallas kernels for 26% -> 28%
where the time goes in v11:
time: 36.1 us; the launch traced here: 35.9 us
  starting transfers between devices  17.1 us (47%)
  Pallas kernels  15.1 us (42%)
  waiting for transfers between devices  2.1 us (6%)
  between operations  1.49 us (4%)
    ppermute x12, starting transfers between devices, swap(): return lax.ppermute(value, axis, pairs)  17.1 us
    pallas_call x1, Pallas kernels, stage(): pl.pallas_call(functools.partial(stage_kernel, size_y=size_y), name='stag...  3.04 us
    pallas_call x1, Pallas kernels, inner(): pl.pallas_call(inner_kernel, name='inner', out_shape=(pltpu.VMEM((count,...  2.6 us
    pallas_call x1, Pallas kernels, outer(): pl.pallas_call(functools.partial(outer_kernel, size_x=size_x, size_y=size...  2.38 us
    pallas_call x1, Pallas kernels, fetch(): pl.pallas_call(fetch_kernel, name='fetch', out_shape=pltpu.VMEM(value.sha...  2.2 us
    pallas_call x1, Pallas kernels, late(): pl.pallas_call(late_kernel, name='late', out_shape=(jax.ShapeDtypeStruct(...  2.13 us
    ppermute x12, waiting for transfers between devices, swap(): return lax.ppermute(value, axis, pairs)  2.1 us
    pallas_call x1, Pallas kernels, payload(): pl.pallas_call(functools.partial(payload_kernel, size_y=size_y), name='pa...  1.04 us
  transfers between devices with their start and end apart: 12, of which 2 were waited for; matrix products, arithmetic and copies ran while one was open for 0% of the time, Pallas kernels for 28%

profile of v11, /device:TPU:0, one launch (start us, length us, event | category | flops | bytes accessed | tf_op | source)
XLA Modules:
  0.0 35.9 jit_solution(1834517216810081634)
XLA Ops:
  0.6 1.0 %payload.1 = (bf16[6,16,128]{2,1,0:T(8,128)(2,1)S(1)}, bf16[6,16,128]{2,1,0:T(8,128)(2,1)S(1)}, bf16[6,16,128]{2,1,0:T(8,128)(2,1)S(1)}, s32[18]{0:T(128)S(4)}, ...) custom-call(s32[18]{0:T(128)} %dest_hbm.1, f32[2,8]{1,0:T(2,128)} %props_hbm.1, f32[18,128]{1,0:T(8,128)} %bitcast.4, ...), custom_call_target="tpu_custom_call" | custom-call | tf_op jit(solution)/shard_map/payload/pallas_call | solution.py:112
  1.7 2.5 %collective-permute-start = (bf16[6,16,128]{2,1,0:T(8,128)(2,1)S(1)}, bf16[6,16,128]{2,1,0:T(8,128)(2,1)S(1)}, u32[]{:S(2)}, u32[]{:S(2)}) collective-permute-start(bf16[6,16,128]{2,1,0:T(8,128)(2,1)S(1)} %get-tuple-element.41), channel_id=1, source_target_pairs={{0,24},{8,16},{16,8},{24,0},{1,25},{9,17},{17,9},{25,1},{2,26},{10... | collective-permute-start | bytes 73736 | tf_op jit(solution)/shard_map/ppermute | solution.py:47
  4.2 0.7 %collective-permute-start.1 = (bf16[6,16,128]{2,1,0:T(8,128)(2,1)S(1)}, bf16[6,16,128]{2,1,0:T(8,128)(2,1)S(1)}, u32[]{:S(2)}, u32[]{:S(2)}) collective-permute-start(bf16[6,16,128]{2,1,0:T(8,128)(2,1)S(1)} %get-tuple-element.42), channel_id=1, source_target_pairs={{0,8},{8,0},{16,24},{24,16},{1,9},{9,1},{17,25},{25,17},{2,10},{10... | collective-permute-start | bytes 73736 | tf_op jit(solution)/shard_map/ppermute | solution.py:47
  4.8 2.2 %fetch.1.weight = bf16[128,128,128]{2,1,0:T(8,128)(2,1)S(1)} custom-call(bf16[128,128,128]{2,1,0:T(8,128)(2,1)} %source.1), custom_call_target="tpu_custom_call" | custom-call | bytes 8388608 | tf_op jit(solution)/shard_map/fetch/pallas_call | solution.py:201
  7.0 0.0 collective-permute-done.first
  7.1 0.0 collective-permute-done.1.second
  7.1 4.6 %collective-permute-start.2 = (bf16[6,16,128]{2,1,0:T(8,128)(2,1)S(1)}, bf16[6,16,128]{2,1,0:T(8,128)(2,1)S(1)}, u32[]{:S(2)}, u32[]{:S(2)}) collective-permute-start(bf16[6,16,128]{2,1,0:T(8,128)(2,1)S(1)} %pad_maximum_fusion), channel_id=1, source_target_pairs={{0,7},{1,2},{2,1},{3,4},{4,3},{5,6},{6,5},{7,0},{8,15},{9,10},{10,... | collective-permute-start | bytes 73736 | tf_op jit(solution)/shard_map/ppermute | solution.py:47
  11.7 0.0 collective-permute-start.3
  12.4 3.0 %stage.1 = (f32[18,12,88,128]{3,2,1,0:T(8,128)S(1)}, bf16[128,128,128]{2,1,0:T(8,128)(2,1)S(1)}, s32[128]{0:T(128)S(4)}, s32[128]{0:T(128)S(4)}, s32[128]{0:T(128)S(4)}) custom-call(s32[128]{0:T(128)S(4)} %get-tuple-element.33.tile_slot, s32[128]{0:T(128)S(4)} %get-tuple-element.34.tile_cell, s32[1]{0:T(128)S(6)} %copy.27.tile_count, f32[12,64,2048]{2,1,0:T(8,128)} %cell.1, ...), custom_call_target="tpu_custom_call" | custom-call | bytes 12582912 | tf_op jit(solution)/shard_map/stage/pallas_call | solution.py:176
  15.4 0.0 collective-permute-done.2.south
  15.4 0.1 collective-permute-done.3.north
  15.5 1.0 %deposit.1 = (f32[18,12,88,128]{3,2,1,0:T(8,128)S(1)}, bf16[192,128]{1,0:T(8,128)(2,1)S(1)}, bf16[192,128]{1,0:T(8,128)(2,1)S(1)}, bf16[384,128]{1,0:T(8,128)(2,1)S(1)}, bf16[384,128]{1,0:T(8,128)(2,1)S(1)}) custom-call(s32[128]{0:T(128)S(4)} %get-tuple-element.37.slots, s32[128]{0:T(128)S(4)} %get-tuple-element.39.spots, ...), custom_call_target="tpu_custom_call", output_to_operand_aliasing={{0}: (8, {})} | custom-call | tf_op jit(solution)/shard_map/deposit/pallas_call | solution.py:289
  16.6 2.0 %collective-permute-start.6 = (bf16[384,128]{1,0:T(8,128)(2,1)S(1)}, bf16[384,128]{1,0:T(8,128)(2,1)S(1)}, u32[]{:S(2)}, u32[]{:S(2)}) collective-permute-start(bf16[384,128]{1,0:T(8,128)(2,1)S(1)} %get-tuple-element.46), channel_id=1, source_target_pairs={{0,1},{1,0},{2,3},{3,2},{4,5},{5,4},{6,7},{7,6},{8,9},{9,8},{10,11... | collective-permute-start | bytes 294920 | tf_op jit(solution)/shard_map/ppermute | solution.py:47
  18.6 0.7 %collective-permute-start.7 = (bf16[384,128]{1,0:T(8,128)(2,1)S(1)}, bf16[384,128]{1,0:T(8,128)(2,1)S(1)}, u32[]{:S(2)}, u32[]{:S(2)}) collective-permute-start(bf16[384,128]{1,0:T(8,128)(2,1)S(1)} %get-tuple-element.47), channel_id=1, source_target_pairs={{0,0},{1,2},{2,1},{3,4},{4,3},{5,6},{6,5},{7,7},{8,8},{9,10},{10,9... | collective-permute-start | bytes 294920 | tf_op jit(solution)/shard_map/ppermute | solution.py:47
  19.2 0.1 collective-permute-start.4
  19.3 1.2 %collective-permute-start.5 = (bf16[192,128]{1,0:T(8,128)(2,1)S(1)}, bf16[192,128]{1,0:T(8,128)(2,1)S(1)}, u32[]{:S(2)}, u32[]{:S(2)}) collective-permute-start(bf16[192,128]{1,0:T(8,128)(2,1)S(1)} %get-tuple-element.45), channel_id=1, source_target_pairs={{0,8},{8,0},{16,24},{24,16},{1,9},{9,1},{17,25},{25,17},{2,10},{10... | collective-permute-start | bytes 147464 | tf_op jit(solution)/shard_map/ppermute | solution.py:47
  20.5 2.6 %inner.1 = (f32[12,64,2048]{2,1,0:T(8,128)S(1)}, f32[16,64,128]{2,1,0:T(8,128)S(1)}, f32[18,3,88,128]{3,2,1,0:T(8,128)S(1)}) custom-call(f32[2,8]{1,0:T(2,128)S(4)} %get-tuple-element.32.props, f32[18,12,88,128]{3,2,1,0:T(8,128)S(1)} %get-tuple-element.49.state.state_in), custom_call_target="tpu_custom_call" | custom-call | flops 48660480 | bytes 19464192 | tf_op jit(solution)/shard_map/inner/pallas_call | solution.py:430
  23.2 0.0 collective-permute-done.4.edge_x1
  23.2 0.0 collective-permute-done.5.edge_x2
  23.2 0.0 collective-permute-done.6.edge_y2
  23.2 0.0 collective-permute-done.7.edge_y1
  23.2 2.4 %outer.1 = (f32[12,64,2048]{2,1,0:T(8,128)}, f32[18,12,88,128]{3,2,1,0:T(8,128)S(1)}, f32[18,3,88,128]{3,2,1,0:T(8,128)S(1)}, f32[16,64,128]{2,1,0:T(8,128)S(1)}...) custom-call(f32[2,8]{1,0:T(2,128)S(4)} %get-tuple-element.32.props, ...), custom_call_target="tpu_custom_call", output_to_operand_aliasing={{1}: (8, {}), {2}: (9, {}), {3}: (10, {}), {4}: (11, {})} | custom-call | tf_op jit(solution)/shard_map/outer/pallas_call | solution.py:519
  25.6 0.9 %collective-permute-start.8 = (f32[6,128]{1,0:T(8,128)S(1)}, f32[6,128]{1,0:T(8,128)S(1)}, u32[]{:S(2)}, u32[]{:S(2)}) collective-permute-start(f32[6,128]{1,0:T(8,128)S(1)} %get-tuple-element.60), channel_id=1, source_target_pairs={{0,7},{1,2},{2,1},{3,4},{4,3},{5,6},{6,5},{7,0},{8,15},{9,10},{10,... | collective-permute-start | bytes 9224 | tf_op jit(solution)/shard_map/ppermute | solution.py:47
  26.5 3.5 %collective-permute-start.9 = (f32[6,128]{1,0:T(8,128)S(1)}, f32[6,128]{1,0:T(8,128)S(1)}, u32[]{:S(2)}, u32[]{:S(2)}) collective-permute-start(f32[6,128]{1,0:T(8,128)S(1)} %get-tuple-element.61), channel_id=1, source_target_pairs={{0,1},{1,0},{2,3},{3,2},{4,5},{5,4},{6,7},{7,6},{8,9},{9,8},{10,11... | collective-permute-start | bytes 9224 | tf_op jit(solution)/shard_map/ppermute | solution.py:47
  29.9 2.1 %late.1 = (f32[12,64,2048]{2,1,0:T(8,128)}, f32[12,64,2048]{2,1,0:T(8,128)S(1)}) custom-call(f32[18,12,88,128]{3,2,1,0:T(8,128)S(1)} %get-tuple-element.53.state, f32[18,3,88,128]{3,2,1,0:T(8,128)S(1)} %get-tuple-element.54.speed, f32[12,64,2048]{2,1,0:T(8,128)S(1)} %get-tuple-element.55.fresh_in, ...), custom_call_target="tpu_custom_call", output_to_operand_aliasing={{1}: (2, {}), {0}: (3, {})} | custom-call | flops 12165120 | bytes 19464192 | tf_op jit(solution)/shard_map/late/pallas_call | solution.py:579
  32.1 0.0 collective-permute-done.8
  32.1 0.0 collective-permute-done.9
  32.1 0.1 collective-permute-start.10
  32.2 1.0 %collective-permute-start.11 = (f32[6,128]{1,0:T(8,128)S(1)}, f32[6,128]{1,0:T(8,128)S(1)}, u32[]{:S(2)}, u32[]{:S(2)}) collective-permute-start(f32[6,128]{1,0:T(8,128)S(1)} %pad_maximum_fusion.4), channel_id=1, source_target_pairs={{0,8},{8,0},{16,24},{24,16},{1,9},{9,1},{17,25},{25,17},{2,10},{10... | collective-permute-start | bytes 9224 | tf_op jit(solution)/shard_map/ppermute | solution.py:47
  33.3 2.0 %collective-permute-done.10.first = f32[6,128]{1,0:T(8,128)S(1)} collective-permute-done((f32[6,128]{1,0:T(8,128)S(1)}, f32[6,128]{1,0:T(8,128)S(1)}, u32[]{:S(2)}, u32[]{:S(2)}) %collective-permute-start.10) | collective-permute-done | bytes 3104 | tf_op jit(solution)/shard_map/ppermute | solution.py:47
  35.2 0.0 collective-permute-done.11.second
  35.2 0.6 %pick.1 = bf16[18,128]{1,0:T(8,128)(2,1)} custom-call(s32[18]{0:T(128)S(4)} %get-tuple-element.58.place, f32[6,128]{1,0:T(8,128)S(1)} %pad_maximum_fusion.2.own, f32[6,128]{1,0:T(8,128)S(1)} %collective-permute-done.10.first, f32[6,128]{1,0:T(8,128)S(1)} %collective-permute-done.11.second), custom_call_target="tpu_custom_call" | custom-call | tf_op jit(solution)/shard_map/pick/pallas_call | solution.py:602
  (11 shorter events, 0.1 us)
Async XLA Ops:
  1.7 5.4 %collective-permute-start = (bf16[6,16,128]{2,1,0:T(8,128)(2,1)S(1)}, bf16[6,16,128]{2,1,0:T(8,128)(2,1)S(1)}, u32[]{:S(2)}, u32[]{:S(2)}) collective-permute-start(bf16[6,16,128]{2,1,0:T(8,128)(2,1)S(1)} %get-tuple-element.41), channel_id=1, source_target_pairs={{0,24},{8,16},{16,8},{24,0},{1,25},{9,17},{17,9},{25,1},{2,26},{10... | collective-permute-start | bytes 73736 | tf_op jit(solution)/shard_map/ppermute | solution.py:47
  4.2 2.9 %collective-permute-start.1 = (bf16[6,16,128]{2,1,0:T(8,128)(2,1)S(1)}, bf16[6,16,128]{2,1,0:T(8,128)(2,1)S(1)}, u32[]{:S(2)}, u32[]{:S(2)}) collective-permute-start(bf16[6,16,128]{2,1,0:T(8,128)(2,1)S(1)} %get-tuple-element.42), channel_id=1, source_target_pairs={{0,8},{8,0},{16,24},{24,16},{1,9},{9,1},{17,25},{25,17},{2,10},{10... | collective-permute-start | bytes 73736 | tf_op jit(solution)/shard_map/ppermute | solution.py:47
  7.1 8.3 %collective-permute-start.2 = (bf16[6,16,128]{2,1,0:T(8,128)(2,1)S(1)}, bf16[6,16,128]{2,1,0:T(8,128)(2,1)S(1)}, u32[]{:S(2)}, u32[]{:S(2)}) collective-permute-start(bf16[6,16,128]{2,1,0:T(8,128)(2,1)S(1)} %pad_maximum_fusion), channel_id=1, source_target_pairs={{0,7},{1,2},{2,1},{3,4},{4,3},{5,6},{6,5},{7,0},{8,15},{9,10},{10,... | collective-permute-start | bytes 73736 | tf_op jit(solution)/shard_map/ppermute | solution.py:47
  11.7 3.8 %collective-permute-start.3 = (bf16[6,16,128]{2,1,0:T(8,128)(2,1)S(1)}, bf16[6,16,128]{2,1,0:T(8,128)(2,1)S(1)}, u32[]{:S(2)}, u32[]{:S(2)}) collective-permute-start(bf16[6,16,128]{2,1,0:T(8,128)(2,1)S(1)} %pad_maximum_fusion.1), channel_id=1, source_target_pairs={{0,1},{1,0},{2,3},{3,2},{4,5},{5,4},{6,7},{7,6},{8,9},{9,8},{10,11... | collective-permute-start | bytes 73736 | tf_op jit(solution)/shard_map/ppermute | solution.py:47
  16.6 6.6 %collective-permute-start.6 = (bf16[384,128]{1,0:T(8,128)(2,1)S(1)}, bf16[384,128]{1,0:T(8,128)(2,1)S(1)}, u32[]{:S(2)}, u32[]{:S(2)}) collective-permute-start(bf16[384,128]{1,0:T(8,128)(2,1)S(1)} %get-tuple-element.46), channel_id=1, source_target_pairs={{0,1},{1,0},{2,3},{3,2},{4,5},{5,4},{6,7},{7,6},{8,9},{9,8},{10,11... | collective-permute-start | bytes 294920 | tf_op jit(solution)/shard_map/ppermute | solution.py:47
  18.6 4.6 %collective-permute-start.7 = (bf16[384,128]{1,0:T(8,128)(2,1)S(1)}, bf16[384,128]{1,0:T(8,128)(2,1)S(1)}, u32[]{:S(2)}, u32[]{:S(2)}) collective-permute-start(bf16[384,128]{1,0:T(8,128)(2,1)S(1)} %get-tuple-element.47), channel_id=1, source_target_pairs={{0,0},{1,2},{2,1},{3,4},{4,3},{5,6},{6,5},{7,7},{8,8},{9,10},{10,9... | collective-permute-start | bytes 294920 | tf_op jit(solution)/shard_map/ppermute | solution.py:47
  19.2 3.9 %collective-permute-start.4 = (bf16[192,128]{1,0:T(8,128)(2,1)S(1)}, bf16[192,128]{1,0:T(8,128)(2,1)S(1)}, u32[]{:S(2)}, u32[]{:S(2)}) collective-permute-start(bf16[192,128]{1,0:T(8,128)(2,1)S(1)} %get-tuple-element.44), channel_id=1, source_target_pairs={{0,24},{8,16},{16,8},{24,0},{1,25},{9,17},{17,9},{25,1},{2,26},{10... | collective-permute-start | bytes 147464 | tf_op jit(solution)/shard_map/ppermute | solution.py:47
  19.3 3.9 %collective-permute-start.5 = (bf16[192,128]{1,0:T(8,128)(2,1)S(1)}, bf16[192,128]{1,0:T(8,128)(2,1)S(1)}, u32[]{:S(2)}, u32[]{:S(2)}) collective-permute-start(bf16[192,128]{1,0:T(8,128)(2,1)S(1)} %get-tuple-element.45), channel_id=1, source_target_pairs={{0,8},{8,0},{16,24},{24,16},{1,9},{9,1},{17,25},{25,17},{2,10},{10... | collective-permute-start | bytes 147464 | tf_op jit(solution)/shard_map/ppermute | solution.py:47
  25.6 6.5 %collective-permute-start.8 = (f32[6,128]{1,0:T(8,128)S(1)}, f32[6,128]{1,0:T(8,128)S(1)}, u32[]{:S(2)}, u32[]{:S(2)}) collective-permute-start(f32[6,128]{1,0:T(8,128)S(1)} %get-tuple-element.60), channel_id=1, source_target_pairs={{0,7},{1,2},{2,1},{3,4},{4,3},{5,6},{6,5},{7,0},{8,15},{9,10},{10,... | collective-permute-start | bytes 9224 | tf_op jit(solution)/shard_map/ppermute | solution.py:47
  26.5 5.6 %collective-permute-start.9 = (f32[6,128]{1,0:T(8,128)S(1)}, f32[6,128]{1,0:T(8,128)S(1)}, u32[]{:S(2)}, u32[]{:S(2)}) collective-permute-start(f32[6,128]{1,0:T(8,128)S(1)} %get-tuple-element.61), channel_id=1, source_target_pairs={{0,1},{1,0},{2,3},{3,2},{4,5},{5,4},{6,7},{7,6},{8,9},{9,8},{10,11... | collective-permute-start | bytes 9224 | tf_op jit(solution)/shard_map/ppermute | solution.py:47
  32.1 3.1 %collective-permute-start.10 = (f32[6,128]{1,0:T(8,128)S(1)}, f32[6,128]{1,0:T(8,128)S(1)}, u32[]{:S(2)}, u32[]{:S(2)}) collective-permute-start(f32[6,128]{1,0:T(8,128)S(1)} %pad_maximum_fusion.3), channel_id=1, source_target_pairs={{0,24},{8,16},{16,8},{24,0},{1,25},{9,17},{17,9},{25,1},{2,26},{10... | collective-permute-start | bytes 9224 | tf_op jit(solution)/shard_map/ppermute | solution.py:47
  32.2 3.0 %collective-permute-start.11 = (f32[6,128]{1,0:T(8,128)S(1)}, f32[6,128]{1,0:T(8,128)S(1)}, u32[]{:S(2)}, u32[]{:S(2)}) collective-permute-start(f32[6,128]{1,0:T(8,128)S(1)} %pad_maximum_fusion.4), channel_id=1, source_target_pairs={{0,8},{8,0},{16,24},{24,16},{1,9},{9,1},{17,25},{25,17},{2,10},{10... | collective-permute-start | bytes 9224 | tf_op jit(solution)/shard_map/ppermute | solution.py:47
